TPU v7x, 128 devices: a whole 4x4x4 slice. The times are simulated.
128 devices in a mesh: expert: 8 (over z, y_lo), tensor: 16 (over y_hi, x, core).
Axes of the slice: x: 4, y: 4 (y_hi: 2, y_lo: 2; y = y_hi * 2 + y_lo), z: 4, core: 2. Of those that a mesh axis runs over, the one named last changes fastest.
Arguments:
- tokens: bfloat16 [2048, 3072], P('expert'), may hold values from -6 to 6
- cotangent: bfloat16 [2048, 3072], P('expert'), may hold values from -6 to 6
- expert_ids: int32 [2048, 2], P('expert'), may hold values from 0 to 7, all different within a row; in each aligned block of 256 rows (0 to 255, 256 to 511, ...) at most 96 rows name the same one
- gates: float32 [2048, 2], P('expert'), may hold values from 0.1 to 1
- w_gate: bfloat16 [8, 3072, 8192], P('expert', None, 'tensor'), may hold values from -0.109375 to 0.109375
- w_up: bfloat16 [8, 3072, 8192], P('expert', None, 'tensor'), may hold values from -0.109375 to 0.109375
- w_down: bfloat16 [8, 8192, 3072], P('expert', 'tensor'), may hold values from -0.0625 to 0.0625
Outputs:
- mixed: bfloat16 [2048, 3072], P('expert')
- token_grad: bfloat16 [2048, 3072], P('expert')
- grad_gate: bfloat16 [8, 3072, 8192], P('expert', None, 'tensor')
- grad_up: bfloat16 [8, 3072, 8192], P('expert', None, 'tensor')
- grad_down: bfloat16 [8, 8192, 3072], P('expert', 'tensor')
Inputs may be any that keep to these rules, and one draw needn't show every extreme that they name: `expert_ids`: each token names two different experts. In one block of 256 rows no expert is named more than 96 times, and in every draw some block names some expert exactly 96 times.
All inputs are finite; a program needn't handle non-finite values.
Results may differ from a plain program's by a relative error of at most 0.02.
Values may be sent and summed in bfloat16 or wider, within the bound.
No kernel may reach another device: no remote copies, remote signals or barrier semaphores. Data moves between devices by JAX's collectives and lax.ppermute only.
A program may use at most 128 MiB of HBM per device.

v0:
```python
import jax
import jax.numpy as jnp
from jax import lax
from jax.sharding import PartitionSpec as P


def contract(left_arr, right_arr, left_dim, right_dim):
    return lax.dot_general(
        left_arr,
        right_arr,
        (((left_dim,), (right_dim,)), ((), ())),
        preferred_element_type=jnp.float32,
    )


def bring_home(partial_value, experts, slot_cap, features):
    shaped = partial_value.reshape(experts, slot_cap, features)
    summed = lax.psum_scatter(
        shaped.astype(jnp.bfloat16), "tensor", scatter_dimension=2, tiled=True
    )
    arrived = lax.all_to_all(summed, "expert", split_axis=0, concat_axis=0, tiled=True)
    whole = lax.all_gather(arrived, "tensor", axis=2, tiled=True)
    return whole.reshape(experts * slot_cap, features)


def on_device(tokens, cotangent, expert_ids, gates, w_gate, w_up, w_down):
    tok_rows, features = tokens.shape
    experts = lax.axis_size("expert")
    slot_cap = 3 * tok_rows // experts
    gate_w = w_gate[0]
    up_w = w_up[0]
    down_w = w_down[0]
    flat_ids = expert_ids.reshape(-1)
    onehot = (flat_ids[:, None] == jnp.arange(experts, dtype=jnp.int32)[None, :]).astype(jnp.int32)
    before = jnp.cumsum(onehot, axis=0) - onehot
    ranked = jnp.sum(before * onehot, axis=1)
    position = (flat_ids * slot_cap + ranked).reshape(tok_rows, 2)
    slot_rows = experts * slot_cap
    matched = (
        position[:, :, None] == jnp.arange(slot_rows, dtype=jnp.int32)[None, None, :]
    ).astype(jnp.float32)
    placing = jnp.sum(matched, axis=1).astype(jnp.bfloat16)
    slot_gate = jnp.sum(jnp.sum(matched * gates[:, :, None], axis=1), axis=0)
    pair_place = matched.reshape(tok_rows * 2, slot_rows).astype(jnp.bfloat16)
    routed = (
        contract(placing, tokens, 0, 0).astype(jnp.bfloat16).reshape(experts, slot_cap, features)
    )
    placed_cot = contract(placing, cotangent, 0, 0)
    d_routed = (
        (placed_cot * slot_gate[:, None]).astype(jnp.bfloat16).reshape(experts, slot_cap, features)
    )
    arrived = lax.all_to_all(routed, "expert", split_axis=0, concat_axis=0, tiled=True)
    grouped = arrived.reshape(slot_rows, features)
    gate_act = jnp.dot(grouped, gate_w, preferred_element_type=jnp.float32)
    up_act = jnp.dot(grouped, up_w, preferred_element_type=jnp.float32)
    squashed = jax.nn.sigmoid(gate_act)
    silu_act = gate_act * squashed
    hidden = (silu_act * up_act).astype(jnp.bfloat16)
    out_partial = jnp.dot(hidden, down_w, preferred_element_type=jnp.float32)
    expert_out = bring_home(out_partial, experts, slot_cap, features)
    taken_pairs = jnp.dot(pair_place, expert_out, preferred_element_type=jnp.float32).reshape(
        tok_rows, 2, features
    )
    mixed = jnp.sum(taken_pairs * gates[:, :, None], axis=1).astype(jnp.bfloat16)
    arrived_cot = lax.all_to_all(d_routed, "expert", split_axis=0, concat_axis=0, tiled=True)
    grouped_cot = arrived_cot.reshape(slot_rows, features)
    d_hidden = contract(grouped_cot, down_w, 1, 1)
    grad_down = contract(hidden, grouped_cot, 0, 0).astype(jnp.bfloat16)
    d_up = (d_hidden * silu_act).astype(jnp.bfloat16)
    d_gate = (d_hidden * up_act * squashed * (1.0 + gate_act * (1.0 - squashed))).astype(
        jnp.bfloat16
    )
    grad_gate = contract(grouped, d_gate, 0, 0).astype(jnp.bfloat16)
    grad_up = contract(grouped, d_up, 0, 0).astype(jnp.bfloat16)
    in_partial = contract(d_gate, gate_w, 1, 1) + contract(d_up, up_w, 1, 1)
    returned = bring_home(in_partial, experts, slot_cap, features)
    token_grad = jnp.dot(placing, returned, preferred_element_type=jnp.float32).astype(jnp.bfloat16)
    return (mixed, token_grad, grad_gate[None], grad_up[None], grad_down[None])


def solution(mesh):
    placed = (
        P("expert", None),
        P("expert", None),
        P("expert", None),
        P("expert", None),
        P("expert", None, "tensor"),
        P("expert", None, "tensor"),
        P("expert", "tensor", None),
    )
    return jax.shard_map(
        on_device,
        mesh=mesh,
        in_specs=placed,
        out_specs=(
            P("expert", None),
            P("expert", None),
            P("expert", None, "tensor"),
            P("expert", None, "tensor"),
            P("expert", "tensor", None),
        ),
        check_vma=False,
    )
```

profile of v0, /device:TPU:1, one launch (start us, length us, event | category | flops | bytes accessed | tf_op | source)
XLA Modules:
  0.0 489.9 jit_solution(14326119158565506340)
XLA Ops:
  7.2 0.0 copy-start
  7.2 1.0 copy.49
  8.2 0.1 eq.63
  8.3 0.1 eq.59
  8.5 1.1 reduce-window.6
  9.6 0.2 slice_reduce_fusion
  9.9 0.1 fusion.18
  9.9 0.1 reduce_sum.43
  10.1 0.1 copy.51
  10.2 0.7 multiply_add_fusion
  10.9 1.1 select_reduce_fusion
  11.9 4.9 %convolution_convert_fusion.1 = bf16[768,3072]{1,0:T(8,128)(2,1)} fusion(bf16[256,3072]{1,0:T(8,128)(2,1)} %param.7, bf16[256,768]{1,0:T(8,128)(2,1)S(1)} %get-tuple-element.6), kind=kOutput, calls=%fused_computation.4 | convolution fusion | flops 1210318848 | bytes 6684672 | tf_op jit(solution)/shard_map/dot_general | solution.py:8
  16.9 6.9 %all-to-all-start = ((bf16[8,96,3072]{2,1,0:T(8,128)(2,1)}), bf16[8,96,3072]{2,1,0:T(8,128)(2,1)}, u32[]{:S(2)}, u32[]{:S(2)}) async-start(bf16[8,96,3072]{2,1,0:T(8,128)(2,1)} %bitcast.68), calls=%async_computation | async-start | bytes 9437184 | tf_op jit(solution)/shard_map/all_to_all | solution.py:52
  23.8 5.0 %multiply_convert_fusion = bf16[768,3072]{1,0:T(8,128)(2,1)} fusion(bf16[256,3072]{1,0:T(8,128)(2,1)} %param.8, f32[768]{0:T(1024)S(1)} %get-tuple-element.5, bf16[256,768]{1,0:T(8,128)(2,1)S(1)} %get-tuple-element.6), kind=kOutput, calls=%fused_computation.1 | convolution fusion | flops 1212678144 | bytes 6687744 | tf_op jit(solution)/shard_map/dot_general | solution.py:8
  28.8 49.3 %all-to-all-done = bf16[8,96,3072]{2,1,0:T(8,128)(2,1)} async-done(((bf16[8,96,3072]{2,1,0:T(8,128)(2,1)}), bf16[8,96,3072]{2,1,0:T(8,128)(2,1)}, u32[]{:S(2)}, u32[]{:S(2)}) %all-to-all-start) | async-done | bytes 4718624 | tf_op jit(solution)/shard_map/all_to_all | solution.py:52
  78.0 4.6 all-to-all-start.2
  82.6 0.0 reduce-scatter.7.cloned.1.call-start
  82.7 0.0 copy-start.6
  82.7 7.2 %fusion.7 = f32[768,512]{1,0:T(8,128)} fusion(bf16[768,3072]{1,0:T(8,128)(2,1)} %bitcast.4, bf16[1,3072,512]{2,1,0:T(8,128)(2,1)} %param.12), kind=kOutput, calls=%fused_computation.16 | convolution fusion | flops 2415919104 | bytes 9437184 | tf_op jit(solution)/shard_map/dot_general | solution.py:55
  89.9 0.0 copy-done.6
  89.9 6.1 %fusion.11 = f32[768,512]{1,0:T(8,128)} fusion(bf16[768,3072]{1,0:T(8,128)(2,1)} %bitcast.4, bf16[1,3072,512]{2,1,0:T(8,128)(2,1)S(1)} %copy-done.6), kind=kOutput, calls=%fused_computation.20 | convolution fusion | flops 2415919104 | bytes 9437184 | tf_op jit(solution)/shard_map/dot_general | solution.py:54
  96.0 39.9 %all-to-all-done.2 = bf16[8,96,3072]{2,1,0:T(8,128)(2,1)} async-done(((bf16[8,96,3072]{2,1,0:T(8,128)(2,1)}), bf16[8,96,3072]{2,1,0:T(8,128)(2,1)}, u32[]{:S(2)}, u32[]{:S(2)}) %all-to-all-start.2) | async-done | bytes 4718624 | tf_op jit(solution)/shard_map/all_to_all | solution.py:65
  135.9 0.0 copy-done
  135.9 7.0 %multiply_convert_fusion.1 = (bf16[768,512]{1,0:T(8,128)(2,1)}, bf16[768,512]{1,0:T(8,128)(2,1)}, bf16[768,512]{1,0:T(8,128)(2,1)S(1)}) fusion(f32[768,512]{1,0:T(8,128)} %fusion.11, f32[768,512]{1,0:T(8,128)} %fusion.7, bf16[768,3072]{1,0:T(8,128)(2,1)} %bitcast.13, bf16[1,512,3072]{2,1,0:T(8,128)(2,1)S(1)} %copy-done), kind=kOutput, calls=%fused_computation.22 | convolution fusion | flops 2421817344 | bytes 13369344 | tf_op jit(solution)/shard_map/dot_general | solution.py:8
  142.9 0.9 copy-done.7
  143.7 4.3 convolution_convert_fusion
  148.0 8.6 %copy.56 = bf16[8,96,3072]{1,0,2:T(8,128)(2,1)} copy(bf16[8,96,3072]{2,1,0:T(8,128)(2,1)} %convolution_convert_fusion) | data formatting | bytes 9437184
  156.6 10.8 %reshape.99 = bf16[3072,768]{1,0:T(8,128)(2,1)} reshape(bf16[3072,8,96]{2,1,0:T(8,128)(2,1)} %bitcast.69) | data formatting | bytes 9437184
  167.4 0.0 reduce-scatter.7.cloned.1.call-update
  167.4 0.2 reduce-scatter.9.cloned.1.call-start
  167.7 0.0 copy-start.2
  167.7 0.0 copy-start.3
  167.7 4.9 %fusion.9 = f32[768,3072]{1,0:T(8,128)S(1)} fusion(bf16[768,512]{1,0:T(8,128)(2,1)} %get-tuple-element.8, bf16[1,3072,512]{2,1,0:T(8,128)(2,1)} %param.11), kind=kOutput, calls=%fused_computation.18 | convolution fusion | flops 2415919104 | bytes 13369344 | tf_op jit(solution)/shard_map/dot_general | solution.py:8
  172.6 0.0 copy-done.2
  172.6 4.4 add_convert_fusion
  177.0 8.8 %copy.58 = bf16[8,96,3072]{1,0,2:T(8,128)(2,1)} copy(bf16[8,96,3072]{2,1,0:T(8,128)(2,1)} %bitcast.71) | data formatting | bytes 9437184
  185.8 11.0 %reshape.101 = bf16[3072,768]{1,0:T(8,128)(2,1)} reshape(bf16[3072,8,96]{2,1,0:T(8,128)(2,1)} %bitcast.70) | data formatting | bytes 9437184
  196.8 0.0 reduce-scatter.9.cloned.1.call-update
  196.9 0.0 all-gather.3.cloned.1.call-start
  196.9 54.0 %reduce-scatter.7.cloned.1.call-done = bf16[192,768]{1,0:T(8,128)(2,1)} async-done(((bf16[3072,768]{1,0:T(8,128)(2,1)}), bf16[192,768]{1,0:T(8,128)(2,1)}) %reduce-scatter.7.cloned.1.call-update) | async-done | bytes 294928
  250.9 1.4 reshape.100
  252.3 0.0 copy-start.8
  252.3 0.3 copy.57
  252.6 11.0 %all_to_all.20 = bf16[8,96,192]{2,1,0:T(8,128)(2,1)S(1)} all-to-all(bf16[8,96,192]{2,1,0:T(8,128)(2,1)S(1)} %copy.57), channel_id=1, replica_groups=mesh['expert'=8,'tensor'=16] {'expert'}, dimensions={0} | all-to-all | bytes 589824 | tf_op jit(solution)/shard_map/all_to_all | solution.py:21
  263.7 1.0 copy.52
  264.6 0.0 all-gather.3.cloned.1.call-update
  264.7 0.0 all-gather.5.cloned.1.call-start
  264.7 72.5 %reduce-scatter.9.cloned.1.call-done = bf16[192,768]{1,0:T(8,128)(2,1)} async-done(((bf16[3072,768]{1,0:T(8,128)(2,1)}), bf16[192,768]{1,0:T(8,128)(2,1)}) %reduce-scatter.9.cloned.1.call-update) | async-done | bytes 294928
  337.2 1.4 reshape.102
  338.6 0.3 copy.59
  338.9 11.0 %all_to_all.21 = bf16[8,96,192]{2,1,0:T(8,128)(2,1)S(1)} all-to-all(bf16[8,96,192]{2,1,0:T(8,128)(2,1)S(1)} %copy.59), channel_id=1, replica_groups=mesh['expert'=8,'tensor'=16] {'expert'}, dimensions={0} | all-to-all | bytes 589824 | tf_op jit(solution)/shard_map/all_to_all | solution.py:21
  349.9 1.0 copy.54
  350.9 0.0 all-gather.5.cloned.1.call-update
  351.0 0.0 copy-done.8
  351.0 0.0 copy-start.4
  351.0 6.5 %fusion.2 = bf16[1,512,3072]{2,1,0:T(8,128)(2,1)} fusion(bf16[768,512]{1,0:T(8,128)(2,1)S(1)} %copy-done.8, bf16[768,3072]{1,0:T(8,128)(2,1)} %bitcast.13), kind=kOutput, calls=%fused_computation.10 | convolution fusion | flops 2417491968 | bytes 8650752 | tf_op jit(solution)/shard_map/dot_general | solution.py:8
  357.5 6.5 %fusion.1 = bf16[1,3072,512]{2,1,0:T(8,128)(2,1)} fusion(bf16[768,3072]{1,0:T(8,128)(2,1)} %bitcast.4, bf16[768,512]{1,0:T(8,128)(2,1)S(1)} %copy-done.4), kind=kOutput, calls=%fused_computation.9 | convolution fusion | flops 2417491968 | bytes 8650752 | tf_op jit(solution)/shard_map/dot_general | solution.py:8
  364.0 6.4 %fusion = bf16[1,3072,512]{2,1,0:T(8,128)(2,1)} fusion(bf16[768,3072]{1,0:T(8,128)(2,1)} %bitcast.4, bf16[768,512]{1,0:T(8,128)(2,1)S(1)} %copy-done.9), kind=kOutput, calls=%fused_computation.8 | convolution fusion | flops 2417491968 | bytes 8650752 | tf_op jit(solution)/shard_map/dot_general | solution.py:8
  370.4 34.5 %all-gather.3.cloned.1.call-done = bf16[8,96,3072]{1,0,2:T(8,128)(2,1)} async-done(((bf16[8,96,192]{1,0,2:T(8,128)(2,1)}), bf16[8,96,3072]{1,0,2:T(8,128)(2,1)}) %all-gather.3.cloned.1.call-update) | async-done | bytes 4718608 | tf_op jit(solution)/shard_map/all_gather | solution.py:22
  404.9 8.6 %copy.53 = bf16[8,96,3072]{2,1,0:T(8,128)(2,1)} copy(bf16[8,96,3072]{1,0,2:T(8,128)(2,1)} %all-gather.3.cloned.1.call-done) | data formatting | bytes 9437184 | tf_op jit(solution)/shard_map/all_gather | solution.py:22
  413.4 7.4 %multiply_reduce_fusion = bf16[256,3072]{1,0:T(8,128)(2,1)} fusion(bf16[768,3072,1]{1,0,2:T(8,128)(2,1)} %bitcast.73, f32[256,2]{0,1:T(2,128)S(1)} %copy-done.5, s32[256,2]{0,1:T(2,128)S(1)} %multiply_add_fusion), kind=kOutput, calls=%fused_computation.2 | convolution fusion | flops 2419458048 | bytes 6295552 | tf_op jit(solution)/shard_map/dot_general | solution.py:61
  420.8 49.0 %all-gather.5.cloned.1.call-done = bf16[8,96,3072]{1,0,2:T(8,128)(2,1)} async-done(((bf16[8,96,192]{1,0,2:T(8,128)(2,1)}), bf16[8,96,3072]{1,0,2:T(8,128)(2,1)}) %all-gather.5.cloned.1.call-update) | async-done | bytes 4718608 | tf_op jit(solution)/shard_map/all_gather | solution.py:22
  469.8 8.5 %copy.55 = bf16[8,96,3072]{2,1,0:T(8,128)(2,1)} copy(bf16[8,96,3072]{1,0,2:T(8,128)(2,1)} %all-gather.5.cloned.1.call-done) | data formatting | bytes 9437184 | tf_op jit(solution)/shard_map/all_gather | solution.py:22
  478.3 5.0 %convolution_convert_fusion.5 = bf16[256,3072]{1,0:T(8,128)(2,1)} fusion(bf16[768,3072]{1,0:T(8,128)(2,1)} %bitcast.74, bf16[256,768]{1,0:T(8,128)(2,1)S(1)} %get-tuple-element.6), kind=kOutput, calls=%fused_computation.11 | convolution fusion | flops 1208745984 | bytes 6684672 | tf_op jit(solution)/shard_map/dot_general | solution.py:77
  (12 shorter events, 0.1 us)
Async XLA Ops:
  7.2 128.7 %copy-start = (bf16[1,512,3072]{2,1,0:T(8,128)(2,1)S(1)}, bf16[1,512,3072]{2,1,0:T(8,128)(2,1)}, u32[]{:S(2)}) copy-start(bf16[1,512,3072]{2,1,0:T(8,128)(2,1)} %param.13) | copy-start | bytes 9437188
  16.9 61.1 %all-to-all-start = ((bf16[8,96,3072]{2,1,0:T(8,128)(2,1)}), bf16[8,96,3072]{2,1,0:T(8,128)(2,1)}, u32[]{:S(2)}, u32[]{:S(2)}) async-start(bf16[8,96,3072]{2,1,0:T(8,128)(2,1)} %bitcast.68), calls=%async_computation | async-start | bytes 9437184 | tf_op jit(solution)/shard_map/all_to_all | solution.py:52
  78.0 57.9 %all-to-all-start.2 = ((bf16[8,96,3072]{2,1,0:T(8,128)(2,1)}), bf16[8,96,3072]{2,1,0:T(8,128)(2,1)}, u32[]{:S(2)}, u32[]{:S(2)}) async-start(bf16[8,96,3072]{2,1,0:T(8,128)(2,1)} %bitcast.72), calls=%async_computation.2 | async-start | bytes 9437184 | tf_op jit(solution)/shard_map/all_to_all | solution.py:65
  82.6 168.3 %reduce-scatter.7.cloned.1.call-start = ((), (), s32[]{:S(2)}) async-start(), calls=%async_computation.8 | async-start | bytes 5013504
  82.7 7.2 %copy-start.6 = (bf16[1,3072,512]{2,1,0:T(8,128)(2,1)S(1)}, bf16[1,3072,512]{2,1,0:T(8,128)(2,1)}, u32[]{:S(2)}) copy-start(bf16[1,3072,512]{2,1,0:T(8,128)(2,1)} %param.11) | copy-start | bytes 9437188
  142.9 0.9 copy-start.7
  167.4 169.8 %reduce-scatter.9.cloned.1.call-start = ((), (), s32[]{:S(2)}) async-start(), calls=%async_computation.9 | async-start | bytes 5013504
  167.7 4.9 %copy-start.2 = (bf16[1,3072,512]{2,1,0:T(8,128)(2,1)S(1)}, bf16[1,3072,512]{2,1,0:T(8,128)(2,1)}, u32[]{:S(2)}) copy-start(bf16[1,3072,512]{2,1,0:T(8,128)(2,1)} %param.12) | copy-start | bytes 9437188
  167.7 4.9 %copy-start.3 = (bf16[768,512]{1,0:T(8,128)(2,1)S(1)}, bf16[768,512]{1,0:T(8,128)(2,1)}, u32[]{:S(2)}) copy-start(bf16[768,512]{1,0:T(8,128)(2,1)} %get-tuple-element.7) | copy-start | bytes 2359300
  196.9 208.0 %all-gather.3.cloned.1.call-start = ((), (), s32[]{:S(2)}) async-start(), calls=%async_computation.6 | async-start | bytes 6684672 | tf_op jit(solution)/shard_map/all_gather | solution.py:22
  252.3 98.6 %copy-start.8 = (bf16[768,512]{1,0:T(8,128)(2,1)S(1)}, bf16[768,512]{1,0:T(8,128)(2,1)}, u32[]{:S(2)}) copy-start(bf16[768,512]{1,0:T(8,128)(2,1)} %copy-done.7) | copy-start | bytes 2359300
  264.7 205.2 %all-gather.5.cloned.1.call-start = ((), (), s32[]{:S(2)}) async-start(), calls=%async_computation.7 | async-start | bytes 6684672 | tf_op jit(solution)/shard_map/all_gather | solution.py:22
  351.0 6.5 %copy-start.4 = (bf16[768,512]{1,0:T(8,128)(2,1)S(1)}, bf16[768,512]{1,0:T(8,128)(2,1)}, u32[]{:S(2)}) copy-start(bf16[768,512]{1,0:T(8,128)(2,1)} %get-tuple-element.7) | copy-start | bytes 2359300
  357.5 6.5 %copy-start.9 = (bf16[768,512]{1,0:T(8,128)(2,1)S(1)}, bf16[768,512]{1,0:T(8,128)(2,1)}, u32[]{:S(2)}) copy-start(bf16[768,512]{1,0:T(8,128)(2,1)} %get-tuple-element.8) | copy-start | bytes 2359300
  370.4 43.0 %copy-start.5 = (f32[256,2]{0,1:T(2,128)S(1)}, f32[256,2]{0,1:T(2,128)}, u32[]{:S(2)}) copy-start(f32[256,2]{0,1:T(2,128)} %param.10) | copy-start | bytes 6148
  478.3 5.0 %copy-start.1 = (bf16[1,512,3072]{2,1,0:T(8,128)(2,1)S(1)}, bf16[1,512,3072]{2,1,0:T(8,128)(2,1)}, u32[]{:S(2)}) copy-start(bf16[1,512,3072]{2,1,0:T(8,128)(2,1)} %param.13) | copy-start | bytes 9437188
Sparse Core Ops, SparseCore 0:
  167.6 83.3 reduce-scatter.6
  255.5 81.6 reduce-scatter.8
  340.2 64.5 all-gather.2
  407.2 62.6 all-gather.4
where the time goes:
time: 492 us; the launch traced here: 490 us
  waiting for transfers between devices  299 us (61%)
  matrix products  75.5 us (15%)
  local copies, waits for them, and re-layouts  64.2 us (13%)
  blocking collectives  22.1 us (4%)
  between operations  13.9 us (3%)
  starting transfers between devices  11.8 us (2%)
    unnamed x6, waiting for transfers between devices  127 us
    all_gather x2, waiting for transfers between devices, bring_home(): whole = lax.all_gather(arrived, 'tensor', axis=2, tiled=True)  83.5 us
    all_to_all x1, waiting for transfers between devices, on_device(): lax.all_to_all(routed, 'expert', split_axis=0, concat_axis=0, tiled=True)  49.3 us
    dot_general x8, matrix products, contract(): lax.dot_general(left_arr, right_arr, (((left_dim,), (right_dim,)), ((), (...  45.6 us
    unnamed x29, local copies, waits for them, and re-layouts  44.5 us
    all_to_all x1, waiting for transfers between devices, on_device(): lax.all_to_all(d_routed, 'expert', split_axis=0, concat_axis=0, tiled=True)  39.9 us
    all_to_all x2, blocking collectives, bring_home(): lax.all_to_all(summed, 'expert', split_axis=0, concat_axis=0, tiled=True)  22.1 us
    all_gather x2, local copies, waits for them, and re-layouts, bring_home(): whole = lax.all_gather(arrived, 'tensor', axis=2, tiled=True)  17.1 us
  transfers between devices with their start and end apart: 6, of which 6 were waited for; matrix products, arithmetic and copies ran while one was open for 18% of the time, Pallas kernels for 0%

commit v1 on v0

v1 whole, which is shorter than its diff:
```python
import jax
import jax.numpy as jnp
from jax import lax
from jax.experimental import pallas as pl
from jax.experimental.pallas import tpu as pltpu
from jax.sharding import Mesh, PartitionSpec as P

F32, BF16 = jnp.float32, jnp.bfloat16
EXP = ("z", "yl")
TEN = ("yh", "x", "c")
NN = (((1,), (0,)), ((), ()))
NT = (((1,), (1,)), ((), ()))
TN = (((0,), (0,)), ((), ()))


def mm(a, b, dims=NN):
    return lax.dot_general(a, b, dims, preferred_element_type=F32)


def call(kernel, out_shape, grid, in_specs, out_specs, scratch=(), mib=24):
    return pl.pallas_call(
        kernel,
        out_shape=out_shape,
        grid_spec=pltpu.PrefetchScalarGridSpec(
            num_scalar_prefetch=1,
            grid=grid,
            in_specs=in_specs,
            out_specs=out_specs,
            scratch_shapes=list(scratch),
        ),
        compiler_params=pltpu.CompilerParams(vmem_limit_bytes=mib * 2**20),
    )


def shape(*dims, dtype=BF16):
    return jax.ShapeDtypeStruct(dims, dtype)


def in_hbm(*values):
    return [pltpu.with_memory_space_constraint(v, pltpu.HBM) for v in values]


def block(dims, index=None):
    return pl.BlockSpec(
        dims, index or (lambda *_: (0,) * len(dims)), pipeline_mode=pl.Buffered(1)
    )


def chunk_index(s, j):
    core = s[0] if j < 4 else 1 - s[0]
    return core * 4 + lax.rem(s[1] + j % 4, 4)


def to_index(s, r):
    return ((s[2] + r // 2) & 3) * 2 + (s[3] ^ (r % 2))


def from_index(s, r):
    return ((s[2] + 4 - r // 2) & 3) * 2 + (s[3] ^ (r % 2))


def route(scal, ids, gates, tokens, cotangent, experts, cap):
    toks, features = tokens.shape
    half, part, slots = features // 2, features // 8, experts * cap

    def kernel(s, ids_ref, gates_ref, tok_ref, cot_ref, *outs):
        rows = outs[-1]
        ids_here = jnp.transpose(ids_ref[...])
        named0, named1 = ids_here[:, 0:1], ids_here[:, 1:2]
        lane = lax.broadcasted_iota(jnp.int32, (toks, 128), 1)
        named = ((named0 == lane) | (named1 == lane)).astype(F32).astype(BF16)
        row = lax.broadcasted_iota(jnp.int32, (toks, toks), 0)
        col = lax.broadcasted_iota(jnp.int32, (toks, toks), 1)
        earlier = (col < row).astype(F32).astype(BF16)
        count = mm(earlier, named).astype(BF16)
        ex = lax.broadcasted_iota(jnp.int32, (128, slots), 0) * cap
        at = lax.broadcasted_iota(jnp.int32, (128, slots), 1)
        spread = ((at >= ex) & (at < ex + cap)).astype(F32).astype(BF16)
        rank = mm(count, spread)
        slot = lax.broadcasted_iota(jnp.int32, (toks, slots), 1)
        first, second = named0 * cap, named1 * cap
        in0 = (slot >= first) & (slot < first + cap)
        in1 = (slot >= second) & (slot < second + cap)
        base = jnp.where(in0, first, jnp.where(in1, second, -4 * slots))
        hit = rank.astype(jnp.int32) + base == slot
        g = jnp.transpose(gates_ref[...])
        weight = jnp.where(hit, jnp.where(in0, g[:, 0:1], g[:, 1:2]), 0.0)
        placing = hit.astype(F32).astype(BF16)
        hi = weight.astype(BF16)
        lo = (weight - hi.astype(F32)).astype(BF16)
        outs[9][...] = placing
        outs[10][...] = hi
        outs[11][...] = lo
        cot = cot_ref[...]
        outs[8][...] = (mm(hi, cot, TN) + mm(lo, cot, TN)).astype(BF16)
        rows[...] = mm(placing, tok_ref[...], TN).astype(BF16)
        for r in range(experts):
            at = pl.multiple_of(to_index(s, r) * cap, cap)
            outs[r][...] = rows[pl.ds(at, cap)]

    out = call(
        kernel,
        [pltpu.HBM((cap, half), BF16)] * 8 + [shape(slots, part)] + [shape(toks, slots)] * 3,
        (1,),
        [
            block(ids.shape[::-1]),
            block(gates.shape[::-1]),
            block((toks, half), lambda k, s: (0, s[0])),
            block((toks, part), lambda k, s: (0, s[0] * 4 + s[1])),
        ],
        [block((cap, half))] * 8 + [block((slots, part))] + [block((toks, slots))] * 3,
        [pltpu.VMEM((slots, half), BF16)],
    )(scal, ids.T, gates.T, *in_hbm(tokens, cotangent))
    return out[:8], out[8], out[9], out[10], out[11]


def gate_up(scal, own, oth, wg, wu):
    cap, half = own[0].shape
    rows, ff, tiles = 8 * cap, wg.shape[1], 2
    tile, kb = rows // tiles, wg.shape[0] // 4

    def kernel(s, *refs):
        own_refs, oth_refs, (wg_ref, wu_ref) = refs[:8], refs[8:16], refs[16:18]
        hid_ref, a_ref, b_ref, all_ref, wg_v, wu_v, sem, wsem = refs[18:]
        copies, wcopies = [], []
        for k in range(4):
            here = pl.ds(k * kb, kb)
            wcopies.append(pltpu.make_async_copy(wg_ref.at[here], wg_v.at[here], wsem.at[2 * k]))
            wcopies.append(
                pltpu.make_async_copy(wu_ref.at[here], wu_v.at[here], wsem.at[2 * k + 1])
            )
        for r in range(8):
            at = pl.ds(pl.multiple_of(from_index(s, r) * cap, cap), cap)
            for side, ref in ((0, own_refs[r]), (1, oth_refs[r])):
                core = s[0] if side == 0 else 1 - s[0]
                lanes = pl.ds(pl.multiple_of(core * half, 256), half)
                copies.append(
                    pltpu.make_async_copy(ref, all_ref.at[at, lanes], sem.at[2 * r + side])
                )
        for cp in copies + wcopies:
            cp.start()
        for cp in copies:
            cp.wait()
        for t in range(tiles):
            here = pl.ds(t * tile, tile)
            gate = up = None
            for k in range(4):
                if t == 0:
                    wcopies[2 * k].wait()
                    wcopies[2 * k + 1].wait()
                left = all_ref[here, pl.ds(k * kb, kb)]
                pg = mm(left, wg_v[pl.ds(k * kb, kb)])
                pu = mm(left, wu_v[pl.ds(k * kb, kb)])
                gate = pg if k == 0 else gate + pg
                up = pu if k == 0 else up + pu
            sig = jax.nn.sigmoid(gate)
            silu = gate * sig
            hid_ref[here] = (silu * up).astype(BF16)
            a_ref[here] = silu
            b_ref[here] = up * sig * (1.0 + gate * (1.0 - sig))

    anywhere = pl.BlockSpec(memory_space=pl.ANY)
    return call(
        kernel,
        [
            pltpu.VMEM((rows, ff), BF16),
            pltpu.VMEM((rows, ff), F32),
            pltpu.VMEM((rows, ff), F32),
            pltpu.HBM((rows, 2 * half), BF16),
        ],
        (1,),
        [anywhere] * 18,
        [block((rows, ff))] * 3 + [block((rows, 2 * half))],
        [
            pltpu.VMEM(wg.shape, BF16),
            pltpu.VMEM(wu.shape, BF16),
            pltpu.SemaphoreType.DMA((16,)),
            pltpu.SemaphoreType.DMA((8,)),
        ],
    )(scal, *in_hbm(*own, *oth, wg, wu))


def back_hidden(scal, chunks, wd, silu, dsilu):
    rows, cols = chunks[0].shape
    ff = wd.shape[0]

    def kernel(s, *refs):
        cr, (wd_ref, a_ref, b_ref, dgu_ref) = refs[:8], refs[8:]
        acc = None
        for j in range(8):
            at = pl.multiple_of(chunk_index(s, j) * cols, 128)
            part = mm(cr[j][...], wd_ref[:, pl.ds(at, cols)], NT)
            acc = part if acc is None else acc + part
        dgu_ref[:, :ff] = (acc * b_ref[...]).astype(BF16)
        dgu_ref[:, ff:] = (acc * a_ref[...]).astype(BF16)

    return call(
        kernel,
        pltpu.VMEM((rows, 2 * ff), BF16),
        (1,),
        [block((rows, cols))] * 8 + [block(wd.shape)] + [block((rows, ff))] * 2,
        block((rows, 2 * ff)),
    )(scal, *in_hbm(*chunks, wd), silu, dsilu)


def in_part(scal, d, mine, theirs, wg, wu, wg2, wu2):
    rows, ff = mine.shape[0], mine.shape[1] // 2
    cols = wg2.shape[0] // 4

    def kernel(s, m, t, w0, w1, w2, w3, out_ref):
        acc = mm(m[:, :ff], w0[...], NT) + mm(t[:, :ff], w2[...], NT)
        acc += mm(m[:, ff:], w1[...], NT) + mm(t[:, ff:], w3[...], NT)
        out_ref[...] = acc.astype(BF16)

    here = lambda k, s: (s[0] * 4 + lax.rem(s[1] + d, 4), 0)
    there = lambda k, s: (lax.rem(s[1] + d, 4), 0)
    return call(
        kernel,
        pltpu.HBM((rows, cols), BF16),
        (1,),
        [block((rows, 2 * ff))] * 2
        + [block((cols, ff), here)] * 2
        + [block((cols, ff), there)] * 2,
        block((rows, cols)),
        mib=16,
    )(scal, mine, theirs, *in_hbm(wg, wu, wg2, wu2))


def out_half(scal, hid, hid2, wd, wd2):
    rows, ff = hid.shape
    half = wd2.shape[1]
    cols = half // 2

    def kernel(s, h0, h1, w0, w1, out):
        out[...] = (mm(h0[...], w0[...]) + mm(h1[...], w1[...])).astype(BF16)

    return call(
        kernel,
        pltpu.HBM((rows, half), BF16),
        (2,),
        [
            block((rows, ff)),
            block((rows, ff)),
            pl.BlockSpec((ff, cols), lambda k, s: (0, s[0] * 2 + k)),
            pl.BlockSpec((ff, cols), lambda k, s: (0, k)),
        ],
        pl.BlockSpec((rows, cols), lambda k, s: (0, k)),
        mib=16,
    )(scal, hid, hid2, *in_hbm(wd, wd2))


def add(scal, *parts):
    rows, cols = parts[0].shape

    def kernel(s, *refs):
        acc = refs[0][...].astype(F32)
        for ref in refs[1:-1]:
            acc = acc + ref[...].astype(F32)
        refs[-1][...] = acc.astype(BF16)

    return call(
        kernel,
        shape(rows, cols),
        (1,),
        [block((rows, cols))] * len(parts),
        block((rows, cols)),
        mib=8,
    )(scal, *parts)


def combine(scal, mats, home, quarters):
    toks, slots = mats[0].shape
    cols = home.shape[1]
    n = len(mats)

    def kernel(s, *refs):
        mat_refs, home_ref, rest = refs[:n], refs[n], refs[n + 1 :]
        acc = mm(mat_refs[0][...], home_ref[...])
        for m in mat_refs[1:]:
            acc += mm(m[...], home_ref[...])
        if quarters:
            whole = rest[-1]
            whole[...] = acc
            for d in range(4):
                at = pl.multiple_of(lax.rem(s[1] + d, 4) * (cols // 4), 128)
                rest[d][...] = whole[:, pl.ds(at, cols // 4)].astype(BF16)
        else:
            rest[0][...] = acc.astype(BF16)

    if quarters:
        dims, k, extra = (toks, cols // 4), 4, [pltpu.VMEM((toks, cols), F32)]
    else:
        dims, k, extra = (toks, cols), 1, []
    return call(
        kernel,
        [shape(*dims)] * k,
        (1,),
        [block((toks, slots))] * n + [block((slots, cols))],
        [block(dims)] * k,
        extra,
        mib=12,
    )(scal, *mats, home)


def grad_in(scal, routed, dgu):
    rows, features = routed.shape
    ff = dgu.shape[1] // 2
    kb = features // 4

    def kernel(s, left_ref, dgu_ref, gg_ref, gu_ref):
        res = mm(left_ref[...], dgu_ref[...], TN).astype(BF16)
        gg_ref[...] = res[:, :ff]
        gu_ref[...] = res[:, ff:]

    return call(
        kernel,
        [pltpu.HBM((features, ff), BF16)] * 2,
        (4,),
        [pl.BlockSpec((rows, kb), lambda k, s: (0, k)), block(dgu.shape)],
        [pl.BlockSpec((kb, ff), lambda k, s: (k, 0))] * 2,
        mib=20,
    )(scal, *in_hbm(routed), dgu)


def grad_out(scal, hid, chunks):
    rows, cols = chunks[0].shape
    ff = hid.shape[1]

    def kernel(s, hid_ref, *refs):
        for j in range(8):
            at = pl.multiple_of(chunk_index(s, j) * cols, 128)
            refs[8][:, pl.ds(at, cols)] = mm(hid_ref[...], refs[j][...], TN).astype(BF16)

    return call(
        kernel,
        pltpu.HBM((ff, 8 * cols), BF16),
        (1,),
        [block((rows, ff))] + [block((rows, cols))] * 8,
        block((ff, 8 * cols)),
        mib=20,
    )(scal, hid, *in_hbm(*chunks))


def assemble(scal, chunks):
    rows, cols = chunks[0].shape

    def kernel(s, *refs):
        for j in range(8):
            at = pl.multiple_of(chunk_index(s, j) * cols, 128)
            refs[8][:, pl.ds(at, cols)] = refs[j][...]

    return call(
        kernel,
        shape(rows, 8 * cols),
        (1,),
        [block((rows, cols))] * 8,
        block((rows, 8 * cols)),
        mib=8,
    )(scal, *chunks)


def swap(v, axis="c"):
    return lax.ppermute(v, axis, [(0, 1), (1, 0)])


def shift(v, axis, d):
    n = lax.axis_size(axis)
    return lax.ppermute(v, axis, [(i, (i + d) % n) for i in range(n)])


def pairs(dz, dy):
    step = 0 if dy == 0 else 1 if dz % 2 == 0 else -1
    out = []
    for z in range(4):
        for y in range(4):
            to = (y + step) % 4
            out.append(
                ((z * 2 + y % 2) * 2 + y // 2, ((z + dz) % 4 * 2 + to % 2) * 2 + to // 2)
            )
    return out


def exchange(blocks):
    out = list(blocks)
    for r in (4, 5, 2, 3, 6, 7, 1):
        out[r] = lax.ppermute(blocks[r], ("z", "yl", "yh"), pairs(r // 2, r % 2))
    return out


def all_exchange(rows):
    cut = rows.reshape(8, rows.shape[0] // 8, rows.shape[1])
    return lax.all_to_all(cut, EXP, split_axis=0, concat_axis=0, tiled=True).reshape(rows.shape)


def gather_x(v):
    far, right, left = shift(v, "x", -2), shift(v, "x", -1), shift(v, "x", 1)
    return [v, right, far, left]


def after(value, *earlier):
    return lax.optimization_barrier((value, earlier))[0]


def finish(scal, mine):
    total = add(scal, mine, swap(mine, "yh"))
    chunks = gather_x(total)
    return assemble(scal, chunks + [swap(v) for v in chunks])


def on_device(tokens, cotangent, expert_ids, gates, w_gate, w_up, w_down):
    tok_rows, features = tokens.shape
    experts = lax.axis_size("z") * lax.axis_size("yl")
    cap = 3 * tok_rows // experts
    half = features // 2
    wg, wu, wd = w_gate[0], w_up[0], w_down[0]
    c = lax.axis_index("c")
    scal = jnp.stack([c] + [lax.axis_index(a) for a in ("x", "z", "yl")]).astype(jnp.int32)

    t_blocks, d_mine, placing, w_hi, w_lo = route(
        scal, expert_ids, gates, tokens, cotangent, experts, cap
    )
    d_mine = all_exchange(d_mine)

    wg2 = lax.dynamic_slice_in_dim(wg, (1 - c) * half, half, 0)
    wu2 = lax.dynamic_slice_in_dim(wu, (1 - c) * half, half, 0)
    wd2 = lax.dynamic_slice_in_dim(wd, (1 - c) * half, half, 1)
    d_mine, t_blocks, wg2, wu2, wd2 = lax.optimization_barrier((d_mine, t_blocks, wg2, wu2, wd2))
    wg2, wu2, wd2 = swap(wg2), swap(wu2), swap(wd2)

    d_own = gather_x(d_mine)
    t_own = exchange(t_blocks)
    t_oth = [swap(v) for v in t_own]
    d_chunks = d_own + [swap(v) for v in d_own]

    hid, silu, dsilu, routed = gate_up(scal, t_own, t_oth, wg, wu)
    hid2 = swap(hid)
    dgu = back_hidden(scal, d_chunks, wd, silu, dsilu)
    dgu2 = swap(dgu)

    out = out_half(scal, hid, hid2, wd, wd2)
    home = all_exchange(out)

    dgu, dgu2 = after((dgu, dgu2), out)
    parts, sent = {}, []
    for d in (2, 1, 3, 0):
        parts[d] = in_part(scal, d, dgu, dgu2, wg, wu, wg2, wu2)
        if d:
            sent.append(shift(parts[d], "x", d))
    home, parts[0] = lax.optimization_barrier((home, parts[0]))
    quarters = combine(scal, [w_hi, w_lo], home, True)
    m_sent = [shift(quarters[d], "x", d) for d in (2, 1, 3)]
    grad_down = grad_out(scal, after(hid, parts[0]), d_chunks)
    sent, grad_down = lax.optimization_barrier((sent, grad_down))
    g_home = add(scal, parts[0], *sent)
    grad_gate, grad_up = grad_in(scal, routed, after(dgu, g_home))
    g_home = all_exchange(g_home)
    g_home, grad_gate, grad_up = lax.optimization_barrier((g_home, grad_gate, grad_up))
    g_mine = combine(scal, [placing], g_home, False)[0]
    g_mine, m_sent = lax.optimization_barrier((g_mine, m_sent))
    token_grad = finish(scal, g_mine)
    mixed = finish(scal, add(scal, quarters[0], *m_sent))
    return (mixed, token_grad, grad_gate[None], grad_up[None], grad_down[None])


def solution(mesh):
    fine = Mesh(mesh.devices.reshape(4, 2, 2, 4, 2), ("z", "yl", "yh", "x", "c"))
    placed = (
        P(EXP, None),
        P(EXP, None),
        P(EXP, None),
        P(EXP, None),
        P(EXP, None, TEN),
        P(EXP, None, TEN),
        P(EXP, TEN, None),
    )
    return jax.shard_map(
        on_device,
        mesh=fine,
        in_specs=placed,
        out_specs=(
            P(EXP, None),
            P(EXP, None),
            P(EXP, None, TEN),
            P(EXP, None, TEN),
            P(EXP, TEN, None),
        ),
        check_vma=False,
    )
```

time: 492 us -> 218 us (0.44)
  waiting for transfers between devices: 299 us -> 53.8 us
  Pallas kernels: 0 us -> 78 us
  matrix products: 75.5 us -> 0 us
  starting transfers between devices: 11.8 us -> 72.6 us
  local copies, waits for them, and re-layouts: 64.2 us -> 12.2 us
  blocking collectives: 22.1 us -> 0 us
  between operations: 13.9 us -> 0.99 us
    unnamed x6 -> x0, waiting for transfers between devices: 127 us -> none
    all_gather x2 -> x0, waiting for transfers between devices: 83.5 us -> none  [bring_home(): whole = lax.all_gather(arrived, 'tensor', axis=2, tiled=True)]
    pallas_call x0 -> x18, Pallas kernels: none -> 78 us  [the longest x4 18.1 us: in_part(): call(kernel, pltpu.HBM((rows, cols), BF16), (1,), [block((rows, 2 * ff))]...]
    all_to_all x2 -> x3, waiting for transfers between devices: 89.2 us -> 12.7 us  [all_exchange(): lax.all_to_all(cut, EXP, split_axis=0, concat_axis=0, tiled=True)]
    dot_general x13 -> x0, matrix products: 75.5 us -> none  [the longest x8 45.6 us: contract(): lax.dot_general(left_arr, right_arr, (((left_dim,), (right_dim,)), ((), (...]
    ppermute x0 -> x49, starting transfers between devices: none -> 56.6 us  [the longest x27 31.6 us: swap(): return lax.ppermute(v, axis, [(0, 1), (1, 0)])]
    ppermute x0 -> x49, waiting for transfers between devices: none -> 41.1 us  [the longest x15 19.6 us: shift(): return lax.ppermute(v, axis, [(i, (i + d) % n) for i in range(n)])]
    unnamed x29 -> x66, local copies, waits for them, and re-layouts: 44.5 us -> 6.09 us
  transfers between devices with their start and end apart: 6 -> 52, of which waited for: 6 -> 13; matrix products, arithmetic and copies ran while one was open for 18% -> 3% of each run, Pallas kernels for 0% -> 31%
where the time goes in v1:
time: 218 us
  Pallas kernels  78 us (36%)
  starting transfers between devices  72.6 us (33%)
  waiting for transfers between devices  53.8 us (25%)
  local copies, waits for them, and re-layouts  12.2 us (6%)
    ppermute x27, starting transfers between devices, swap(): return lax.ppermute(v, axis, [(0, 1), (1, 0)])  31.6 us
    ppermute x15, waiting for transfers between devices, shift(): return lax.ppermute(v, axis, [(i, (i + d) % n) for i in range(n)])  19.6 us
    pallas_call x4, Pallas kernels, in_part(): call(kernel, pltpu.HBM((rows, cols), BF16), (1,), [block((rows, 2 * ff))]...  18.1 us
    ppermute x7, waiting for transfers between devices, exchange(): out[r] = lax.ppermute(blocks[r], ('z', 'yl', 'yh'), pairs(r // 2, r % 2))  16.6 us
    all_to_all x3, starting transfers between devices, all_exchange(): lax.all_to_all(cut, EXP, split_axis=0, concat_axis=0, tiled=True)  16 us
    ppermute x15, starting transfers between devices, shift(): return lax.ppermute(v, axis, [(i, (i + d) % n) for i in range(n)])  15.7 us
    all_to_all x3, waiting for transfers between devices, all_exchange(): lax.all_to_all(cut, EXP, split_axis=0, concat_axis=0, tiled=True)  12.7 us
    pallas_call x1, Pallas kernels, gate_up(): call(kernel, [pltpu.VMEM((rows, ff), BF16), pltpu.VMEM((rows, ff), F32),...  10.5 us
  transfers between devices with their start and end apart: 52, of which 13 were waited for; matrix products, arithmetic and copies ran while one was open for 3% of the time, Pallas kernels for 31%

profile of v1, /device:TPU:1, one launch (start us, length us, event | category | flops | bytes accessed | tf_op | source)
XLA Modules:
  0.0 217.7 jit_solution(3269786807573939837)
XLA Ops:
  0.7 0.7 copy-done.7
  1.4 0.7 copy-done.8
  2.1 5.7 %shard_map.110 = (bf16[96,1536]{1,0:T(8,128)(2,1)}, bf16[96,1536]{1,0:T(8,128)(2,1)}, bf16[96,1536]{1,0:T(8,128)(2,1)}, bf16[96,1536]{1,0:T(8,128)(2,1)}, bf16[9...) custom-call(s32[4]{0:T(128)S(1)} %pad_add_fusion.s, ...), custom_call_target="tpu_custom_call" | custom-call | tf_op jit(solution)/shard_map/pallas_call | solution.py:101
  7.8 0.8 copy-done.3
  8.6 0.8 copy-done.5
  9.3 6.9 %all-to-all-start = ((bf16[8,96,384]{2,1,0:T(8,128)(2,1)}), bf16[8,96,384]{2,1,0:T(8,128)(2,1)}, u32[]{:S(2)}, u32[]{:S(2)}) async-start(bf16[8,96,384]{2,1,0:T(8,128)(2,1)} %bitcast.6), calls=%async_computation | async-start | bytes 1179648 | tf_op jit(solution)/shard_map/all_to_all | solution.py:392
  16.2 2.8 %dynamic-slice_bitcast_fusion = bf16[512,1536]{1,0:T(8,128)(2,1)} fusion(bf16[1,512,3072]{2,1,0:T(8,128)(2,1)} %param.13, s32[]{:T(128)S(6)} %select_n.2), kind=kLoop, calls=%fused_computation | loop fusion | bytes 3145732 | tf_op jit(solution)/shard_map/dynamic_slice | solution.py:426
  19.0 3.3 %dynamic-slice_bitcast_fusion.1 = (bf16[1536,512]{1,0:T(8,128)(2,1)}, bf16[1536,512]{1,0:T(8,128)(2,1)}) fusion(bf16[1,3072,512]{2,1,0:T(8,128)(2,1)} %param.12, s32[]{:T(128)S(6)} %select_n.2, bf16[1,3072,512]{2,1,0:T(8,128)(2,1)S(1)} %copy-done.9), kind=kLoop, calls=%fused_computation.1 | loop fusion | bytes 6291460 | tf_op jit(solution)/shard_map/dynamic_slice | solution.py:425
  22.4 3.8 %all-to-all-done = bf16[8,96,384]{2,1,0:T(8,128)(2,1)} async-done(((bf16[8,96,384]{2,1,0:T(8,128)(2,1)}), bf16[8,96,384]{2,1,0:T(8,128)(2,1)}, u32[]{:S(2)}, u32[]{:S(2)}) %all-to-all-start) | async-done | bytes 589856 | tf_op jit(solution)/shard_map/all_to_all | solution.py:392
  26.2 2.1 collective-permute-start.2
  28.3 1.8 collective-permute-start.3
  30.1 2.6 %collective-permute-start.5 = (bf16[96,1536]{1,0:T(8,128)(2,1)}, bf16[96,1536]{1,0:T(8,128)(2,1)S(1)}, u32[]{:S(2)}, u32[]{:S(2)}) collective-permute-start(bf16[96,1536]{1,0:T(8,128)(2,1)} %get-tuple-element.73), channel_id=1, source_target_pairs={{0,96},{16,112},{8,104},{24,120},{32,0},{48,16},{40,8},{56,24},{64... | collective-permute-start | bytes 884744 | tf_op jit(solution)/shard_map/ppermute | solution.py:386
  32.7 2.7 %collective-permute-start.6 = (bf16[96,1536]{1,0:T(8,128)(2,1)}, bf16[96,1536]{1,0:T(8,128)(2,1)S(1)}, u32[]{:S(2)}, u32[]{:S(2)}) collective-permute-start(bf16[96,1536]{1,0:T(8,128)(2,1)} %get-tuple-element.74), channel_id=1, source_target_pairs={{0,120},{16,96},{8,112},{24,104},{32,24},{48,0},{40,16},{56,8},{64... | collective-permute-start | bytes 884744 | tf_op jit(solution)/shard_map/ppermute | solution.py:386
  35.5 14.8 %collective-permute-done.3.refs_4_ = bf16[96,1536]{1,0:T(8,128)(2,1)S(1)} collective-permute-done((bf16[96,1536]{1,0:T(8,128)(2,1)}, bf16[96,1536]{1,0:T(8,128)(2,1)S(1)}, u32[]{:S(2)}, u32[]{:S(2)}) %collective-permute-start.3) | collective-permute-done | bytes 294944 | tf_op jit(solution)/shard_map/ppermute | solution.py:386
  50.3 4.4 %collective-permute-start.7 = (bf16[96,1536]{1,0:T(8,128)(2,1)}, bf16[96,1536]{1,0:T(8,128)(2,1)S(1)}, u32[]{:S(2)}, u32[]{:S(2)}) collective-permute-start(bf16[96,1536]{1,0:T(8,128)(2,1)} %get-tuple-element.67.refs_0_), channel_id=1, source_target_pairs={{0,1},{1,0},{2,3},{3,2},{4,5},{5,4},{6,7},{7,6},{8,9},{9,8},{10,11... | collective-permute-start | bytes 884744 | tf_op jit(solution)/shard_map/ppermute | solution.py:363
  54.7 1.7 collective-permute-done.5.refs_6_
  56.4 1.5 collective-permute-start.10
  58.5 3.6 %collective-permute-start.13 = (bf16[96,1536]{1,0:T(8,128)(2,1)S(1)}, bf16[96,1536]{1,0:T(8,128)(2,1)S(1)}, u32[]{:S(2)}, u32[]{:S(2)}) collective-permute-start(bf16[96,1536]{1,0:T(8,128)(2,1)S(1)} %collective-permute-done.5.refs_6_), channel_id=1, source_target_pairs={{0,1},{1,0},{2,3},{3,2},{4,5},{5,4},{6,7},{7,6},{8,9},{9,8},{10,11... | collective-permute-start | bytes 884744 | tf_op jit(solution)/shard_map/ppermute | solution.py:363
  63.3 2.5 %collective-permute-start.17 = (bf16[768,384]{1,0:T(8,128)(2,1)}, bf16[768,384]{1,0:T(8,128)(2,1)S(1)}, u32[]{:S(2)}, u32[]{:S(2)}) collective-permute-start(bf16[768,384]{1,0:T(8,128)(2,1)} %bitcast.7.refs_0_), channel_id=1, source_target_pairs={{0,6},{2,0},{4,2},{6,4},{1,7},{3,1},{5,3},{7,5},{8,14},{10,8},{12,... | collective-permute-start | bytes 1769480 | tf_op jit(solution)/shard_map/ppermute | solution.py:368
  65.7 0.7 collective-permute-start.18
  66.9 1.2 collective-permute-start.20
  68.2 10.5 %shard_map.111 = (bf16[768,512]{1,0:T(8,128)(2,1)S(1)}, f32[768,512]{1,0:T(8,128)S(1)}, f32[768,512]{1,0:T(8,128)S(1)}, bf16[768,3072]{1,0:T(8,128)(2,1)}) custom-call(s32[4]{0:T(128)S(1)} %pad_add_fusion.s, bf16[96,1536]{1,0:T(8,128)(2,1)} %get-tuple-element.67.refs_0_, bf16[96,1536]{1,0:T(8,128)(2,1)} %copy-done.23, bf16[96,1536]{1,0:T(8,128)(2,1)} %copy-done.24, ...), custom_call_target="tpu_custom_call" | custom-call | tf_op jit(solution)/shard_map/pallas_call | solution.py:163
  78.7 12.2 %collective-permute-done.17.refs_1_ = bf16[768,384]{1,0:T(8,128)(2,1)S(1)} collective-permute-done((bf16[768,384]{1,0:T(8,128)(2,1)}, bf16[768,384]{1,0:T(8,128)(2,1)S(1)}, u32[]{:S(2)}, u32[]{:S(2)}) %collective-permute-start.17) | collective-permute-done | bytes 589856 | tf_op jit(solution)/shard_map/ppermute | solution.py:368
  90.9 1.4 collective-permute-start.15
  92.4 3.0 %collective-permute-done.19.refs_3_ = bf16[768,384]{1,0:T(8,128)(2,1)S(1)} collective-permute-done((bf16[768,384]{1,0:T(8,128)(2,1)}, bf16[768,384]{1,0:T(8,128)(2,1)S(1)}, u32[]{:S(2)}, u32[]{:S(2)}) %collective-permute-start.19) | collective-permute-done | bytes 589856 | tf_op jit(solution)/shard_map/ppermute | solution.py:368
  95.9 1.5 collective-permute-done.22.refs_6_
  97.5 0.8 collective-permute-done.23.refs_7_
  98.4 0.8 copy-done.16
  99.2 7.3 %shard_map.113.m.dgu_ref = bf16[768,1024]{1,0:T(8,128)(2,1)S(1)} custom-call(s32[4]{0:T(128)S(1)} %pad_add_fusion.s, bf16[768,384]{1,0:T(8,128)(2,1)} %bitcast.7.refs_0_, bf16[768,384]{1,0:T(8,128)(2,1)} %copy-done.10, bf16[768,384]{1,0:T(8,128)(2,1)} %copy-done.11, bf16[768,384]{1,0:T(8,128)(2,1)} %copy-done.12, bf16[768,384]{1,0:T(8,128)(2,1)} %copy-done.13, ...), custom_call_target="tpu_custom_call" | custom-call | tf_op jit(solution)/shard_map/pallas_call | solution.py:197
  107.5 1.1 copy-done.17
  108.6 5.7 %shard_map.112 = bf16[768,1536]{1,0:T(8,128)(2,1)} custom-call(s32[4]{0:T(128)S(1)} %pad_add_fusion.s, bf16[768,512]{1,0:T(8,128)(2,1)S(1)} %get-tuple-element.88.h0.hid_ref, bf16[768,512]{1,0:T(8,128)(2,1)S(1)} %collective-permute-done.15.h1, bf16[512,3072]{1,0:T(8,128)(2,1)} %bitcast.38, bf16[512,1536]{1,0:T(8,128)(2,1)} %copy-done.17), custom_call_target="tpu_custom_call" | custom-call | tf_op jit(solution)/shard_map/pallas_call | solution.py:237
  114.4 4.4 %all-to-all-start.1 = ((bf16[8,96,1536]{2,1,0:T(8,128)(2,1)}), bf16[8,96,1536]{2,1,0:T(8,128)(2,1)}, u32[]{:S(2)}, u32[]{:S(2)}) async-start(bf16[8,96,1536]{2,1,0:T(8,128)(2,1)} %bitcast.39), calls=%async_computation.1 | async-start | bytes 4718592 | tf_op jit(solution)/shard_map/all_to_all | solution.py:392
  118.8 4.5 %shard_map.118 = bf16[768,384]{1,0:T(8,128)(2,1)} custom-call(s32[4]{0:T(128)S(1)} %pad_add_fusion.s, bf16[768,1024]{1,0:T(8,128)(2,1)S(1)} %shard_map.113.m.dgu_ref, bf16[768,1024]{1,0:T(8,128)(2,1)S(1)} %collective-permute-done.24.t, bf16[3072,512]{1,0:T(8,128)(2,1)} %bitcast.28, bf16[3072,512]{1,0:T(8,128)(2,1)} %bitcast.33, ...), custom_call_target="tpu_custom_call" | custom-call | tf_op jit(solution)/shard_map/pallas_call | solution.py:217
  123.3 1.7 collective-permute-start.29
  125.0 4.5 %shard_map.117 = bf16[768,384]{1,0:T(8,128)(2,1)} custom-call(s32[4]{0:T(128)S(1)} %pad_add_fusion.s, bf16[768,1024]{1,0:T(8,128)(2,1)S(1)} %shard_map.113.m.dgu_ref, bf16[768,1024]{1,0:T(8,128)(2,1)S(1)} %collective-permute-done.24.t, bf16[3072,512]{1,0:T(8,128)(2,1)} %bitcast.29, bf16[3072,512]{1,0:T(8,128)(2,1)} %bitcast.34, ...), custom_call_target="tpu_custom_call" | custom-call | tf_op jit(solution)/shard_map/pallas_call | solution.py:217
  129.5 4.5 %shard_map.116 = bf16[768,384]{1,0:T(8,128)(2,1)} custom-call(s32[4]{0:T(128)S(1)} %pad_add_fusion.s, bf16[768,1024]{1,0:T(8,128)(2,1)S(1)} %shard_map.113.m.dgu_ref, bf16[768,1024]{1,0:T(8,128)(2,1)S(1)} %collective-permute-done.24.t, bf16[3072,512]{1,0:T(8,128)(2,1)} %bitcast.30, bf16[3072,512]{1,0:T(8,128)(2,1)} %bitcast.35, ...), custom_call_target="tpu_custom_call" | custom-call | tf_op jit(solution)/shard_map/pallas_call | solution.py:217
  134.0 1.2 collective-permute-start.27
  135.2 4.5 %shard_map.114.refs_0_ = bf16[768,384]{1,0:T(8,128)(2,1)} custom-call(s32[4]{0:T(128)S(1)} %pad_add_fusion.s, bf16[768,1024]{1,0:T(8,128)(2,1)S(1)} %shard_map.113.m.dgu_ref, bf16[768,1024]{1,0:T(8,128)(2,1)S(1)} %collective-permute-done.24.t, bf16[3072,512]{1,0:T(8,128)(2,1)} %bitcast.31, bf16[3072,512]{1,0:T(8,128)(2,1)} %bitcast.36, ...), custom_call_target="tpu_custom_call" | custom-call | tf_op jit(solution)/shard_map/pallas_call | solution.py:217
  139.7 8.8 %all-to-all-done.1 = bf16[8,96,1536]{2,1,0:T(8,128)(2,1)} async-done(((bf16[8,96,1536]{2,1,0:T(8,128)(2,1)}), bf16[8,96,1536]{2,1,0:T(8,128)(2,1)}, u32[]{:S(2)}, u32[]{:S(2)}) %all-to-all-start.1) | async-done | bytes 2359328 | tf_op jit(solution)/shard_map/all_to_all | solution.py:392
  148.6 1.1 copy-done.1
  149.7 8.0 %shard_map.119 = bf16[512,3072]{1,0:T(8,128)(2,1)} custom-call(s32[4]{0:T(128)S(1)} %pad_add_fusion.s, bf16[768,512]{1,0:T(8,128)(2,1)S(1)} %copy-done.1, bf16[768,384]{1,0:T(8,128)(2,1)} %bitcast.7.refs_0_, bf16[768,384]{1,0:T(8,128)(2,1)} %copy-done.10, bf16[768,384]{1,0:T(8,128)(2,1)} %copy-done.11, bf16[768,384]{1,0:T(8,128)(2,1)} %copy-done.12, ...), custom_call_target="tpu_custom_call" | custom-call | tf_op jit(solution)/shard_map/pallas_call | solution.py:334
  158.2 3.1 %shard_map.120 = bf16[768,384]{1,0:T(8,128)(2,1)} custom-call(s32[4]{0:T(128)S(1)} %pad_add_fusion.s, bf16[768,384]{1,0:T(8,128)(2,1)S(1)} %copy-done.2, bf16[768,384]{1,0:T(8,128)(2,1)} %collective-permute-done.27.refs_1_, bf16[768,384]{1,0:T(8,128)(2,1)} %collective-permute-done.28.refs_2_, bf16[768,384]{1,0:T(8,128)(2,1)} %collective-permute-done.29.refs_3_), custom_call_target="tpu_custom_call" | custom-call | tf_op jit(solution)/shard_map/pallas_call | solution.py:261
  161.3 4.7 %all-to-all-start.2 = ((bf16[8,96,384]{2,1,0:T(8,128)(2,1)}), bf16[8,96,384]{2,1,0:T(8,128)(2,1)S(1)}, u32[]{:S(2)}, u32[]{:S(2)}) async-start(bf16[8,96,384]{2,1,0:T(8,128)(2,1)} %bitcast.16), calls=%async_computation.2 | async-start | bytes 1179648 | tf_op jit(solution)/shard_map/all_to_all | solution.py:392
  166.0 4.6 %shard_map.115 = (bf16[256,384]{1,0:T(8,128)(2,1)S(1)}, bf16[256,384]{1,0:T(8,128)(2,1)}, bf16[256,384]{1,0:T(8,128)(2,1)}, bf16[256,384]{1,0:T(8,128)(2,1)}) custom-call(s32[4]{0:T(128)S(1)} %pad_add_fusion.s, bf16[256,768]{1,0:T(8,128)(2,1)S(1)} %copy-done.4, bf16[256,768]{1,0:T(8,128)(2,1)S(1)} %copy-done.6, bf16[768,1536]{1,0:T(8,128)(2,1)} %bitcast.15.refs_2_), custom_call_target="tpu_custom_call" | custom-call | tf_op jit(solution)/shard_map/pallas_call | solution.py:294
  171.3 2.5 %collective-permute-start.32 = (bf16[256,384]{1,0:T(8,128)(2,1)}, bf16[256,384]{1,0:T(8,128)(2,1)S(1)}, u32[]{:S(2)}, u32[]{:S(2)}) collective-permute-start(bf16[256,384]{1,0:T(8,128)(2,1)} %get-tuple-element.99), channel_id=1, source_target_pairs={{0,6},{2,0},{4,2},{6,4},{1,7},{3,1},{5,3},{7,5},{8,14},{10,8},{12,... | collective-permute-start | bytes 589832 | tf_op jit(solution)/shard_map/ppermute | solution.py:368
  173.8 8.5 %shard_map.121 = (bf16[3072,512]{1,0:T(8,128)(2,1)}, bf16[3072,512]{1,0:T(8,128)(2,1)}) custom-call(s32[4]{0:T(128)S(1)} %pad_add_fusion.s, bf16[768,3072]{1,0:T(8,128)(2,1)} %get-tuple-element.92.left_ref, bf16[768,1024]{1,0:T(8,128)(2,1)S(1)} %shard_map.113.m.dgu_ref), custom_call_target="tpu_custom_call" | custom-call | tf_op jit(solution)/shard_map/pallas_call | solution.py:315
  182.3 0.9 shard_map.122.refs_0_
  183.3 1.5 collective-permute-start.41
  184.8 0.6 shard_map.123.refs_0_
  185.4 1.6 collective-permute-start.33
  187.0 2.3 %collective-permute-done.41.refs_1_ = bf16[256,384]{1,0:T(8,128)(2,1)S(1)} collective-permute-done((bf16[256,384]{1,0:T(8,128)(2,1)S(1)}, bf16[256,384]{1,0:T(8,128)(2,1)S(1)}, u32[]{:S(2)}, u32[]{:S(2)}) %collective-permute-start.41) | collective-permute-done | bytes 196640 | tf_op jit(solution)/shard_map/ppermute | solution.py:363
  189.4 0.6 shard_map.126.refs_0_
  190.1 1.3 collective-permute-start.43
  191.4 0.8 collective-permute-start.44
  192.1 5.8 %collective-permute-start.45 = (bf16[256,384]{1,0:T(8,128)(2,1)S(1)}, bf16[256,384]{1,0:T(8,128)(2,1)S(1)}, u32[]{:S(2)}, u32[]{:S(2)}) collective-permute-start(bf16[256,384]{1,0:T(8,128)(2,1)S(1)} %shard_map.126.refs_0_), channel_id=1, source_target_pairs={{0,1},{1,0},{2,3},{3,2},{4,5},{5,4},{6,7},{7,6},{8,9},{9,8},{10,11... | collective-permute-start | bytes 589832 | tf_op jit(solution)/shard_map/ppermute | solution.py:363
  198.5 1.9 collective-permute-start.34
  200.4 1.2 collective-permute-start.35
  201.6 0.8 collective-permute-start.36
  202.4 2.2 %collective-permute-start.46 = (bf16[256,384]{1,0:T(8,128)(2,1)S(1)}, bf16[256,384]{1,0:T(8,128)(2,1)S(1)}, u32[]{:S(2)}, u32[]{:S(2)}) collective-permute-start(bf16[256,384]{1,0:T(8,128)(2,1)S(1)} %collective-permute-done.42.refs_1_), channel_id=1, source_target_pairs={{0,1},{1,0},{2,3},{3,2},{4,5},{5,4},{6,7},{7,6},{8,9},{9,8},{10,11... | collective-permute-start | bytes 589832 | tf_op jit(solution)/shard_map/ppermute | solution.py:363
  204.6 1.6 collective-permute-done.34.refs_1_
  206.2 4.3 %collective-permute-start.37 = (bf16[256,384]{1,0:T(8,128)(2,1)S(1)}, bf16[256,384]{1,0:T(8,128)(2,1)S(1)}, u32[]{:S(2)}, u32[]{:S(2)}) collective-permute-start(bf16[256,384]{1,0:T(8,128)(2,1)S(1)} %shard_map.124.refs_0_), channel_id=1, source_target_pairs={{0,1},{1,0},{2,3},{3,2},{4,5},{5,4},{6,7},{7,6},{8,9},{9,8},{10,11... | collective-permute-start | bytes 589832 | tf_op jit(solution)/shard_map/ppermute | solution.py:363
  210.5 2.5 %collective-permute-done.36.refs_3_ = bf16[256,384]{1,0:T(8,128)(2,1)S(1)} collective-permute-done((bf16[256,384]{1,0:T(8,128)(2,1)S(1)}, bf16[256,384]{1,0:T(8,128)(2,1)S(1)}, u32[]{:S(2)}, u32[]{:S(2)}) %collective-permute-start.36) | collective-permute-done | bytes 196640 | tf_op jit(solution)/shard_map/ppermute | solution.py:368
  214.0 1.8 shard_map.127
  215.8 1.8 shard_map.125
  (127 shorter events, 6.9 us)
Async XLA Ops:
  9.3 16.9 %all-to-all-start = ((bf16[8,96,384]{2,1,0:T(8,128)(2,1)}), bf16[8,96,384]{2,1,0:T(8,128)(2,1)}, u32[]{:S(2)}, u32[]{:S(2)}) async-start(bf16[8,96,384]{2,1,0:T(8,128)(2,1)} %bitcast.6), calls=%async_computation | async-start | bytes 1179648 | tf_op jit(solution)/shard_map/all_to_all | solution.py:392
  26.2 9.3 %collective-permute-start.2 = (bf16[96,1536]{1,0:T(8,128)(2,1)}, bf16[96,1536]{1,0:T(8,128)(2,1)S(1)}, u32[]{:S(2)}, u32[]{:S(2)}) collective-permute-start(bf16[96,1536]{1,0:T(8,128)(2,1)} %get-tuple-element.70), channel_id=1, source_target_pairs={{0,56},{16,32},{8,48},{24,40},{32,88},{48,64},{40,80},{56,72},{64,... | collective-permute-start | bytes 884744 | tf_op jit(solution)/shard_map/ppermute | solution.py:386
  28.3 22.0 %collective-permute-start.3 = (bf16[96,1536]{1,0:T(8,128)(2,1)}, bf16[96,1536]{1,0:T(8,128)(2,1)S(1)}, u32[]{:S(2)}, u32[]{:S(2)}) collective-permute-start(bf16[96,1536]{1,0:T(8,128)(2,1)} %get-tuple-element.71), channel_id=1, source_target_pairs={{0,64},{16,80},{8,72},{24,88},{32,96},{48,112},{40,104},{56,120},{... | collective-permute-start | bytes 884744 | tf_op jit(solution)/shard_map/ppermute | solution.py:386
  30.1 20.2 %collective-permute-start.4 = (bf16[96,1536]{1,0:T(8,128)(2,1)}, bf16[96,1536]{1,0:T(8,128)(2,1)S(1)}, u32[]{:S(2)}, u32[]{:S(2)}) collective-permute-start(bf16[96,1536]{1,0:T(8,128)(2,1)} %get-tuple-element.72), channel_id=1, source_target_pairs={{0,80},{16,72},{8,88},{24,64},{32,112},{48,104},{40,120},{56,96},{... | collective-permute-start | bytes 884744 | tf_op jit(solution)/shard_map/ppermute | solution.py:386
  30.1 26.3 %collective-permute-start.5 = (bf16[96,1536]{1,0:T(8,128)(2,1)}, bf16[96,1536]{1,0:T(8,128)(2,1)S(1)}, u32[]{:S(2)}, u32[]{:S(2)}) collective-permute-start(bf16[96,1536]{1,0:T(8,128)(2,1)} %get-tuple-element.73), channel_id=1, source_target_pairs={{0,96},{16,112},{8,104},{24,120},{32,0},{48,16},{40,8},{56,24},{64... | collective-permute-start | bytes 884744 | tf_op jit(solution)/shard_map/ppermute | solution.py:386
  32.7 25.2 %collective-permute-start.6 = (bf16[96,1536]{1,0:T(8,128)(2,1)}, bf16[96,1536]{1,0:T(8,128)(2,1)S(1)}, u32[]{:S(2)}, u32[]{:S(2)}) collective-permute-start(bf16[96,1536]{1,0:T(8,128)(2,1)} %get-tuple-element.74), channel_id=1, source_target_pairs={{0,120},{16,96},{8,112},{24,104},{32,24},{48,0},{40,16},{56,8},{64... | collective-permute-start | bytes 884744 | tf_op jit(solution)/shard_map/ppermute | solution.py:386
  35.5 32.6 %copy-start.18 = (bf16[96,1536]{1,0:T(8,128)(2,1)}, bf16[96,1536]{1,0:T(8,128)(2,1)S(1)}, u32[]{:S(2)}) copy-start(bf16[96,1536]{1,0:T(8,128)(2,1)S(1)} %collective-permute-done.2.refs_3_) | copy-start | bytes 884740
  35.5 22.6 %collective-permute-start = (bf16[96,1536]{1,0:T(8,128)(2,1)}, bf16[96,1536]{1,0:T(8,128)(2,1)S(1)}, u32[]{:S(2)}, u32[]{:S(2)}) collective-permute-start(bf16[96,1536]{1,0:T(8,128)(2,1)} %get-tuple-element.68), channel_id=1, source_target_pairs={{0,16},{16,8},{8,24},{24,0},{32,48},{48,40},{40,56},{56,32},{64,80... | collective-permute-start | bytes 884744 | tf_op jit(solution)/shard_map/ppermute | solution.py:386
  50.3 17.8 %copy-start.19 = (bf16[96,1536]{1,0:T(8,128)(2,1)}, bf16[96,1536]{1,0:T(8,128)(2,1)S(1)}, u32[]{:S(2)}) copy-start(bf16[96,1536]{1,0:T(8,128)(2,1)S(1)} %collective-permute-done.3.refs_4_) | copy-start | bytes 884740
  50.3 8.1 %collective-permute-start.1 = (bf16[96,1536]{1,0:T(8,128)(2,1)}, bf16[96,1536]{1,0:T(8,128)(2,1)S(1)}, u32[]{:S(2)}, u32[]{:S(2)}) collective-permute-start(bf16[96,1536]{1,0:T(8,128)(2,1)} %get-tuple-element.69), channel_id=1, source_target_pairs={{0,32},{16,48},{8,40},{24,56},{32,64},{48,80},{40,72},{56,88},{64,... | collective-permute-start | bytes 884744 | tf_op jit(solution)/shard_map/ppermute | solution.py:386
  50.3 17.8 %copy-start.20 = (bf16[96,1536]{1,0:T(8,128)(2,1)}, bf16[96,1536]{1,0:T(8,128)(2,1)S(1)}, u32[]{:S(2)}) copy-start(bf16[96,1536]{1,0:T(8,128)(2,1)S(1)} %collective-permute-done.4.refs_5_) | copy-start | bytes 884740
  50.3 11.7 %collective-permute-start.7 = (bf16[96,1536]{1,0:T(8,128)(2,1)}, bf16[96,1536]{1,0:T(8,128)(2,1)S(1)}, u32[]{:S(2)}, u32[]{:S(2)}) collective-permute-start(bf16[96,1536]{1,0:T(8,128)(2,1)} %get-tuple-element.67.refs_0_), channel_id=1, source_target_pairs={{0,1},{1,0},{2,3},{3,2},{4,5},{5,4},{6,7},{7,6},{8,9},{9,8},{10,11... | collective-permute-start | bytes 884744 | tf_op jit(solution)/shard_map/ppermute | solution.py:363
  56.4 11.7 %copy-start.21 = (bf16[96,1536]{1,0:T(8,128)(2,1)}, bf16[96,1536]{1,0:T(8,128)(2,1)S(1)}, u32[]{:S(2)}) copy-start(bf16[96,1536]{1,0:T(8,128)(2,1)S(1)} %collective-permute-done.5.refs_6_) | copy-start | bytes 884740
  56.4 5.7 %collective-permute-start.10 = (bf16[96,1536]{1,0:T(8,128)(2,1)S(1)}, bf16[96,1536]{1,0:T(8,128)(2,1)S(1)}, u32[]{:S(2)}, u32[]{:S(2)}) collective-permute-start(bf16[96,1536]{1,0:T(8,128)(2,1)S(1)} %collective-permute-done.2.refs_3_), channel_id=1, source_target_pairs={{0,1},{1,0},{2,3},{3,2},{4,5},{5,4},{6,7},{7,6},{8,9},{9,8},{10,11... | collective-permute-start | bytes 884744 | tf_op jit(solution)/shard_map/ppermute | solution.py:363
  58.0 10.2 %copy-start.22 = (bf16[96,1536]{1,0:T(8,128)(2,1)}, bf16[96,1536]{1,0:T(8,128)(2,1)S(1)}, u32[]{:S(2)}) copy-start(bf16[96,1536]{1,0:T(8,128)(2,1)S(1)} %collective-permute-done.6.refs_7_) | copy-start | bytes 884740
  58.0 4.6 %collective-permute-start.11 = (bf16[96,1536]{1,0:T(8,128)(2,1)S(1)}, bf16[96,1536]{1,0:T(8,128)(2,1)S(1)}, u32[]{:S(2)}, u32[]{:S(2)}) collective-permute-start(bf16[96,1536]{1,0:T(8,128)(2,1)S(1)} %collective-permute-done.3.refs_4_), channel_id=1, source_target_pairs={{0,1},{1,0},{2,3},{3,2},{4,5},{5,4},{6,7},{7,6},{8,9},{9,8},{10,11... | collective-permute-start | bytes 884744 | tf_op jit(solution)/shard_map/ppermute | solution.py:363
  58.0 10.1 %copy-start.23 = (bf16[96,1536]{1,0:T(8,128)(2,1)}, bf16[96,1536]{1,0:T(8,128)(2,1)S(1)}, u32[]{:S(2)}) copy-start(bf16[96,1536]{1,0:T(8,128)(2,1)S(1)} %collective-permute-done.refs_1_) | copy-start | bytes 884740
  58.1 4.6 %collective-permute-start.12 = (bf16[96,1536]{1,0:T(8,128)(2,1)S(1)}, bf16[96,1536]{1,0:T(8,128)(2,1)S(1)}, u32[]{:S(2)}, u32[]{:S(2)}) collective-permute-start(bf16[96,1536]{1,0:T(8,128)(2,1)S(1)} %collective-permute-done.4.refs_5_), channel_id=1, source_target_pairs={{0,1},{1,0},{2,3},{3,2},{4,5},{5,4},{6,7},{7,6},{8,9},{9,8},{10,11... | collective-permute-start | bytes 884744 | tf_op jit(solution)/shard_map/ppermute | solution.py:363
  58.5 9.7 %copy-start.24 = (bf16[96,1536]{1,0:T(8,128)(2,1)}, bf16[96,1536]{1,0:T(8,128)(2,1)S(1)}, u32[]{:S(2)}) copy-start(bf16[96,1536]{1,0:T(8,128)(2,1)S(1)} %collective-permute-done.1.refs_2_) | copy-start | bytes 884740
  58.5 4.8 %collective-permute-start.13 = (bf16[96,1536]{1,0:T(8,128)(2,1)S(1)}, bf16[96,1536]{1,0:T(8,128)(2,1)S(1)}, u32[]{:S(2)}, u32[]{:S(2)}) collective-permute-start(bf16[96,1536]{1,0:T(8,128)(2,1)S(1)} %collective-permute-done.5.refs_6_), channel_id=1, source_target_pairs={{0,1},{1,0},{2,3},{3,2},{4,5},{5,4},{6,7},{7,6},{8,9},{9,8},{10,11... | collective-permute-start | bytes 884744 | tf_op jit(solution)/shard_map/ppermute | solution.py:363
  62.0 3.7 %collective-permute-start.14 = (bf16[96,1536]{1,0:T(8,128)(2,1)S(1)}, bf16[96,1536]{1,0:T(8,128)(2,1)S(1)}, u32[]{:S(2)}, u32[]{:S(2)}) collective-permute-start(bf16[96,1536]{1,0:T(8,128)(2,1)S(1)} %collective-permute-done.6.refs_7_), channel_id=1, source_target_pairs={{0,1},{1,0},{2,3},{3,2},{4,5},{5,4},{6,7},{7,6},{8,9},{9,8},{10,11... | collective-permute-start | bytes 884744 | tf_op jit(solution)/shard_map/ppermute | solution.py:363
  62.1 4.3 %collective-permute-start.8 = (bf16[96,1536]{1,0:T(8,128)(2,1)S(1)}, bf16[96,1536]{1,0:T(8,128)(2,1)S(1)}, u32[]{:S(2)}, u32[]{:S(2)}) collective-permute-start(bf16[96,1536]{1,0:T(8,128)(2,1)S(1)} %collective-permute-done.refs_1_), channel_id=1, source_target_pairs={{0,1},{1,0},{2,3},{3,2},{4,5},{5,4},{6,7},{7,6},{8,9},{9,8},{10,11... | collective-permute-start | bytes 884744 | tf_op jit(solution)/shard_map/ppermute | solution.py:363
  62.6 4.3 %collective-permute-start.9 = (bf16[96,1536]{1,0:T(8,128)(2,1)S(1)}, bf16[96,1536]{1,0:T(8,128)(2,1)S(1)}, u32[]{:S(2)}, u32[]{:S(2)}) collective-permute-start(bf16[96,1536]{1,0:T(8,128)(2,1)S(1)} %collective-permute-done.1.refs_2_), channel_id=1, source_target_pairs={{0,1},{1,0},{2,3},{3,2},{4,5},{5,4},{6,7},{7,6},{8,9},{9,8},{10,11... | collective-permute-start | bytes 884744 | tf_op jit(solution)/shard_map/ppermute | solution.py:363
  62.7 44.8 %collective-permute-start.16 = (bf16[512,1536]{1,0:T(8,128)(2,1)}, bf16[512,1536]{1,0:T(8,128)(2,1)S(1)}, u32[]{:S(2)}, u32[]{:S(2)}) collective-permute-start(bf16[512,1536]{1,0:T(8,128)(2,1)} %dynamic-slice_bitcast_fusion), channel_id=1, source_target_pairs={{0,1},{1,0},{2,3},{3,2},{4,5},{5,4},{6,7},{7,6},{8,9},{9,8},{10,11... | collective-permute-start | bytes 4718600 | tf_op jit(solution)/shard_map/ppermute | solution.py:363
  63.3 27.6 %collective-permute-start.17 = (bf16[768,384]{1,0:T(8,128)(2,1)}, bf16[768,384]{1,0:T(8,128)(2,1)S(1)}, u32[]{:S(2)}, u32[]{:S(2)}) collective-permute-start(bf16[768,384]{1,0:T(8,128)(2,1)} %bitcast.7.refs_0_), channel_id=1, source_target_pairs={{0,6},{2,0},{4,2},{6,4},{1,7},{3,1},{5,3},{7,5},{8,14},{10,8},{12,... | collective-permute-start | bytes 1769480 | tf_op jit(solution)/shard_map/ppermute | solution.py:368
  65.7 26.5 %collective-permute-start.18 = (bf16[768,384]{1,0:T(8,128)(2,1)}, bf16[768,384]{1,0:T(8,128)(2,1)S(1)}, u32[]{:S(2)}, u32[]{:S(2)}) collective-permute-start(bf16[768,384]{1,0:T(8,128)(2,1)} %bitcast.7.refs_0_), channel_id=1, source_target_pairs={{0,4},{2,6},{4,0},{6,2},{1,5},{3,7},{5,1},{7,3},{8,12},{10,14},{12... | collective-permute-start | bytes 1769480 | tf_op jit(solution)/shard_map/ppermute | solution.py:368
  66.4 28.9 %collective-permute-start.19 = (bf16[768,384]{1,0:T(8,128)(2,1)}, bf16[768,384]{1,0:T(8,128)(2,1)S(1)}, u32[]{:S(2)}, u32[]{:S(2)}) collective-permute-start(bf16[768,384]{1,0:T(8,128)(2,1)} %bitcast.7.refs_0_), channel_id=1, source_target_pairs={{0,2},{2,4},{4,6},{6,0},{1,3},{3,5},{5,7},{7,1},{8,10},{10,12},{12... | collective-permute-start | bytes 1769480 | tf_op jit(solution)/shard_map/ppermute | solution.py:368
  66.9 29.0 %collective-permute-start.20 = (bf16[768,384]{1,0:T(8,128)(2,1)}, bf16[768,384]{1,0:T(8,128)(2,1)S(1)}, u32[]{:S(2)}, u32[]{:S(2)}) collective-permute-start(bf16[768,384]{1,0:T(8,128)(2,1)} %bitcast.7.refs_0_), channel_id=1, source_target_pairs={{0,1},{1,0},{2,3},{3,2},{4,5},{5,4},{6,7},{7,6},{8,9},{9,8},{10,11... | collective-permute-start | bytes 1769480 | tf_op jit(solution)/shard_map/ppermute | solution.py:363
  78.7 28.8 %copy-start = (bf16[768,512]{1,0:T(8,128)(2,1)}, bf16[768,512]{1,0:T(8,128)(2,1)S(1)}, u32[]{:S(2)}) copy-start(bf16[768,512]{1,0:T(8,128)(2,1)S(1)} %get-tuple-element.88.h0.hid_ref) | copy-start | bytes 2359300
  90.9 7.4 %copy-start.10 = (bf16[768,384]{1,0:T(8,128)(2,1)}, bf16[768,384]{1,0:T(8,128)(2,1)S(1)}, u32[]{:S(2)}) copy-start(bf16[768,384]{1,0:T(8,128)(2,1)S(1)} %collective-permute-done.17.refs_1_) | copy-start | bytes 1769476
  90.9 16.6 %collective-permute-start.15 = (bf16[768,512]{1,0:T(8,128)(2,1)S(1)}, bf16[768,512]{1,0:T(8,128)(2,1)S(1)}, u32[]{:S(2)}, u32[]{:S(2)}) collective-permute-start(bf16[768,512]{1,0:T(8,128)(2,1)S(1)} %get-tuple-element.88.h0.hid_ref), channel_id=1, source_target_pairs={{0,1},{1,0},{2,3},{3,2},{4,5},{5,4},{6,7},{7,6},{8,9},{9,8},{10,11... | collective-permute-start | bytes 2359304 | tf_op jit(solution)/shard_map/ppermute | solution.py:363
  92.3 3.7 %collective-permute-start.21 = (bf16[768,384]{1,0:T(8,128)(2,1)S(1)}, bf16[768,384]{1,0:T(8,128)(2,1)S(1)}, u32[]{:S(2)}, u32[]{:S(2)}) collective-permute-start(bf16[768,384]{1,0:T(8,128)(2,1)S(1)} %collective-permute-done.17.refs_1_), channel_id=1, source_target_pairs={{0,1},{1,0},{2,3},{3,2},{4,5},{5,4},{6,7},{7,6},{8,9},{9,8},{10,11... | collective-permute-start | bytes 1769480 | tf_op jit(solution)/shard_map/ppermute | solution.py:363
  95.3 2.1 collective-permute-start.22
  95.8 2.5 %collective-permute-start.23 = (bf16[768,384]{1,0:T(8,128)(2,1)S(1)}, bf16[768,384]{1,0:T(8,128)(2,1)S(1)}, u32[]{:S(2)}, u32[]{:S(2)}) collective-permute-start(bf16[768,384]{1,0:T(8,128)(2,1)S(1)} %collective-permute-done.19.refs_3_), channel_id=1, source_target_pairs={{0,1},{1,0},{2,3},{3,2},{4,5},{5,4},{6,7},{7,6},{8,9},{9,8},{10,11... | collective-permute-start | bytes 1769480 | tf_op jit(solution)/shard_map/ppermute | solution.py:363
  106.5 12.3 %collective-permute-start.24 = (bf16[768,1024]{1,0:T(8,128)(2,1)S(1)}, bf16[768,1024]{1,0:T(8,128)(2,1)S(1)}, u32[]{:S(2)}, u32[]{:S(2)}) collective-permute-start(bf16[768,1024]{1,0:T(8,128)(2,1)S(1)} %shard_map.113.m.dgu_ref), channel_id=1, source_target_pairs={{0,1},{1,0},{2,3},{3,2},{4,5},{5,4},{6,7},{7,6},{8,9},{9,8},{10,11... | collective-permute-start | bytes 4718600 | tf_op jit(solution)/shard_map/ppermute | solution.py:363
  107.0 11.8 %collective-permute-start.25 = (bf16[1536,512]{1,0:T(8,128)(2,1)}, bf16[1536,512]{1,0:T(8,128)(2,1)}, u32[]{:S(2)}, u32[]{:S(2)}) collective-permute-start(bf16[1536,512]{1,0:T(8,128)(2,1)} %get-tuple-element.82), channel_id=1, source_target_pairs={{0,1},{1,0},{2,3},{3,2},{4,5},{5,4},{6,7},{7,6},{8,9},{9,8},{10,11... | collective-permute-start | bytes 4718600 | tf_op jit(solution)/shard_map/ppermute | solution.py:363
  107.1 11.7 %collective-permute-start.26 = (bf16[1536,512]{1,0:T(8,128)(2,1)}, bf16[1536,512]{1,0:T(8,128)(2,1)}, u32[]{:S(2)}, u32[]{:S(2)}) collective-permute-start(bf16[1536,512]{1,0:T(8,128)(2,1)} %get-tuple-element.83), channel_id=1, source_target_pairs={{0,1},{1,0},{2,3},{3,2},{4,5},{5,4},{6,7},{7,6},{8,9},{9,8},{10,11... | collective-permute-start | bytes 4718600 | tf_op jit(solution)/shard_map/ppermute | solution.py:363
  114.4 34.2 %all-to-all-start.1 = ((bf16[8,96,1536]{2,1,0:T(8,128)(2,1)}), bf16[8,96,1536]{2,1,0:T(8,128)(2,1)}, u32[]{:S(2)}, u32[]{:S(2)}) async-start(bf16[8,96,1536]{2,1,0:T(8,128)(2,1)} %bitcast.39), calls=%async_computation.1 | async-start | bytes 4718592 | tf_op jit(solution)/shard_map/all_to_all | solution.py:392
  123.3 34.4 %collective-permute-start.29 = (bf16[768,384]{1,0:T(8,128)(2,1)}, bf16[768,384]{1,0:T(8,128)(2,1)}, u32[]{:S(2)}, u32[]{:S(2)}) collective-permute-start(bf16[768,384]{1,0:T(8,128)(2,1)} %shard_map.118), channel_id=1, source_target_pairs={{0,6},{2,0},{4,2},{6,4},{1,7},{3,1},{5,3},{7,5},{8,14},{10,8},{12,... | collective-permute-start | bytes 1769480 | tf_op jit(solution)/shard_map/ppermute | solution.py:368
  129.5 28.6 %collective-permute-start.28 = (bf16[768,384]{1,0:T(8,128)(2,1)}, bf16[768,384]{1,0:T(8,128)(2,1)}, u32[]{:S(2)}, u32[]{:S(2)}) collective-permute-start(bf16[768,384]{1,0:T(8,128)(2,1)} %shard_map.117), channel_id=1, source_target_pairs={{0,2},{2,4},{4,6},{6,0},{1,3},{3,5},{5,7},{7,1},{8,10},{10,12},{12... | collective-permute-start | bytes 1769480 | tf_op jit(solution)/shard_map/ppermute | solution.py:368
  134.0 24.1 %collective-permute-start.27 = (bf16[768,384]{1,0:T(8,128)(2,1)}, bf16[768,384]{1,0:T(8,128)(2,1)}, u32[]{:S(2)}, u32[]{:S(2)}) collective-permute-start(bf16[768,384]{1,0:T(8,128)(2,1)} %shard_map.116), channel_id=1, source_target_pairs={{0,4},{2,6},{4,0},{6,2},{1,5},{3,7},{5,1},{7,3},{8,12},{10,14},{12... | collective-permute-start | bytes 1769480 | tf_op jit(solution)/shard_map/ppermute | solution.py:368
  149.7 8.4 %copy-start.2 = (bf16[768,384]{1,0:T(8,128)(2,1)S(1)}, bf16[768,384]{1,0:T(8,128)(2,1)}, u32[]{:S(2)}) copy-start(bf16[768,384]{1,0:T(8,128)(2,1)} %shard_map.114.refs_0_) | copy-start | bytes 1769476
  157.7 8.2 %copy-start.4 = (bf16[256,768]{1,0:T(8,128)(2,1)S(1)}, bf16[256,768]{1,0:T(8,128)(2,1)}, u32[]{:S(2)}) copy-start(bf16[256,768]{1,0:T(8,128)(2,1)} %copy-done.3) | copy-start | bytes 1179652
  157.7 8.2 %copy-start.6 = (bf16[256,768]{1,0:T(8,128)(2,1)S(1)}, bf16[256,768]{1,0:T(8,128)(2,1)}, u32[]{:S(2)}) copy-start(bf16[256,768]{1,0:T(8,128)(2,1)} %copy-done.5) | copy-start | bytes 1179652
  161.3 21.1 %all-to-all-start.2 = ((bf16[8,96,384]{2,1,0:T(8,128)(2,1)}), bf16[8,96,384]{2,1,0:T(8,128)(2,1)S(1)}, u32[]{:S(2)}, u32[]{:S(2)}) async-start(bf16[8,96,384]{2,1,0:T(8,128)(2,1)} %bitcast.16), calls=%async_computation.2 | async-start | bytes 1179648 | tf_op jit(solution)/shard_map/all_to_all | solution.py:392
  170.6 12.7 %collective-permute-start.30 = (bf16[256,384]{1,0:T(8,128)(2,1)}, bf16[256,384]{1,0:T(8,128)(2,1)S(1)}, u32[]{:S(2)}, u32[]{:S(2)}) collective-permute-start(bf16[256,384]{1,0:T(8,128)(2,1)} %get-tuple-element.97), channel_id=1, source_target_pairs={{0,4},{2,6},{4,0},{6,2},{1,5},{3,7},{5,1},{7,3},{8,12},{10,14},{12... | collective-permute-start | bytes 589832 | tf_op jit(solution)/shard_map/ppermute | solution.py:368
  171.1 12.1 %collective-permute-start.31 = (bf16[256,384]{1,0:T(8,128)(2,1)}, bf16[256,384]{1,0:T(8,128)(2,1)S(1)}, u32[]{:S(2)}, u32[]{:S(2)}) collective-permute-start(bf16[256,384]{1,0:T(8,128)(2,1)} %get-tuple-element.98), channel_id=1, source_target_pairs={{0,2},{2,4},{4,6},{6,0},{1,3},{3,5},{5,7},{7,1},{8,10},{10,12},{12... | collective-permute-start | bytes 589832 | tf_op jit(solution)/shard_map/ppermute | solution.py:368
  171.3 12.0 %collective-permute-start.32 = (bf16[256,384]{1,0:T(8,128)(2,1)}, bf16[256,384]{1,0:T(8,128)(2,1)S(1)}, u32[]{:S(2)}, u32[]{:S(2)}) collective-permute-start(bf16[256,384]{1,0:T(8,128)(2,1)} %get-tuple-element.99), channel_id=1, source_target_pairs={{0,6},{2,0},{4,2},{6,4},{1,7},{3,1},{5,3},{7,5},{8,14},{10,8},{12,... | collective-permute-start | bytes 589832 | tf_op jit(solution)/shard_map/ppermute | solution.py:368
  183.3 6.1 %collective-permute-start.41 = (bf16[256,384]{1,0:T(8,128)(2,1)S(1)}, bf16[256,384]{1,0:T(8,128)(2,1)S(1)}, u32[]{:S(2)}, u32[]{:S(2)}) collective-permute-start(bf16[256,384]{1,0:T(8,128)(2,1)S(1)} %shard_map.122.refs_0_), channel_id=1, source_target_pairs={{0,8},{8,0},{1,9},{9,1},{2,10},{10,2},{3,11},{11,3},{4,12},{12,4},... | collective-permute-start | bytes 589832 | tf_op jit(solution)/shard_map/ppermute | solution.py:363
  185.4 12.5 %collective-permute-start.33 = (bf16[256,384]{1,0:T(8,128)(2,1)S(1)}, bf16[256,384]{1,0:T(8,128)(2,1)S(1)}, u32[]{:S(2)}, u32[]{:S(2)}) collective-permute-start(bf16[256,384]{1,0:T(8,128)(2,1)S(1)} %shard_map.123.refs_0_), channel_id=1, source_target_pairs={{0,8},{8,0},{1,9},{9,1},{2,10},{10,2},{3,11},{11,3},{4,12},{12,4},... | collective-permute-start | bytes 589832 | tf_op jit(solution)/shard_map/ppermute | solution.py:363
  190.0 10.4 %collective-permute-start.42 = (bf16[256,384]{1,0:T(8,128)(2,1)S(1)}, bf16[256,384]{1,0:T(8,128)(2,1)S(1)}, u32[]{:S(2)}, u32[]{:S(2)}) collective-permute-start(bf16[256,384]{1,0:T(8,128)(2,1)S(1)} %shard_map.126.refs_0_), channel_id=1, source_target_pairs={{0,6},{2,0},{4,2},{6,4},{1,7},{3,1},{5,3},{7,5},{8,14},{10,8},{12,... | collective-permute-start | bytes 589832 | tf_op jit(solution)/shard_map/ppermute | solution.py:368
  190.1 11.5 %collective-permute-start.43 = (bf16[256,384]{1,0:T(8,128)(2,1)S(1)}, bf16[256,384]{1,0:T(8,128)(2,1)S(1)}, u32[]{:S(2)}, u32[]{:S(2)}) collective-permute-start(bf16[256,384]{1,0:T(8,128)(2,1)S(1)} %shard_map.126.refs_0_), channel_id=1, source_target_pairs={{0,4},{2,6},{4,0},{6,2},{1,5},{3,7},{5,1},{7,3},{8,12},{10,14},{12... | collective-permute-start | bytes 589832 | tf_op jit(solution)/shard_map/ppermute | solution.py:368
  191.4 11.0 %collective-permute-start.44 = (bf16[256,384]{1,0:T(8,128)(2,1)S(1)}, bf16[256,384]{1,0:T(8,128)(2,1)S(1)}, u32[]{:S(2)}, u32[]{:S(2)}) collective-permute-start(bf16[256,384]{1,0:T(8,128)(2,1)S(1)} %shard_map.126.refs_0_), channel_id=1, source_target_pairs={{0,2},{2,4},{4,6},{6,0},{1,3},{3,5},{5,7},{7,1},{8,10},{10,12},{12... | collective-permute-start | bytes 589832 | tf_op jit(solution)/shard_map/ppermute | solution.py:368
  192.1 12.5 %collective-permute-start.45 = (bf16[256,384]{1,0:T(8,128)(2,1)S(1)}, bf16[256,384]{1,0:T(8,128)(2,1)S(1)}, u32[]{:S(2)}, u32[]{:S(2)}) collective-permute-start(bf16[256,384]{1,0:T(8,128)(2,1)S(1)} %shard_map.126.refs_0_), channel_id=1, source_target_pairs={{0,1},{1,0},{2,3},{3,2},{4,5},{5,4},{6,7},{7,6},{8,9},{9,8},{10,11... | collective-permute-start | bytes 589832 | tf_op jit(solution)/shard_map/ppermute | solution.py:363
  198.5 7.7 %collective-permute-start.34 = (bf16[256,384]{1,0:T(8,128)(2,1)S(1)}, bf16[256,384]{1,0:T(8,128)(2,1)S(1)}, u32[]{:S(2)}, u32[]{:S(2)}) collective-permute-start(bf16[256,384]{1,0:T(8,128)(2,1)S(1)} %shard_map.124.refs_0_), channel_id=1, source_target_pairs={{0,6},{2,0},{4,2},{6,4},{1,7},{3,1},{5,3},{7,5},{8,14},{10,8},{12,... | collective-permute-start | bytes 589832 | tf_op jit(solution)/shard_map/ppermute | solution.py:368
  200.4 10.1 %collective-permute-start.35 = (bf16[256,384]{1,0:T(8,128)(2,1)S(1)}, bf16[256,384]{1,0:T(8,128)(2,1)S(1)}, u32[]{:S(2)}, u32[]{:S(2)}) collective-permute-start(bf16[256,384]{1,0:T(8,128)(2,1)S(1)} %shard_map.124.refs_0_), channel_id=1, source_target_pairs={{0,4},{2,6},{4,0},{6,2},{1,5},{3,7},{5,1},{7,3},{8,12},{10,14},{12... | collective-permute-start | bytes 589832 | tf_op jit(solution)/shard_map/ppermute | solution.py:368
  201.6 11.3 %collective-permute-start.36 = (bf16[256,384]{1,0:T(8,128)(2,1)S(1)}, bf16[256,384]{1,0:T(8,128)(2,1)S(1)}, u32[]{:S(2)}, u32[]{:S(2)}) collective-permute-start(bf16[256,384]{1,0:T(8,128)(2,1)S(1)} %shard_map.124.refs_0_), channel_id=1, source_target_pairs={{0,2},{2,4},{4,6},{6,0},{1,3},{3,5},{5,7},{7,1},{8,10},{10,12},{12... | collective-permute-start | bytes 589832 | tf_op jit(solution)/shard_map/ppermute | solution.py:368
  202.4 11.0 %collective-permute-start.46 = (bf16[256,384]{1,0:T(8,128)(2,1)S(1)}, bf16[256,384]{1,0:T(8,128)(2,1)S(1)}, u32[]{:S(2)}, u32[]{:S(2)}) collective-permute-start(bf16[256,384]{1,0:T(8,128)(2,1)S(1)} %collective-permute-done.42.refs_1_), channel_id=1, source_target_pairs={{0,1},{1,0},{2,3},{3,2},{4,5},{5,4},{6,7},{7,6},{8,9},{9,8},{10,11... | collective-permute-start | bytes 589832 | tf_op jit(solution)/shard_map/ppermute | solution.py:363
  204.6 8.9 %collective-permute-start.47 = (bf16[256,384]{1,0:T(8,128)(2,1)S(1)}, bf16[256,384]{1,0:T(8,128)(2,1)S(1)}, u32[]{:S(2)}, u32[]{:S(2)}) collective-permute-start(bf16[256,384]{1,0:T(8,128)(2,1)S(1)} %collective-permute-done.43.refs_2_), channel_id=1, source_target_pairs={{0,1},{1,0},{2,3},{3,2},{4,5},{5,4},{6,7},{7,6},{8,9},{9,8},{10,11... | collective-permute-start | bytes 589832 | tf_op jit(solution)/shard_map/ppermute | solution.py:363
  206.2 9.6 %collective-permute-start.37 = (bf16[256,384]{1,0:T(8,128)(2,1)S(1)}, bf16[256,384]{1,0:T(8,128)(2,1)S(1)}, u32[]{:S(2)}, u32[]{:S(2)}) collective-permute-start(bf16[256,384]{1,0:T(8,128)(2,1)S(1)} %shard_map.124.refs_0_), channel_id=1, source_target_pairs={{0,1},{1,0},{2,3},{3,2},{4,5},{5,4},{6,7},{7,6},{8,9},{9,8},{10,11... | collective-permute-start | bytes 589832 | tf_op jit(solution)/shard_map/ppermute | solution.py:363
  210.5 3.5 %collective-permute-start.48 = (bf16[256,384]{1,0:T(8,128)(2,1)S(1)}, bf16[256,384]{1,0:T(8,128)(2,1)S(1)}, u32[]{:S(2)}, u32[]{:S(2)}) collective-permute-start(bf16[256,384]{1,0:T(8,128)(2,1)S(1)} %collective-permute-done.44.refs_3_), channel_id=1, source_target_pairs={{0,1},{1,0},{2,3},{3,2},{4,5},{5,4},{6,7},{7,6},{8,9},{9,8},{10,11... | collective-permute-start | bytes 589832 | tf_op jit(solution)/shard_map/ppermute | solution.py:363
  213.0 2.9 %collective-permute-start.38 = (bf16[256,384]{1,0:T(8,128)(2,1)S(1)}, bf16[256,384]{1,0:T(8,128)(2,1)S(1)}, u32[]{:S(2)}, u32[]{:S(2)}) collective-permute-start(bf16[256,384]{1,0:T(8,128)(2,1)S(1)} %collective-permute-done.34.refs_1_), channel_id=1, source_target_pairs={{0,1},{1,0},{2,3},{3,2},{4,5},{5,4},{6,7},{7,6},{8,9},{9,8},{10,11... | collective-permute-start | bytes 589832 | tf_op jit(solution)/shard_map/ppermute | solution.py:363
  213.5 2.4 %collective-permute-start.39 = (bf16[256,384]{1,0:T(8,128)(2,1)S(1)}, bf16[256,384]{1,0:T(8,128)(2,1)S(1)}, u32[]{:S(2)}, u32[]{:S(2)}) collective-permute-start(bf16[256,384]{1,0:T(8,128)(2,1)S(1)} %collective-permute-done.35.refs_2_), channel_id=1, source_target_pairs={{0,1},{1,0},{2,3},{3,2},{4,5},{5,4},{6,7},{7,6},{8,9},{9,8},{10,11... | collective-permute-start | bytes 589832 | tf_op jit(solution)/shard_map/ppermute | solution.py:363
  213.5 2.3 %collective-permute-start.40 = (bf16[256,384]{1,0:T(8,128)(2,1)S(1)}, bf16[256,384]{1,0:T(8,128)(2,1)S(1)}, u32[]{:S(2)}, u32[]{:S(2)}) collective-permute-start(bf16[256,384]{1,0:T(8,128)(2,1)S(1)} %collective-permute-done.36.refs_3_), channel_id=1, source_target_pairs={{0,1},{1,0},{2,3},{3,2},{4,5},{5,4},{6,7},{7,6},{8,9},{9,8},{10,11... | collective-permute-start | bytes 589832 | tf_op jit(solution)/shard_map/ppermute | solution.py:363
  (21 other events, 57.3 us)

commit v2 on v1

v2 whole, which is shorter than its diff:
```python
import jax
import jax.numpy as jnp
from jax import lax
from jax.experimental import pallas as pl
from jax.experimental.pallas import tpu as pltpu
from jax.sharding import Mesh, PartitionSpec as P

F32, BF16 = jnp.float32, jnp.bfloat16
EXP = ("z", "yl")
TEN = ("yh", "x", "c")
NN = (((1,), (0,)), ((), ()))
NT = (((1,), (1,)), ((), ()))
TN = (((0,), (0,)), ((), ()))


def mm(a, b, dims=NN):
    return lax.dot_general(a, b, dims, preferred_element_type=F32)


def call(kernel, out_shape, grid, in_specs, out_specs, scratch=(), mib=24):
    return pl.pallas_call(
        kernel,
        out_shape=out_shape,
        grid_spec=pltpu.PrefetchScalarGridSpec(
            num_scalar_prefetch=1,
            grid=grid,
            in_specs=in_specs,
            out_specs=out_specs,
            scratch_shapes=list(scratch),
        ),
        compiler_params=pltpu.CompilerParams(vmem_limit_bytes=mib * 2**20),
        cost_estimate=pl.CostEstimate(flops=1, transcendentals=0, bytes_accessed=1),
    )


def shape(*dims, dtype=BF16):
    return jax.ShapeDtypeStruct(dims, dtype)


def in_hbm(*values):
    return [pltpu.with_memory_space_constraint(v, pltpu.HBM) for v in values]


def block(dims, index=None):
    return pl.BlockSpec(
        dims, index or (lambda *_: (0,) * len(dims)), pipeline_mode=pl.Buffered(1)
    )


def chunk_index(s, j):
    core = s[0] if j < 4 else 1 - s[0]
    return core * 4 + lax.rem(s[1] + j % 4, 4)


def route(scal, ids, gates, cotangent, experts, cap):
    toks, features = cotangent.shape
    part, slots = features // 8, experts * cap

    def kernel(s, ids_ref, gates_ref, cot_ref, moved_ref, place_ref, hi_ref, lo_ref):
        named = jnp.transpose(ids_ref[...])
        named0, named1 = named[:, 0:1], named[:, 1:2]
        lane = lax.broadcasted_iota(jnp.int32, (toks, 128), 1)
        onehot = ((named0 == lane) | (named1 == lane)).astype(F32).astype(BF16)
        row = lax.broadcasted_iota(jnp.int32, (toks, toks), 0)
        col = lax.broadcasted_iota(jnp.int32, (toks, toks), 1)
        earlier = (col < row).astype(F32).astype(BF16)
        count = mm(earlier, onehot).astype(BF16)
        ex = lax.broadcasted_iota(jnp.int32, (128, slots), 0) * cap
        at = lax.broadcasted_iota(jnp.int32, (128, slots), 1)
        spread = ((at >= ex) & (at < ex + cap)).astype(F32).astype(BF16)
        rank = mm(count, spread)
        slot = lax.broadcasted_iota(jnp.int32, (toks, slots), 1)
        first, second = named0 * cap, named1 * cap
        in0 = (slot >= first) & (slot < first + cap)
        in1 = (slot >= second) & (slot < second + cap)
        base = jnp.where(in0, first, jnp.where(in1, second, -4 * slots))
        hit = rank.astype(jnp.int32) + base == slot
        g = jnp.transpose(gates_ref[...])
        weight = jnp.where(hit, jnp.where(in0, g[:, 0:1], g[:, 1:2]), 0.0)
        hi = weight.astype(BF16)
        lo = (weight - hi.astype(F32)).astype(BF16)
        place_ref[...] = hit.astype(F32).astype(BF16)
        hi_ref[...] = hi
        lo_ref[...] = lo
        cot = cot_ref[...]
        moved_ref[...] = (mm(hi, cot, TN) + mm(lo, cot, TN)).astype(BF16)

    return call(
        kernel,
        [pltpu.HBM((slots, part), BF16), pltpu.VMEM((toks, slots), BF16)]
        + [pltpu.HBM((toks, slots), BF16)] * 2,
        (1,),
        [
            block(ids.shape[::-1]),
            block(gates.shape[::-1]),
            block((toks, part), lambda k, s: (0, s[0] * 4 + s[1])),
        ],
        [block((slots, part))] + [block((toks, slots))] * 3,
    )(scal, *in_hbm(ids.T, gates.T, cotangent))


def place(scal, placing, tokens):
    toks, slots = placing.shape
    half = tokens.shape[1] // 2

    def kernel(s, place_ref, tok_ref, out_ref):
        out_ref[...] = mm(place_ref[...], tok_ref[...], TN).astype(BF16)

    return call(
        kernel,
        pltpu.HBM((slots, half), BF16),
        (3,),
        [
            block((toks, slots)),
            pl.BlockSpec((toks, half // 3), lambda k, s: (0, s[0] * 3 + k)),
        ],
        pl.BlockSpec((slots, half // 3), lambda k, s: (0, k)),
        mib=12,
    )(scal, placing, *in_hbm(tokens))


def gate_up(scal, t_half, wg, wu, sums):
    rows, half = t_half.shape
    ff = wg.shape[1]
    rb = rows // 3
    last = sums is not None

    def kernel(s, t_ref, wg_ref, wu_ref, *refs):
        left = t_ref[...]
        gate, up = mm(left, wg_ref[...]), mm(left, wu_ref[...])
        if not last:
            refs[0][...], refs[1][...] = gate, up
            return
        gate, up = gate + refs[0][...], up + refs[1][...]
        sig = jax.nn.sigmoid(gate)
        silu = gate * sig
        refs[2][...] = (silu * up).astype(BF16)
        refs[3][...] = silu
        refs[4][...] = up * sig * (1.0 + gate * (1.0 - sig))

    rows_of = pl.BlockSpec((rb, ff), lambda k, s: (k, 0))
    weights = block((half, ff), lambda k, s: ((1 - s[0]) if last else s[0], 0))
    wide = pltpu.VMEM((rows, ff), F32)
    return call(
        kernel,
        [pltpu.VMEM((rows, ff), BF16), wide, wide] if last else [wide, wide],
        (3,),
        [pl.BlockSpec((rb, half), lambda k, s: (k, 0)), weights, weights]
        + ([rows_of] * 2 if last else []),
        [rows_of] * (3 if last else 2),
        mib=20,
    )(scal, *in_hbm(t_half, wg, wu), *(sums or ()))


def back_hidden(scal, chunks, wd, sums):
    rows, cols = chunks[0].shape
    ff = wd.shape[0]
    rb = rows
    last = sums is not None

    def kernel(s, c0, c1, c2, c3, wd_ref, *refs):
        acc = refs[0][...] if last else None
        for j, ref in enumerate((c0, c1, c2, c3)):
            at = pl.multiple_of(lax.rem(s[1] + j, 4) * cols, 128)
            part = mm(ref[...], wd_ref[:, pl.ds(at, cols)], NT)
            acc = part if acc is None else acc + part
        if not last:
            refs[0][...] = acc
            return
        refs[3][:, :ff] = (acc * refs[2][...]).astype(BF16)
        refs[3][:, ff:] = (acc * refs[1][...]).astype(BF16)

    rows_of = block((rb, ff))
    return call(
        kernel,
        pltpu.VMEM((rows, 2 * ff), BF16) if last else pltpu.VMEM((rows, ff), F32),
        (1,),
        [block((rb, cols))] * 4
        + [block((ff, 4 * cols), lambda k, s: (0, (1 - s[0]) if last else s[0]))]
        + ([rows_of] * 3 if last else []),
        block((rb, 2 * ff)) if last else rows_of,
        mib=20,
    )(scal, *chunks, *in_hbm(wd), *(sums or ()))


def in_part(scal, steps, mine, theirs, wg, wu, wgu2):
    rows, ff = mine.shape[0], mine.shape[1] // 2
    cols = wgu2.shape[0] // 8

    def kernel(s, m, t, *refs):
        weights = [
            jnp.concatenate([refs[2 * k][...], refs[2 * k + 1][...]], axis=0) for k in range(4)
        ]
        acc = mm(m[:, :ff], weights[0], NT) + mm(m[:, ff:], weights[1], NT)
        acc += mm(t[:, :ff], weights[2], NT) + mm(t[:, ff:], weights[3], NT)
        for k in range(2):
            refs[8 + k][...] = acc[:, k * cols : (k + 1) * cols].astype(BF16)

    here = [block((cols, ff), lambda k, s, d=d: (s[0] * 4 + lax.rem(s[1] + d, 4), 0)) for d in steps]
    there = [
        block((cols, ff), lambda k, s, d=d, b=b: (b + lax.rem(s[1] + d, 4), 0))
        for b in (0, 4)
        for d in steps
    ]
    return call(
        kernel,
        [pltpu.HBM((rows, cols), BF16)] * 2,
        (1,),
        [block((rows, 2 * ff))] * 2 + here * 2 + there,
        [block((rows, cols))] * 2,
        mib=20,
    )(scal, mine, theirs, *in_hbm(wg, wg, wu, wu, *[wgu2] * 4))


def out_half(scal, hid, hid2, wd, wd2):
    rows, ff = hid.shape
    half = wd2.shape[1]
    cols = half // 2

    def kernel(s, h0, h1, w0, w1, out):
        out[...] = (mm(h0[...], w0[...]) + mm(h1[...], w1[...])).astype(BF16)

    return call(
        kernel,
        pltpu.HBM((rows, half), BF16),
        (2,),
        [
            block((rows, ff)),
            block((rows, ff)),
            pl.BlockSpec((ff, cols), lambda k, s: (0, s[0] * 2 + k)),
            pl.BlockSpec((ff, cols), lambda k, s: (0, k)),
        ],
        pl.BlockSpec((rows, cols), lambda k, s: (0, k)),
        mib=16,
    )(scal, hid, hid2, *in_hbm(wd, wd2))


def add(scal, *parts):
    rows, cols = parts[0].shape
    rb = rows // 4 if rows > 256 else rows

    def kernel(s, *refs):
        acc = refs[0][...].astype(F32)
        for ref in refs[1:-1]:
            acc = acc + ref[...].astype(F32)
        refs[-1][...] = acc.astype(BF16)

    rows_of = pl.BlockSpec((rb, cols), lambda k, s: (k, 0))
    return call(
        kernel,
        shape(rows, cols),
        (rows // rb,),
        [rows_of] * len(parts),
        rows_of,
        mib=8,
    )(scal, *parts)


def combine(scal, mats, home, quarters):
    toks, slots = mats[0].shape
    cols = home.shape[1]
    n = len(mats)

    def kernel(s, *refs):
        mat_refs, home_ref, rest = refs[:n], refs[n], refs[n + 1 :]
        acc = mm(mat_refs[0][...], home_ref[...])
        for m in mat_refs[1:]:
            acc += mm(m[...], home_ref[...])
        if quarters:
            whole = rest[-1]
            whole[...] = acc
            for d in range(4):
                at = pl.multiple_of(lax.rem(s[1] + d, 4) * (cols // 4), 128)
                rest[d][...] = whole[:, pl.ds(at, cols // 4)].astype(BF16)
        else:
            rest[0][...] = acc.astype(BF16)

    if quarters:
        dims, k, extra = (toks, cols // 4), 4, [pltpu.VMEM((toks, cols), F32)]
    else:
        dims, k, extra = (toks, cols), 1, []
    return call(
        kernel,
        [shape(*dims)] * k,
        (1,),
        [block((toks, slots))] * n + [block((slots, cols))],
        [block(dims)] * k,
        extra,
        mib=12,
    )(scal, *mats, home)


def grad_in(scal, own, oth, dgu):
    rows, half = own.shape
    ff = dgu.shape[1] // 2
    kb = half // 2

    def kernel(s, own_ref, oth_ref, dgu_ref, gg_ref, gu_ref):
        def put(left_ref):
            res = mm(left_ref[...], dgu_ref[...], TN).astype(BF16)
            gg_ref[...] = res[:, :ff]
            gu_ref[...] = res[:, ff:]

        k = pl.program_id(0)
        pl.when(k < 2)(lambda: put(own_ref))
        pl.when(k >= 2)(lambda: put(oth_ref))

    def place_of(k, s):
        return (jnp.where(k < 2, s[0], 1 - s[0]) * 2 + k % 2, 0)

    return call(
        kernel,
        [pltpu.HBM((2 * half, ff), BF16)] * 2,
        (4,),
        [
            pl.BlockSpec((rows, kb), lambda k, s: (0, jnp.minimum(k, 1))),
            pl.BlockSpec((rows, kb), lambda k, s: (0, jnp.maximum(k - 2, 0))),
            block(dgu.shape),
        ],
        [pl.BlockSpec((kb, ff), place_of)] * 2,
        mib=20,
    )(scal, *in_hbm(own, oth), dgu)


def grad_out(scal, hid, chunks):
    rows, cols = chunks[0].shape
    ff = hid.shape[1]

    def kernel(s, hid_ref, *refs):
        for j in range(8):
            at = pl.multiple_of(chunk_index(s, j) * cols, 128)
            refs[8][:, pl.ds(at, cols)] = mm(hid_ref[...], refs[j][...], TN).astype(BF16)

    return call(
        kernel,
        pltpu.HBM((ff, 8 * cols), BF16),
        (1,),
        [block((rows, ff))] + [block((rows, cols))] * 8,
        block((ff, 8 * cols)),
        mib=20,
    )(scal, hid, *chunks)


def assemble(scal, chunks):
    rows, cols = chunks[0].shape

    def kernel(s, *refs):
        for j in range(8):
            at = pl.multiple_of(chunk_index(s, j) * cols, 128)
            refs[8][:, pl.ds(at, cols)] = refs[j][...]

    return call(
        kernel,
        shape(rows, 8 * cols),
        (1,),
        [block((rows, cols))] * 8,
        block((rows, 8 * cols)),
        mib=8,
    )(scal, *chunks)


def swap(v, axis="c"):
    return lax.ppermute(v, axis, [(0, 1), (1, 0)])


def shift(v, axis, d):
    n = lax.axis_size(axis)
    return lax.ppermute(v, axis, [(i, (i + d) % n) for i in range(n)])


def all_exchange(rows):
    cut = rows.reshape(8, rows.shape[0] // 8, rows.shape[1])
    return lax.all_to_all(cut, EXP, split_axis=0, concat_axis=0, tiled=True).reshape(rows.shape)


def to_q(v, d, over_y):
    return swap(v, "yh") if d == 2 and over_y else shift(v, "x", d)


def gather_q(v, over_y):
    far, right, left = to_q(v, 2, over_y), to_q(v, 3, over_y), to_q(v, 1, over_y)
    return [v, right, far, left]


def after(value, *earlier):
    return lax.optimization_barrier((value, earlier))[0]


def finish(scal, mine):
    other = [(yh * 4 + x, (1 - yh) * 4 + (x + 2) % 4) for yh in range(2) for x in range(4)]
    total = add(scal, mine, lax.ppermute(mine, ("yh", "x"), other))
    chunks = gather_q(total, True)
    return assemble(scal, chunks + [swap(v) for v in chunks])


def on_device(tokens, cotangent, expert_ids, gates, w_gate, w_up, w_down):
    tok_rows, features = tokens.shape
    experts = lax.axis_size("z") * lax.axis_size("yl")
    cap = 3 * tok_rows // experts
    half = features // 2
    wg, wu, wd = w_gate[0], w_up[0], w_down[0]
    c = lax.axis_index("c")
    q = lax.rem(lax.axis_index("x") + 2 * lax.axis_index("yh"), 4)
    scal = jnp.stack([c, q]).astype(jnp.int32)

    d_mine, placing, w_hi, w_lo = route(scal, expert_ids, gates, cotangent, experts, cap)
    d_mine = all_exchange(d_mine)

    t_rows = place(scal, placing, tokens)
    wgu2 = jnp.concatenate(
        [lax.dynamic_slice_in_dim(w, (1 - c) * half, half, 0) for w in (wg, wu)], axis=0
    )
    wd2 = lax.dynamic_slice_in_dim(wd, (1 - c) * half, half, 1)
    d_mine, t_rows, wgu2, wd2 = lax.optimization_barrier((d_mine, t_rows, wgu2, wd2))

    t_own = all_exchange(t_rows)
    d_own = gather_q(d_mine, False)
    wgu2, wd2 = swap(wgu2), swap(wd2)
    t_own, d_own, wgu2, wd2 = lax.optimization_barrier((t_own, d_own, wgu2, wd2))
    t_oth = swap(t_own)
    d_oth = [swap(v) for v in d_own]

    sums = gate_up(scal, t_own, wg, wu, None)
    d_sum = back_hidden(scal, d_own, wd, None)
    hid, silu, dsilu = gate_up(scal, t_oth, wg, wu, sums)
    hid2 = swap(hid)
    dgu = back_hidden(scal, d_oth, wd, (d_sum, silu, dsilu))
    dgu2 = swap(dgu)

    out = out_half(scal, hid, hid2, wd, wd2)
    home = all_exchange(out)

    dgu, dgu2 = after((dgu, dgu2), out)
    parts, sent = {}, {}
    parts[2], parts[1] = in_part(scal, (2, 1), dgu, dgu2, wg, wu, wgu2)
    sent[2], sent[1] = to_q(parts[2], 2, False), to_q(parts[1], 1, False)
    dgu = after(dgu, parts[1])
    parts[3], parts[0] = in_part(scal, (3, 0), dgu, dgu2, wg, wu, wgu2)
    sent[3] = to_q(parts[3], 3, False)
    dgu, hid = after((dgu, hid), parts[0])
    grad_gate, grad_up = grad_in(scal, t_own, t_oth, dgu)
    hid, sent[2], sent[1] = after((hid, sent[2], sent[1]), grad_up)
    hid = after(hid, sent[2], sent[1])
    grad_down = grad_out(scal, hid, d_own + d_oth)
    sent, home, grad_gate, grad_up, grad_down = lax.optimization_barrier(
        (sent, home, grad_gate, grad_up, grad_down)
    )
    g_home = add(scal, parts[0], sent[2], sent[1], sent[3])
    quarters = combine(scal, [w_hi, w_lo], home, True)
    g_home = all_exchange(g_home)
    m_sent = [to_q(quarters[d], d, True) for d in (2, 1, 3)]
    g_mine = combine(scal, [placing], g_home, False)[0]
    m_sent = after(m_sent, g_mine)
    token_grad = finish(scal, g_mine)
    mixed = finish(scal, add(scal, quarters[0], *m_sent))
    return (mixed, token_grad, grad_gate[None], grad_up[None], grad_down[None])


def solution(mesh):
    fine = Mesh(mesh.devices.reshape(4, 2, 2, 4, 2), ("z", "yl", "yh", "x", "c"))
    placed = (
        P(EXP, None),
        P(EXP, None),
        P(EXP, None),
        P(EXP, None),
        P(EXP, None, TEN),
        P(EXP, None, TEN),
        P(EXP, TEN, None),
    )
    return jax.shard_map(
        on_device,
        mesh=fine,
        in_specs=placed,
        out_specs=(
            P(EXP, None),
            P(EXP, None),
            P(EXP, None, TEN),
            P(EXP, None, TEN),
            P(EXP, TEN, None),
        ),
        check_vma=False,
    )
```

time: 218 us -> 190 us (0.87)
  waiting for transfers between devices: 53.8 us -> 40.8 us
  starting transfers between devices: 72.6 us -> 64 us
  local copies, waits for them, and re-layouts: 12.2 us -> 7.68 us
  Pallas kernels: 78 us -> 73.7 us
    ppermute x15 -> x12, waiting for transfers between devices: 19.6 us -> 36.2 us  [shift(): return lax.ppermute(v, axis, [(i, (i + d) % n) for i in range(n)])]
    ppermute x7 -> x2, waiting for transfers between devices: 16.6 us -> 2.31 us  [finish(): total = add(scal, mine, lax.ppermute(mine, ('yh', 'x'), other))]
    all_to_all x3 -> x4, waiting for transfers between devices: 12.7 us -> 0.64 us  [all_exchange(): lax.all_to_all(cut, EXP, split_axis=0, concat_axis=0, tiled=True)]
    ppermute x27 -> x20, starting transfers between devices: 31.6 us -> 20.2 us  [swap(): return lax.ppermute(v, axis, [(0, 1), (1, 0)])]
    all_to_all x3 -> x4, starting transfers between devices: 16 us -> 22.3 us  [all_exchange(): lax.all_to_all(cut, EXP, split_axis=0, concat_axis=0, tiled=True)]
    ppermute x7 -> x2, starting transfers between devices: 9.28 us -> 4.77 us  [finish(): total = add(scal, mine, lax.ppermute(mine, ('yh', 'x'), other))]
    ppermute x27 -> x20, waiting for transfers between devices: 4.92 us -> 1.61 us  [swap(): return lax.ppermute(v, axis, [(0, 1), (1, 0)])]
    pallas_call x1, Pallas kernels: 8.03 us -> 5.66 us  [grad_out(): call(kernel, pltpu.HBM((ff, 8 * cols), BF16), (1,), [block((rows, ff))] +...]
  transfers between devices with their start and end apart: 52 -> 38, of which waited for: 13 -> 10; matrix products, arithmetic and copies ran while one was open for 3% -> 3% of each run, Pallas kernels for 31% -> 31%
where the time goes in v2:
time: 190 us; the launch traced here: 189 us
  Pallas kernels  73.7 us (39%)
  starting transfers between devices  64 us (34%)
  waiting for transfers between devices  40.8 us (21%)
  local copies, waits for them, and re-layouts  7.68 us (4%)
  other arithmetic  1.94 us (1%)
    ppermute x12, waiting for transfers between devices, shift(): return lax.ppermute(v, axis, [(i, (i + d) % n) for i in range(n)])  36.2 us
    all_to_all x4, starting transfers between devices, all_exchange(): lax.all_to_all(cut, EXP, split_axis=0, concat_axis=0, tiled=True)  22.3 us
    ppermute x20, starting transfers between devices, swap(): return lax.ppermute(v, axis, [(0, 1), (1, 0)])  20.2 us
    ppermute x12, starting transfers between devices, shift(): return lax.ppermute(v, axis, [(i, (i + d) % n) for i in range(n)])  16.6 us
    pallas_call x2, Pallas kernels, in_part(): call(kernel, [pltpu.HBM((rows, cols), BF16)] * 2, (1,), [block((rows, 2 *...  12.1 us
    pallas_call x2, Pallas kernels, gate_up(): call(kernel, [pltpu.VMEM((rows, ff), BF16), wide, wide] if last else [wid...  12 us
    pallas_call x1, Pallas kernels, grad_in(): call(kernel, [pltpu.HBM((2 * half, ff), BF16)] * 2, (4,), [pl.BlockSpec((...  9.82 us
    pallas_call x2, Pallas kernels, back_hidden(): call(kernel, pltpu.VMEM((rows, 2 * ff), BF16) if last else pltpu.VMEM((ro...  7.55 us
  transfers between devices with their start and end apart: 38, of which 10 were waited for; matrix products, arithmetic and copies ran while one was open for 3% of the time, Pallas kernels for 31%

profile of v2, /device:TPU:1, one launch (start us, length us, event | category | flops | bytes accessed | tf_op | source)
XLA Modules:
  0.0 189.2 jit_solution(1541374340768270061)
XLA Ops:
  0.7 4.2 %shard_map.110 = (bf16[768,384]{1,0:T(8,128)(2,1)}, bf16[256,768]{1,0:T(8,128)(2,1)S(1)}, bf16[256,768]{1,0:T(8,128)(2,1)}, bf16[256,768]{1,0:T(8,128)(2,1)}) custom-call(s32[2]{0:T(128)S(1)} %pad_add_fusion.s, s32[2,256]{1,0:T(2,128)} %bitcast.49, f32[2,256]{1,0:T(2,128)} %bitcast.50, bf16[256,3072]{1,0:T(8,128)(2,1)} %cot_ref.1), custom_call_target="tpu_custom_call" | custom-call | flops 1 | bytes 1 | tf_op jit(solution)/shard_map/pallas_call | solution.py:88
  4.9 6.9 %all-to-all-start = ((bf16[8,96,384]{2,1,0:T(8,128)(2,1)}), bf16[8,96,384]{2,1,0:T(8,128)(2,1)S(1)}, u32[]{:S(2)}, u32[]{:S(2)}) async-start(bf16[8,96,384]{2,1,0:T(8,128)(2,1)} %bitcast.48), calls=%async_computation | async-start | bytes 1179648 | tf_op jit(solution)/shard_map/all_to_all | solution.py:373
  11.8 2.2 %dynamic-slice_bitcast_fusion.1 = (bf16[1536,512]{1,0:T(8,128)(2,1)S(1)}, bf16[1536,512]{1,0:T(8,128)(2,1)S(1)}) fusion(bf16[1,3072,512]{2,1,0:T(8,128)(2,1)} %param.12, s32[]{:T(128)S(6)} %select_n.2, bf16[1,3072,512]{2,1,0:T(8,128)(2,1)} %param.11), kind=kLoop, calls=%fused_computation.2 | loop fusion | bytes 6291460 | tf_op jit(solution)/shard_map/dynamic_slice | solution.py:411
  14.0 0.6 copy-done.25
  14.6 1.2 dynamic-slice_bitcast_fusion
  15.8 4.3 %shard_map.111 = bf16[768,1536]{1,0:T(8,128)(2,1)} custom-call(s32[2]{0:T(128)S(1)} %pad_add_fusion.s, bf16[256,768]{1,0:T(8,128)(2,1)S(1)} %get-tuple-element.57.place_ref.refs_0_, bf16[256,3072]{1,0:T(8,128)(2,1)} %tok_ref.1), custom_call_target="tpu_custom_call" | custom-call | flops 1 | bytes 1 | tf_op jit(solution)/shard_map/pallas_call | solution.py:109
  20.2 1.9 pad_maximum_fusion
  22.0 1.5 collective-permute-start.3
  23.5 4.9 %all-to-all-start.1 = ((bf16[8,96,1536]{2,1,0:T(8,128)(2,1)}), bf16[8,96,1536]{2,1,0:T(8,128)(2,1)}, u32[]{:S(2)}, u32[]{:S(2)}) async-start(bf16[8,96,1536]{2,1,0:T(8,128)(2,1)} %bitcast.9), calls=%async_computation.1 | async-start | bytes 4718592 | tf_op jit(solution)/shard_map/all_to_all | solution.py:373
  28.4 0.3 collective-permute-start.4
  28.7 1.2 collective-permute-start.2
  29.9 2.5 %collective-permute-start.1 = (bf16[768,384]{1,0:T(8,128)(2,1)S(1)}, bf16[768,384]{1,0:T(8,128)(2,1)S(1)}, u32[]{:S(2)}, u32[]{:S(2)}) collective-permute-start(bf16[768,384]{1,0:T(8,128)(2,1)S(1)} %bitcast.25), channel_id=1, source_target_pairs={{0,4},{2,6},{4,0},{6,2},{1,5},{3,7},{5,1},{7,3},{8,12},{10,14},{12... | collective-permute-start | bytes 1769480 | tf_op jit(solution)/shard_map/ppermute | solution.py:368
  32.4 1.1 collective-permute-start
  33.5 11.2 %collective-permute-done.2.c3.refs_3_ = bf16[768,384]{1,0:T(8,128)(2,1)S(1)} collective-permute-done((bf16[768,384]{1,0:T(8,128)(2,1)S(1)}, bf16[768,384]{1,0:T(8,128)(2,1)S(1)}, u32[]{:S(2)}, u32[]{:S(2)}) %collective-permute-start.2) | collective-permute-done | bytes 589856 | tf_op jit(solution)/shard_map/ppermute | solution.py:368
  44.8 13.6 %collective-permute-done.1.c2.refs_2_ = bf16[768,384]{1,0:T(8,128)(2,1)S(1)} collective-permute-done((bf16[768,384]{1,0:T(8,128)(2,1)S(1)}, bf16[768,384]{1,0:T(8,128)(2,1)S(1)}, u32[]{:S(2)}, u32[]{:S(2)}) %collective-permute-start.1) | collective-permute-done | bytes 589856 | tf_op jit(solution)/shard_map/ppermute | solution.py:368
  58.4 1.0 collective-permute-start.9
  59.4 5.8 %shard_map.113 = (f32[768,512]{1,0:T(8,128)S(1)}, f32[768,512]{1,0:T(8,128)S(1)}) custom-call(s32[2]{0:T(128)S(1)} %pad_add_fusion.s, bf16[768,1536]{1,0:T(8,128)(2,1)} %bitcast.10.t_ref.own_ref, bf16[3072,512]{1,0:T(8,128)(2,1)} %bitcast.31, bf16[3072,512]{1,0:T(8,128)(2,1)} %bitcast.37), custom_call_target="tpu_custom_call" | custom-call | flops 1 | bytes 1 | tf_op jit(solution)/shard_map/pallas_call | solution.py:144
  65.2 1.4 copy-done.26
  66.6 6.2 %shard_map.114 = (bf16[768,512]{1,0:T(8,128)(2,1)S(1)}, f32[768,512]{1,0:T(8,128)S(1)}, f32[768,512]{1,0:T(8,128)S(1)}) custom-call(s32[2]{0:T(128)S(1)} %pad_add_fusion.s, bf16[768,1536]{1,0:T(8,128)(2,1)} %copy-done.26, bf16[3072,512]{1,0:T(8,128)(2,1)} %bitcast.32, bf16[3072,512]{1,0:T(8,128)(2,1)} %bitcast.38, f32[768,512]{1,0:T(8,128)S(1)} %get-tuple-element.67.refs_0_, ...), custom_call_target="tpu_custom_call" | custom-call | flops 1 | bytes 1 | tf_op jit(solution)/shard_map/pallas_call | solution.py:144
  72.9 0.5 collective-permute-start.5
  73.5 0.4 collective-permute-start.7
  74.0 3.8 %shard_map.112.refs_0_ = f32[768,512]{1,0:T(8,128)S(1)} custom-call(s32[2]{0:T(128)S(1)} %pad_add_fusion.s, bf16[768,384]{1,0:T(8,128)(2,1)S(1)} %bitcast.28, bf16[768,384]{1,0:T(8,128)(2,1)S(1)} %collective-permute-done.c1.refs_1_, bf16[768,384]{1,0:T(8,128)(2,1)S(1)} %collective-permute-done.1.c2.refs_2_, ...), custom_call_target="tpu_custom_call" | custom-call | flops 1 | bytes 1 | tf_op jit(solution)/shard_map/pallas_call | solution.py:174
  77.8 0.7 collective-permute-done.8.c3.refs_7_
  78.5 3.8 %shard_map.115.m.dgu_ref = bf16[768,1024]{1,0:T(8,128)(2,1)S(1)} custom-call(s32[2]{0:T(128)S(1)} %pad_add_fusion.s, bf16[768,384]{1,0:T(8,128)(2,1)S(1)} %collective-permute-done.5.c0.refs_4_, bf16[768,384]{1,0:T(8,128)(2,1)S(1)} %collective-permute-done.6.c1.refs_5_, bf16[768,384]{1,0:T(8,128)(2,1)S(1)} %collective-permute-done.7.c2.refs_6_, ...), custom_call_target="tpu_custom_call" | custom-call | flops 1 | bytes 1 | tf_op jit(solution)/shard_map/pallas_call | solution.py:174
  82.4 0.2 collective-permute-start.10
  82.6 5.9 %shard_map.116 = bf16[768,1536]{1,0:T(8,128)(2,1)} custom-call(s32[2]{0:T(128)S(1)} %pad_add_fusion.s, bf16[768,512]{1,0:T(8,128)(2,1)S(1)} %get-tuple-element.88.h0.hid_ref, bf16[768,512]{1,0:T(8,128)(2,1)S(1)} %collective-permute-done.11.h1, bf16[512,3072]{1,0:T(8,128)(2,1)} %bitcast.45, bf16[512,1536]{1,0:T(8,128)(2,1)} %collective-permute-done.4.w1), custom_call_target="tpu_custom_call" | custom-call | flops 1 | bytes 1 | tf_op jit(solution)/shard_map/pallas_call | solution.py:223
  88.5 5.4 %all-to-all-start.2 = ((bf16[8,96,1536]{2,1,0:T(8,128)(2,1)}), bf16[8,96,1536]{2,1,0:T(8,128)(2,1)}, u32[]{:S(2)}, u32[]{:S(2)}) async-start(bf16[8,96,1536]{2,1,0:T(8,128)(2,1)} %bitcast.46), calls=%async_computation.2 | async-start | bytes 4718592 | tf_op jit(solution)/shard_map/all_to_all | solution.py:373
  93.9 6.1 %shard_map.117 = (bf16[768,384]{1,0:T(8,128)(2,1)}, bf16[768,384]{1,0:T(8,128)(2,1)}) custom-call(s32[2]{0:T(128)S(1)} %pad_add_fusion.s, bf16[768,1024]{1,0:T(8,128)(2,1)S(1)} %shard_map.115.m.dgu_ref, bf16[768,1024]{1,0:T(8,128)(2,1)S(1)} %collective-permute-done.10.t, bf16[3072,512]{1,0:T(8,128)(2,1)} %bitcast.33, bf16[3072,512]{1,0:T(8,128)(2,1)} %bitcast.34, ...), custom_call_target="tpu_custom_call" | custom-call | flops 1 | bytes 1 | tf_op jit(solution)/shard_map/pallas_call | solution.py:205
  100.0 2.4 %collective-permute-start.12 = (bf16[768,384]{1,0:T(8,128)(2,1)}, bf16[768,384]{1,0:T(8,128)(2,1)S(1)}, u32[]{:S(2)}, u32[]{:S(2)}) collective-permute-start(bf16[768,384]{1,0:T(8,128)(2,1)} %get-tuple-element.80), channel_id=1, source_target_pairs={{0,4},{2,6},{4,0},{6,2},{1,5},{3,7},{5,1},{7,3},{8,12},{10,14},{12... | collective-permute-start | bytes 1769480 | tf_op jit(solution)/shard_map/ppermute | solution.py:368
  102.5 6.0 %shard_map.118 = (bf16[768,384]{1,0:T(8,128)(2,1)}, bf16[768,384]{1,0:T(8,128)(2,1)}) custom-call(s32[2]{0:T(128)S(1)} %pad_add_fusion.s, bf16[768,1024]{1,0:T(8,128)(2,1)S(1)} %shard_map.115.m.dgu_ref, bf16[768,1024]{1,0:T(8,128)(2,1)S(1)} %collective-permute-done.10.t, bf16[3072,512]{1,0:T(8,128)(2,1)} %bitcast.35, bf16[3072,512]{1,0:T(8,128)(2,1)} %bitcast.36, ...), custom_call_target="tpu_custom_call" | custom-call | flops 1 | bytes 1 | tf_op jit(solution)/shard_map/pallas_call | solution.py:205
  108.5 2.5 %collective-permute-start.14 = (bf16[768,384]{1,0:T(8,128)(2,1)}, bf16[768,384]{1,0:T(8,128)(2,1)S(1)}, u32[]{:S(2)}, u32[]{:S(2)}) collective-permute-start(bf16[768,384]{1,0:T(8,128)(2,1)} %get-tuple-element.85), channel_id=1, source_target_pairs={{0,6},{2,0},{4,2},{6,4},{1,7},{3,1},{5,3},{7,5},{8,14},{10,8},{12,... | collective-permute-start | bytes 1769480 | tf_op jit(solution)/shard_map/ppermute | solution.py:368
  111.1 9.8 %shard_map.119 = (bf16[3072,512]{1,0:T(8,128)(2,1)}, bf16[3072,512]{1,0:T(8,128)(2,1)}) custom-call(s32[2]{0:T(128)S(1)} %pad_add_fusion.s, bf16[768,1536]{1,0:T(8,128)(2,1)} %bitcast.10.t_ref.own_ref, bf16[768,1536]{1,0:T(8,128)(2,1)} %copy-done.26, bf16[768,1024]{1,0:T(8,128)(2,1)S(1)} %shard_map.115.m.dgu_ref), custom_call_target="tpu_custom_call" | custom-call | flops 1 | bytes 1 | tf_op jit(solution)/shard_map/pallas_call | solution.py:311
  120.9 8.6 %collective-permute-done.13.refs_2_ = bf16[768,384]{1,0:T(8,128)(2,1)S(1)} collective-permute-done((bf16[768,384]{1,0:T(8,128)(2,1)}, bf16[768,384]{1,0:T(8,128)(2,1)S(1)}, u32[]{:S(2)}, u32[]{:S(2)}) %collective-permute-start.13) | collective-permute-done | bytes 589856 | tf_op jit(solution)/shard_map/ppermute | solution.py:368
  129.7 5.7 %shard_map.120 = bf16[512,3072]{1,0:T(8,128)(2,1)} custom-call(s32[2]{0:T(128)S(1)} %pad_add_fusion.s, bf16[768,512]{1,0:T(8,128)(2,1)S(1)} %copy-done.3, bf16[768,384]{1,0:T(8,128)(2,1)S(1)} %bitcast.29, bf16[768,384]{1,0:T(8,128)(2,1)S(1)} %copy-done.9, bf16[768,384]{1,0:T(8,128)(2,1)S(1)} %copy-done.7, bf16[768,384]{1,0:T(8,128)(2,1)S(1)} %copy-done.5, ...), custom_call_target="tpu_custom_call" | custom-call | flops 1 | bytes 1 | tf_op jit(solution)/shard_map/pallas_call | solution.py:334
  135.4 1.1 copy-done.19
  136.4 1.1 copy-done.21
  137.5 2.1 %shard_map.122 = bf16[768,384]{1,0:T(8,128)(2,1)} custom-call(s32[2]{0:T(128)S(1)} %pad_add_fusion.s, bf16[768,384]{1,0:T(8,128)(2,1)S(1)} %copy-done.22, bf16[768,384]{1,0:T(8,128)(2,1)S(1)} %copy-done.19, bf16[768,384]{1,0:T(8,128)(2,1)S(1)} %copy-done.21, bf16[768,384]{1,0:T(8,128)(2,1)S(1)} %collective-permute-done.14.refs_3_), custom_call_target="tpu_custom_call" | custom-call | flops 1 | bytes 1 | tf_op jit(solution)/shard_map/pallas_call | solution.py:249
  139.6 5.1 %all-to-all-start.3 = ((bf16[8,96,384]{2,1,0:T(8,128)(2,1)}), bf16[8,96,384]{2,1,0:T(8,128)(2,1)S(1)}, u32[]{:S(2)}, u32[]{:S(2)}) async-start(bf16[8,96,384]{2,1,0:T(8,128)(2,1)} %bitcast.16), calls=%async_computation.3 | async-start | bytes 1179648 | tf_op jit(solution)/shard_map/all_to_all | solution.py:373
  144.8 3.8 %shard_map.121 = (bf16[256,384]{1,0:T(8,128)(2,1)S(1)}, bf16[256,384]{1,0:T(8,128)(2,1)S(1)}, bf16[256,384]{1,0:T(8,128)(2,1)S(1)}, bf16[256,384]{1,0:T(8,128)(2,1)S(1)}) custom-call(s32[2]{0:T(128)S(1)} %pad_add_fusion.s, bf16[256,768]{1,0:T(8,128)(2,1)S(1)} %copy-done.23, bf16[256,768]{1,0:T(8,128)(2,1)S(1)} %copy-done.24, bf16[768,1536]{1,0:T(8,128)(2,1)} %bitcast.15.refs_2_), custom_call_target="tpu_custom_call" | custom-call | flops 1 | bytes 1 | tf_op jit(solution)/shard_map/pallas_call | solution.py:282
  148.6 2.7 %collective-permute-start.15 = (bf16[256,384]{1,0:T(8,128)(2,1)S(1)}, bf16[256,384]{1,0:T(8,128)(2,1)S(1)}, u32[]{:S(2)}, u32[]{:S(2)}) collective-permute-start(bf16[256,384]{1,0:T(8,128)(2,1)S(1)} %get-tuple-element.91), channel_id=1, source_target_pairs={{0,8},{8,0},{1,9},{9,1},{2,10},{10,2},{3,11},{11,3},{4,12},{12,4},... | collective-permute-start | bytes 589832 | tf_op jit(solution)/shard_map/ppermute | solution.py:363
  151.2 2.7 %collective-permute-start.17 = (bf16[256,384]{1,0:T(8,128)(2,1)S(1)}, bf16[256,384]{1,0:T(8,128)(2,1)S(1)}, u32[]{:S(2)}, u32[]{:S(2)}) collective-permute-start(bf16[256,384]{1,0:T(8,128)(2,1)S(1)} %get-tuple-element.93), channel_id=1, source_target_pairs={{0,6},{2,0},{4,2},{6,4},{1,7},{3,1},{5,3},{7,5},{8,14},{10,8},{12,... | collective-permute-start | bytes 589832 | tf_op jit(solution)/shard_map/ppermute | solution.py:368
  153.9 0.6 all-to-all-done.3
  154.5 0.9 shard_map.123.refs_0_
  155.5 2.2 %collective-permute-start.26 = (bf16[256,384]{1,0:T(8,128)(2,1)S(1)}, bf16[256,384]{1,0:T(8,128)(2,1)S(1)}, u32[]{:S(2)}, u32[]{:S(2)}) collective-permute-start(bf16[256,384]{1,0:T(8,128)(2,1)S(1)} %shard_map.123.refs_0_), channel_id=1, source_target_pairs={{0,12},{2,14},{4,8},{6,10},{8,4},{10,6},{12,0},{14,2},{1,13},{3,15... | collective-permute-start | bytes 589832 | tf_op jit(solution)/shard_map/ppermute | solution.py:391
  157.6 0.8 collective-permute-done.15.refs_1_
  158.4 0.6 shard_map.124.refs_0_
  159.1 2.6 %collective-permute-start.18 = (bf16[256,384]{1,0:T(8,128)(2,1)S(1)}, bf16[256,384]{1,0:T(8,128)(2,1)S(1)}, u32[]{:S(2)}, u32[]{:S(2)}) collective-permute-start(bf16[256,384]{1,0:T(8,128)(2,1)S(1)} %shard_map.124.refs_0_), channel_id=1, source_target_pairs={{0,12},{2,14},{4,8},{6,10},{8,4},{10,6},{12,0},{14,2},{1,13},{3,15... | collective-permute-start | bytes 589832 | tf_op jit(solution)/shard_map/ppermute | solution.py:391
  161.6 2.3 %collective-permute-done.26.refs_1_ = bf16[256,384]{1,0:T(8,128)(2,1)S(1)} collective-permute-done((bf16[256,384]{1,0:T(8,128)(2,1)S(1)}, bf16[256,384]{1,0:T(8,128)(2,1)S(1)}, u32[]{:S(2)}, u32[]{:S(2)}) %collective-permute-start.26) | collective-permute-done | bytes 196640 | tf_op jit(solution)/shard_map/ppermute | solution.py:391
  164.0 0.6 shard_map.127.refs_0_
  164.6 5.3 %collective-permute-start.30 = (bf16[256,384]{1,0:T(8,128)(2,1)S(1)}, bf16[256,384]{1,0:T(8,128)(2,1)S(1)}, u32[]{:S(2)}, u32[]{:S(2)}) collective-permute-start(bf16[256,384]{1,0:T(8,128)(2,1)S(1)} %shard_map.127.refs_0_), channel_id=1, source_target_pairs={{0,1},{1,0},{2,3},{3,2},{4,5},{5,4},{6,7},{7,6},{8,9},{9,8},{10,11... | collective-permute-start | bytes 589832 | tf_op jit(solution)/shard_map/ppermute | solution.py:363
  169.9 2.3 %collective-permute-start.28 = (bf16[256,384]{1,0:T(8,128)(2,1)S(1)}, bf16[256,384]{1,0:T(8,128)(2,1)S(1)}, u32[]{:S(2)}, u32[]{:S(2)}) collective-permute-start(bf16[256,384]{1,0:T(8,128)(2,1)S(1)} %shard_map.127.refs_0_), channel_id=1, source_target_pairs={{0,8},{8,0},{1,9},{9,1},{2,10},{10,2},{3,11},{11,3},{4,12},{12,4},... | collective-permute-start | bytes 589832 | tf_op jit(solution)/shard_map/ppermute | solution.py:363
  172.1 2.7 %collective-permute-start.27 = (bf16[256,384]{1,0:T(8,128)(2,1)S(1)}, bf16[256,384]{1,0:T(8,128)(2,1)S(1)}, u32[]{:S(2)}, u32[]{:S(2)}) collective-permute-start(bf16[256,384]{1,0:T(8,128)(2,1)S(1)} %shard_map.127.refs_0_), channel_id=1, source_target_pairs={{0,6},{2,0},{4,2},{6,4},{1,7},{3,1},{5,3},{7,5},{8,14},{10,8},{12,... | collective-permute-start | bytes 589832 | tf_op jit(solution)/shard_map/ppermute | solution.py:368
  174.8 0.6 shard_map.125.refs_0_
  175.5 0.8 collective-permute-start.20
  176.3 1.2 collective-permute-done.29.refs_3_
  177.6 1.3 collective-permute-start.19
  178.9 1.7 collective-permute-start.33
  180.7 1.5 collective-permute-done.21.refs_3_
  182.2 1.8 collective-permute-start.22
  184.0 0.4 collective-permute-start.31
  184.4 0.4 collective-permute-start.25
  185.0 0.4 collective-permute-start.23
  185.5 1.8 shard_map.128
  187.4 1.8 shard_map.126
  (89 shorter events, 1.0 us)
Async XLA Ops:
  4.9 17.1 %all-to-all-start = ((bf16[8,96,384]{2,1,0:T(8,128)(2,1)}), bf16[8,96,384]{2,1,0:T(8,128)(2,1)S(1)}, u32[]{:S(2)}, u32[]{:S(2)}) async-start(bf16[8,96,384]{2,1,0:T(8,128)(2,1)} %bitcast.48), calls=%async_computation | async-start | bytes 1179648 | tf_op jit(solution)/shard_map/all_to_all | solution.py:373
  11.8 2.8 %copy-start.25 = (bf16[1,512,3072]{2,1,0:T(8,128)(2,1)S(1)}, bf16[1,512,3072]{2,1,0:T(8,128)(2,1)}, u32[]{:S(2)}) copy-start(bf16[1,512,3072]{2,1,0:T(8,128)(2,1)} %param.13) | copy-start | bytes 9437188
  22.0 52.0 %copy-start = (bf16[8,96,384]{2,1,0:T(8,128)(2,1)}, bf16[8,96,384]{2,1,0:T(8,128)(2,1)S(1)}, u32[]{:S(2)}) copy-start(bf16[8,96,384]{2,1,0:T(8,128)(2,1)S(1)} %all-to-all-done) | copy-start | bytes 1769476
  22.0 36.4 %collective-permute-start.3 = (bf16[3072,512]{1,0:T(8,128)(2,1)}, bf16[3072,512]{1,0:T(8,128)(2,1)}, u32[]{:S(2)}, u32[]{:S(2)}) collective-permute-start(bf16[3072,512]{1,0:T(8,128)(2,1)} %pad_maximum_fusion), channel_id=1, source_target_pairs={{0,1},{1,0},{2,3},{3,2},{4,5},{5,4},{6,7},{7,6},{8,9},{9,8},{10,11... | collective-permute-start | bytes 9437192 | tf_op jit(solution)/shard_map/ppermute | solution.py:363
  23.5 34.9 %all-to-all-start.1 = ((bf16[8,96,1536]{2,1,0:T(8,128)(2,1)}), bf16[8,96,1536]{2,1,0:T(8,128)(2,1)}, u32[]{:S(2)}, u32[]{:S(2)}) async-start(bf16[8,96,1536]{2,1,0:T(8,128)(2,1)} %bitcast.9), calls=%async_computation.1 | async-start | bytes 4718592 | tf_op jit(solution)/shard_map/all_to_all | solution.py:373
  28.4 30.0 %collective-permute-start.4 = (bf16[512,1536]{1,0:T(8,128)(2,1)}, bf16[512,1536]{1,0:T(8,128)(2,1)}, u32[]{:S(2)}, u32[]{:S(2)}) collective-permute-start(bf16[512,1536]{1,0:T(8,128)(2,1)} %dynamic-slice_bitcast_fusion), channel_id=1, source_target_pairs={{0,1},{1,0},{2,3},{3,2},{4,5},{5,4},{6,7},{7,6},{8,9},{9,8},{10,11... | collective-permute-start | bytes 4718600 | tf_op jit(solution)/shard_map/ppermute | solution.py:363
  28.7 16.0 %collective-permute-start.2 = (bf16[768,384]{1,0:T(8,128)(2,1)S(1)}, bf16[768,384]{1,0:T(8,128)(2,1)S(1)}, u32[]{:S(2)}, u32[]{:S(2)}) collective-permute-start(bf16[768,384]{1,0:T(8,128)(2,1)S(1)} %bitcast.24), channel_id=1, source_target_pairs={{0,2},{2,4},{4,6},{6,0},{1,3},{3,5},{5,7},{7,1},{8,10},{10,12},{12... | collective-permute-start | bytes 1769480 | tf_op jit(solution)/shard_map/ppermute | solution.py:368
  29.9 28.5 %collective-permute-start.1 = (bf16[768,384]{1,0:T(8,128)(2,1)S(1)}, bf16[768,384]{1,0:T(8,128)(2,1)S(1)}, u32[]{:S(2)}, u32[]{:S(2)}) collective-permute-start(bf16[768,384]{1,0:T(8,128)(2,1)S(1)} %bitcast.25), channel_id=1, source_target_pairs={{0,4},{2,6},{4,0},{6,2},{1,5},{3,7},{5,1},{7,3},{8,12},{10,14},{12... | collective-permute-start | bytes 1769480 | tf_op jit(solution)/shard_map/ppermute | solution.py:368
  32.4 26.0 %collective-permute-start = (bf16[768,384]{1,0:T(8,128)(2,1)S(1)}, bf16[768,384]{1,0:T(8,128)(2,1)S(1)}, u32[]{:S(2)}, u32[]{:S(2)}) collective-permute-start(bf16[768,384]{1,0:T(8,128)(2,1)S(1)} %bitcast.26), channel_id=1, source_target_pairs={{0,6},{2,0},{4,2},{6,4},{1,7},{3,1},{5,3},{7,5},{8,14},{10,8},{12,... | collective-permute-start | bytes 1769480 | tf_op jit(solution)/shard_map/ppermute | solution.py:368
  44.7 29.3 %copy-start.4 = (bf16[768,384]{1,0:T(8,128)(2,1)}, bf16[768,384]{1,0:T(8,128)(2,1)S(1)}, u32[]{:S(2)}) copy-start(bf16[768,384]{1,0:T(8,128)(2,1)S(1)} %collective-permute-done.2.c3.refs_3_) | copy-start | bytes 1769476
  58.4 15.6 %copy-start.6 = (bf16[768,384]{1,0:T(8,128)(2,1)}, bf16[768,384]{1,0:T(8,128)(2,1)S(1)}, u32[]{:S(2)}) copy-start(bf16[768,384]{1,0:T(8,128)(2,1)S(1)} %collective-permute-done.1.c2.refs_2_) | copy-start | bytes 1769476
  58.4 15.6 %copy-start.8 = (bf16[768,384]{1,0:T(8,128)(2,1)}, bf16[768,384]{1,0:T(8,128)(2,1)S(1)}, u32[]{:S(2)}) copy-start(bf16[768,384]{1,0:T(8,128)(2,1)S(1)} %collective-permute-done.c1.refs_1_) | copy-start | bytes 1769476
  58.4 6.8 %collective-permute-start.9 = (bf16[768,1536]{1,0:T(8,128)(2,1)}, bf16[768,1536]{1,0:T(8,128)(2,1)S(1)}, u32[]{:S(2)}, u32[]{:S(2)}) collective-permute-start(bf16[768,1536]{1,0:T(8,128)(2,1)} %bitcast.10.t_ref.own_ref), channel_id=1, source_target_pairs={{0,1},{1,0},{2,3},{3,2},{4,5},{5,4},{6,7},{7,6},{8,9},{9,8},{10,11... | collective-permute-start | bytes 7077896 | tf_op jit(solution)/shard_map/ppermute | solution.py:363
  65.2 1.4 copy-start.26
  72.8 9.8 %copy-start.2 = (bf16[768,512]{1,0:T(8,128)(2,1)}, bf16[768,512]{1,0:T(8,128)(2,1)S(1)}, u32[]{:S(2)}) copy-start(bf16[768,512]{1,0:T(8,128)(2,1)S(1)} %get-tuple-element.88.h0.hid_ref) | copy-start | bytes 2359300
  72.8 9.8 %collective-permute-start.11 = (bf16[768,512]{1,0:T(8,128)(2,1)S(1)}, bf16[768,512]{1,0:T(8,128)(2,1)S(1)}, u32[]{:S(2)}, u32[]{:S(2)}) collective-permute-start(bf16[768,512]{1,0:T(8,128)(2,1)S(1)} %get-tuple-element.88.h0.hid_ref), channel_id=1, source_target_pairs={{0,1},{1,0},{2,3},{3,2},{4,5},{5,4},{6,7},{7,6},{8,9},{9,8},{10,11... | collective-permute-start | bytes 2359304 | tf_op jit(solution)/shard_map/ppermute | solution.py:363
  72.9 4.9 %collective-permute-start.5 = (bf16[768,384]{1,0:T(8,128)(2,1)S(1)}, bf16[768,384]{1,0:T(8,128)(2,1)S(1)}, u32[]{:S(2)}, u32[]{:S(2)}) collective-permute-start(bf16[768,384]{1,0:T(8,128)(2,1)S(1)} %bitcast.27), channel_id=1, source_target_pairs={{0,1},{1,0},{2,3},{3,2},{4,5},{5,4},{6,7},{7,6},{8,9},{9,8},{10,11... | collective-permute-start | bytes 1769480 | tf_op jit(solution)/shard_map/ppermute | solution.py:363
  73.4 4.4 %collective-permute-start.6 = (bf16[768,384]{1,0:T(8,128)(2,1)S(1)}, bf16[768,384]{1,0:T(8,128)(2,1)S(1)}, u32[]{:S(2)}, u32[]{:S(2)}) collective-permute-start(bf16[768,384]{1,0:T(8,128)(2,1)S(1)} %collective-permute-done.c1.refs_1_), channel_id=1, source_target_pairs={{0,1},{1,0},{2,3},{3,2},{4,5},{5,4},{6,7},{7,6},{8,9},{9,8},{10,11... | collective-permute-start | bytes 1769480 | tf_op jit(solution)/shard_map/ppermute | solution.py:363
  73.5 4.3 %collective-permute-start.7 = (bf16[768,384]{1,0:T(8,128)(2,1)S(1)}, bf16[768,384]{1,0:T(8,128)(2,1)S(1)}, u32[]{:S(2)}, u32[]{:S(2)}) collective-permute-start(bf16[768,384]{1,0:T(8,128)(2,1)S(1)} %collective-permute-done.1.c2.refs_2_), channel_id=1, source_target_pairs={{0,1},{1,0},{2,3},{3,2},{4,5},{5,4},{6,7},{7,6},{8,9},{9,8},{10,11... | collective-permute-start | bytes 1769480 | tf_op jit(solution)/shard_map/ppermute | solution.py:363
  73.9 4.6 %collective-permute-start.8 = (bf16[768,384]{1,0:T(8,128)(2,1)S(1)}, bf16[768,384]{1,0:T(8,128)(2,1)S(1)}, u32[]{:S(2)}, u32[]{:S(2)}) collective-permute-start(bf16[768,384]{1,0:T(8,128)(2,1)S(1)} %collective-permute-done.2.c3.refs_3_), channel_id=1, source_target_pairs={{0,1},{1,0},{2,3},{3,2},{4,5},{5,4},{6,7},{7,6},{8,9},{9,8},{10,11... | collective-permute-start | bytes 1769480 | tf_op jit(solution)/shard_map/ppermute | solution.py:363
  77.8 4.5 %copy-start.10 = (bf16[768,384]{1,0:T(8,128)(2,1)}, bf16[768,384]{1,0:T(8,128)(2,1)S(1)}, u32[]{:S(2)}) copy-start(bf16[768,384]{1,0:T(8,128)(2,1)S(1)} %collective-permute-done.5.c0.refs_4_) | copy-start | bytes 1769476
  77.8 4.5 %copy-start.12 = (bf16[768,384]{1,0:T(8,128)(2,1)}, bf16[768,384]{1,0:T(8,128)(2,1)S(1)}, u32[]{:S(2)}) copy-start(bf16[768,384]{1,0:T(8,128)(2,1)S(1)} %collective-permute-done.6.c1.refs_5_) | copy-start | bytes 1769476
  77.8 4.5 %copy-start.14 = (bf16[768,384]{1,0:T(8,128)(2,1)}, bf16[768,384]{1,0:T(8,128)(2,1)S(1)}, u32[]{:S(2)}) copy-start(bf16[768,384]{1,0:T(8,128)(2,1)S(1)} %collective-permute-done.7.c2.refs_6_) | copy-start | bytes 1769476
  78.5 3.8 %copy-start.16 = (bf16[768,384]{1,0:T(8,128)(2,1)}, bf16[768,384]{1,0:T(8,128)(2,1)S(1)}, u32[]{:S(2)}) copy-start(bf16[768,384]{1,0:T(8,128)(2,1)S(1)} %collective-permute-done.8.c3.refs_7_) | copy-start | bytes 1769476
  82.4 11.5 %collective-permute-start.10 = (bf16[768,1024]{1,0:T(8,128)(2,1)S(1)}, bf16[768,1024]{1,0:T(8,128)(2,1)S(1)}, u32[]{:S(2)}, u32[]{:S(2)}) collective-permute-start(bf16[768,1024]{1,0:T(8,128)(2,1)S(1)} %shard_map.115.m.dgu_ref), channel_id=1, source_target_pairs={{0,1},{1,0},{2,3},{3,2},{4,5},{5,4},{6,7},{7,6},{8,9},{9,8},{10,11... | collective-permute-start | bytes 4718600 | tf_op jit(solution)/shard_map/ppermute | solution.py:363
  88.5 46.9 %all-to-all-start.2 = ((bf16[8,96,1536]{2,1,0:T(8,128)(2,1)}), bf16[8,96,1536]{2,1,0:T(8,128)(2,1)}, u32[]{:S(2)}, u32[]{:S(2)}) async-start(bf16[8,96,1536]{2,1,0:T(8,128)(2,1)} %bitcast.46), calls=%async_computation.2 | async-start | bytes 4718592 | tf_op jit(solution)/shard_map/all_to_all | solution.py:373
  100.0 21.0 %collective-permute-start.12 = (bf16[768,384]{1,0:T(8,128)(2,1)}, bf16[768,384]{1,0:T(8,128)(2,1)S(1)}, u32[]{:S(2)}, u32[]{:S(2)}) collective-permute-start(bf16[768,384]{1,0:T(8,128)(2,1)} %get-tuple-element.80), channel_id=1, source_target_pairs={{0,4},{2,6},{4,0},{6,2},{1,5},{3,7},{5,1},{7,3},{8,12},{10,14},{12... | collective-permute-start | bytes 1769480 | tf_op jit(solution)/shard_map/ppermute | solution.py:368
  102.3 27.2 %collective-permute-start.13 = (bf16[768,384]{1,0:T(8,128)(2,1)}, bf16[768,384]{1,0:T(8,128)(2,1)S(1)}, u32[]{:S(2)}, u32[]{:S(2)}) collective-permute-start(bf16[768,384]{1,0:T(8,128)(2,1)} %get-tuple-element.76), channel_id=1, source_target_pairs={{0,2},{2,4},{4,6},{6,0},{1,3},{3,5},{5,7},{7,1},{8,10},{10,12},{12... | collective-permute-start | bytes 1769480 | tf_op jit(solution)/shard_map/ppermute | solution.py:368
  108.5 26.8 %collective-permute-start.14 = (bf16[768,384]{1,0:T(8,128)(2,1)}, bf16[768,384]{1,0:T(8,128)(2,1)S(1)}, u32[]{:S(2)}, u32[]{:S(2)}) collective-permute-start(bf16[768,384]{1,0:T(8,128)(2,1)} %get-tuple-element.85), channel_id=1, source_target_pairs={{0,6},{2,0},{4,2},{6,4},{1,7},{3,1},{5,3},{7,5},{8,14},{10,8},{12,... | collective-permute-start | bytes 1769480 | tf_op jit(solution)/shard_map/ppermute | solution.py:368
  111.0 18.5 %copy-start.1 = (bf16[8,96,384]{2,1,0:T(8,128)(2,1)S(1)}, bf16[8,96,384]{2,1,0:T(8,128)(2,1)}, u32[]{:S(2)}) copy-start(bf16[8,96,384]{2,1,0:T(8,128)(2,1)} %copy-done) | copy-start | bytes 1769476
  111.0 18.5 %copy-start.3 = (bf16[768,512]{1,0:T(8,128)(2,1)S(1)}, bf16[768,512]{1,0:T(8,128)(2,1)}, u32[]{:S(2)}) copy-start(bf16[768,512]{1,0:T(8,128)(2,1)} %copy-done.2) | copy-start | bytes 2359300
  111.0 18.5 %copy-start.5 = (bf16[768,384]{1,0:T(8,128)(2,1)S(1)}, bf16[768,384]{1,0:T(8,128)(2,1)}, u32[]{:S(2)}) copy-start(bf16[768,384]{1,0:T(8,128)(2,1)} %copy-done.4) | copy-start | bytes 1769476
  111.0 18.5 %copy-start.7 = (bf16[768,384]{1,0:T(8,128)(2,1)S(1)}, bf16[768,384]{1,0:T(8,128)(2,1)}, u32[]{:S(2)}) copy-start(bf16[768,384]{1,0:T(8,128)(2,1)} %copy-done.6) | copy-start | bytes 1769476
  111.0 18.5 %copy-start.9 = (bf16[768,384]{1,0:T(8,128)(2,1)S(1)}, bf16[768,384]{1,0:T(8,128)(2,1)}, u32[]{:S(2)}) copy-start(bf16[768,384]{1,0:T(8,128)(2,1)} %copy-done.8) | copy-start | bytes 1769476
  111.1 18.5 %copy-start.11 = (bf16[768,384]{1,0:T(8,128)(2,1)S(1)}, bf16[768,384]{1,0:T(8,128)(2,1)}, u32[]{:S(2)}) copy-start(bf16[768,384]{1,0:T(8,128)(2,1)} %copy-done.10) | copy-start | bytes 1769476
  111.1 18.5 %copy-start.13 = (bf16[768,384]{1,0:T(8,128)(2,1)S(1)}, bf16[768,384]{1,0:T(8,128)(2,1)}, u32[]{:S(2)}) copy-start(bf16[768,384]{1,0:T(8,128)(2,1)} %copy-done.12) | copy-start | bytes 1769476
  111.1 18.5 %copy-start.15 = (bf16[768,384]{1,0:T(8,128)(2,1)S(1)}, bf16[768,384]{1,0:T(8,128)(2,1)}, u32[]{:S(2)}) copy-start(bf16[768,384]{1,0:T(8,128)(2,1)} %copy-done.14) | copy-start | bytes 1769476
  111.1 18.5 %copy-start.17 = (bf16[768,384]{1,0:T(8,128)(2,1)S(1)}, bf16[768,384]{1,0:T(8,128)(2,1)}, u32[]{:S(2)}) copy-start(bf16[768,384]{1,0:T(8,128)(2,1)} %copy-done.16) | copy-start | bytes 1769476
  120.9 14.4 %copy-start.18 = (bf16[768,384]{1,0:T(8,128)(2,1)}, bf16[768,384]{1,0:T(8,128)(2,1)S(1)}, u32[]{:S(2)}) copy-start(bf16[768,384]{1,0:T(8,128)(2,1)S(1)} %collective-permute-done.12.refs_1_) | copy-start | bytes 1769476
  129.6 5.8 %copy-start.20 = (bf16[768,384]{1,0:T(8,128)(2,1)}, bf16[768,384]{1,0:T(8,128)(2,1)S(1)}, u32[]{:S(2)}) copy-start(bf16[768,384]{1,0:T(8,128)(2,1)S(1)} %collective-permute-done.13.refs_2_) | copy-start | bytes 1769476
  129.6 5.7 %copy-start.22 = (bf16[768,384]{1,0:T(8,128)(2,1)S(1)}, bf16[768,384]{1,0:T(8,128)(2,1)}, u32[]{:S(2)}) copy-start(bf16[768,384]{1,0:T(8,128)(2,1)} %get-tuple-element.78.refs_0_) | copy-start | bytes 1769476
  129.6 15.1 %copy-start.23 = (bf16[256,768]{1,0:T(8,128)(2,1)S(1)}, bf16[256,768]{1,0:T(8,128)(2,1)}, u32[]{:S(2)}) copy-start(bf16[256,768]{1,0:T(8,128)(2,1)} %get-tuple-element.54.refs_0_) | copy-start | bytes 1179652
  129.7 15.1 %copy-start.24 = (bf16[256,768]{1,0:T(8,128)(2,1)S(1)}, bf16[256,768]{1,0:T(8,128)(2,1)}, u32[]{:S(2)}) copy-start(bf16[256,768]{1,0:T(8,128)(2,1)} %get-tuple-element.55.refs_1_) | copy-start | bytes 1179652
  135.4 1.1 copy-start.19
  139.6 14.9 %all-to-all-start.3 = ((bf16[8,96,384]{2,1,0:T(8,128)(2,1)}), bf16[8,96,384]{2,1,0:T(8,128)(2,1)S(1)}, u32[]{:S(2)}, u32[]{:S(2)}) async-start(bf16[8,96,384]{2,1,0:T(8,128)(2,1)} %bitcast.16), calls=%async_computation.3 | async-start | bytes 1179648 | tf_op jit(solution)/shard_map/all_to_all | solution.py:373
  148.6 9.9 %collective-permute-start.15 = (bf16[256,384]{1,0:T(8,128)(2,1)S(1)}, bf16[256,384]{1,0:T(8,128)(2,1)S(1)}, u32[]{:S(2)}, u32[]{:S(2)}) collective-permute-start(bf16[256,384]{1,0:T(8,128)(2,1)S(1)} %get-tuple-element.91), channel_id=1, source_target_pairs={{0,8},{8,0},{1,9},{9,1},{2,10},{10,2},{3,11},{11,3},{4,12},{12,4},... | collective-permute-start | bytes 589832 | tf_op jit(solution)/shard_map/ppermute | solution.py:363
  151.2 7.2 %collective-permute-start.16 = (bf16[256,384]{1,0:T(8,128)(2,1)S(1)}, bf16[256,384]{1,0:T(8,128)(2,1)S(1)}, u32[]{:S(2)}, u32[]{:S(2)}) collective-permute-start(bf16[256,384]{1,0:T(8,128)(2,1)S(1)} %get-tuple-element.92), channel_id=1, source_target_pairs={{0,2},{2,4},{4,6},{6,0},{1,3},{3,5},{5,7},{7,1},{8,10},{10,12},{12... | collective-permute-start | bytes 589832 | tf_op jit(solution)/shard_map/ppermute | solution.py:368
  151.2 7.2 %collective-permute-start.17 = (bf16[256,384]{1,0:T(8,128)(2,1)S(1)}, bf16[256,384]{1,0:T(8,128)(2,1)S(1)}, u32[]{:S(2)}, u32[]{:S(2)}) collective-permute-start(bf16[256,384]{1,0:T(8,128)(2,1)S(1)} %get-tuple-element.93), channel_id=1, source_target_pairs={{0,6},{2,0},{4,2},{6,4},{1,7},{3,1},{5,3},{7,5},{8,14},{10,8},{12,... | collective-permute-start | bytes 589832 | tf_op jit(solution)/shard_map/ppermute | solution.py:368
  155.5 8.5 %collective-permute-start.26 = (bf16[256,384]{1,0:T(8,128)(2,1)S(1)}, bf16[256,384]{1,0:T(8,128)(2,1)S(1)}, u32[]{:S(2)}, u32[]{:S(2)}) collective-permute-start(bf16[256,384]{1,0:T(8,128)(2,1)S(1)} %shard_map.123.refs_0_), channel_id=1, source_target_pairs={{0,12},{2,14},{4,8},{6,10},{8,4},{10,6},{12,0},{14,2},{1,13},{3,15... | collective-permute-start | bytes 589832 | tf_op jit(solution)/shard_map/ppermute | solution.py:391
  159.1 15.8 %collective-permute-start.18 = (bf16[256,384]{1,0:T(8,128)(2,1)S(1)}, bf16[256,384]{1,0:T(8,128)(2,1)S(1)}, u32[]{:S(2)}, u32[]{:S(2)}) collective-permute-start(bf16[256,384]{1,0:T(8,128)(2,1)S(1)} %shard_map.124.refs_0_), channel_id=1, source_target_pairs={{0,12},{2,14},{4,8},{6,10},{8,4},{10,6},{12,0},{14,2},{1,13},{3,15... | collective-permute-start | bytes 589832 | tf_op jit(solution)/shard_map/ppermute | solution.py:391
  164.6 11.0 %collective-permute-start.30 = (bf16[256,384]{1,0:T(8,128)(2,1)S(1)}, bf16[256,384]{1,0:T(8,128)(2,1)S(1)}, u32[]{:S(2)}, u32[]{:S(2)}) collective-permute-start(bf16[256,384]{1,0:T(8,128)(2,1)S(1)} %shard_map.127.refs_0_), channel_id=1, source_target_pairs={{0,1},{1,0},{2,3},{3,2},{4,5},{5,4},{6,7},{7,6},{8,9},{9,8},{10,11... | collective-permute-start | bytes 589832 | tf_op jit(solution)/shard_map/ppermute | solution.py:363
  169.9 7.7 %collective-permute-start.29 = (bf16[256,384]{1,0:T(8,128)(2,1)S(1)}, bf16[256,384]{1,0:T(8,128)(2,1)S(1)}, u32[]{:S(2)}, u32[]{:S(2)}) collective-permute-start(bf16[256,384]{1,0:T(8,128)(2,1)S(1)} %shard_map.127.refs_0_), channel_id=1, source_target_pairs={{0,2},{2,4},{4,6},{6,0},{1,3},{3,5},{5,7},{7,1},{8,10},{10,12},{12... | collective-permute-start | bytes 589832 | tf_op jit(solution)/shard_map/ppermute | solution.py:368
  169.9 9.0 %collective-permute-start.28 = (bf16[256,384]{1,0:T(8,128)(2,1)S(1)}, bf16[256,384]{1,0:T(8,128)(2,1)S(1)}, u32[]{:S(2)}, u32[]{:S(2)}) collective-permute-start(bf16[256,384]{1,0:T(8,128)(2,1)S(1)} %shard_map.127.refs_0_), channel_id=1, source_target_pairs={{0,8},{8,0},{1,9},{9,1},{2,10},{10,2},{3,11},{11,3},{4,12},{12,4},... | collective-permute-start | bytes 589832 | tf_op jit(solution)/shard_map/ppermute | solution.py:363
  172.1 8.5 %collective-permute-start.27 = (bf16[256,384]{1,0:T(8,128)(2,1)S(1)}, bf16[256,384]{1,0:T(8,128)(2,1)S(1)}, u32[]{:S(2)}, u32[]{:S(2)}) collective-permute-start(bf16[256,384]{1,0:T(8,128)(2,1)S(1)} %shard_map.127.refs_0_), channel_id=1, source_target_pairs={{0,6},{2,0},{4,2},{6,4},{1,7},{3,1},{5,3},{7,5},{8,14},{10,8},{12,... | collective-permute-start | bytes 589832 | tf_op jit(solution)/shard_map/ppermute | solution.py:368
  175.4 6.8 %collective-permute-start.21 = (bf16[256,384]{1,0:T(8,128)(2,1)S(1)}, bf16[256,384]{1,0:T(8,128)(2,1)S(1)}, u32[]{:S(2)}, u32[]{:S(2)}) collective-permute-start(bf16[256,384]{1,0:T(8,128)(2,1)S(1)} %shard_map.125.refs_0_), channel_id=1, source_target_pairs={{0,2},{2,4},{4,6},{6,0},{1,3},{3,5},{5,7},{7,1},{8,10},{10,12},{12... | collective-permute-start | bytes 589832 | tf_op jit(solution)/shard_map/ppermute | solution.py:368
  175.5 8.5 %collective-permute-start.20 = (bf16[256,384]{1,0:T(8,128)(2,1)S(1)}, bf16[256,384]{1,0:T(8,128)(2,1)S(1)}, u32[]{:S(2)}, u32[]{:S(2)}) collective-permute-start(bf16[256,384]{1,0:T(8,128)(2,1)S(1)} %shard_map.125.refs_0_), channel_id=1, source_target_pairs={{0,8},{8,0},{1,9},{9,1},{2,10},{10,2},{3,11},{11,3},{4,12},{12,4},... | collective-permute-start | bytes 589832 | tf_op jit(solution)/shard_map/ppermute | solution.py:363
  177.6 6.9 %collective-permute-start.19 = (bf16[256,384]{1,0:T(8,128)(2,1)S(1)}, bf16[256,384]{1,0:T(8,128)(2,1)S(1)}, u32[]{:S(2)}, u32[]{:S(2)}) collective-permute-start(bf16[256,384]{1,0:T(8,128)(2,1)S(1)} %shard_map.125.refs_0_), channel_id=1, source_target_pairs={{0,6},{2,0},{4,2},{6,4},{1,7},{3,1},{5,3},{7,5},{8,14},{10,8},{12,... | collective-permute-start | bytes 589832 | tf_op jit(solution)/shard_map/ppermute | solution.py:368
  178.9 6.0 %collective-permute-start.33 = (bf16[256,384]{1,0:T(8,128)(2,1)S(1)}, bf16[256,384]{1,0:T(8,128)(2,1)S(1)}, u32[]{:S(2)}, u32[]{:S(2)}) collective-permute-start(bf16[256,384]{1,0:T(8,128)(2,1)S(1)} %collective-permute-done.29.refs_3_), channel_id=1, source_target_pairs={{0,1},{1,0},{2,3},{3,2},{4,5},{5,4},{6,7},{7,6},{8,9},{9,8},{10,11... | collective-permute-start | bytes 589832 | tf_op jit(solution)/shard_map/ppermute | solution.py:363
  180.7 4.3 %collective-permute-start.32 = (bf16[256,384]{1,0:T(8,128)(2,1)S(1)}, bf16[256,384]{1,0:T(8,128)(2,1)S(1)}, u32[]{:S(2)}, u32[]{:S(2)}) collective-permute-start(bf16[256,384]{1,0:T(8,128)(2,1)S(1)} %collective-permute-done.28.refs_2_), channel_id=1, source_target_pairs={{0,1},{1,0},{2,3},{3,2},{4,5},{5,4},{6,7},{7,6},{8,9},{9,8},{10,11... | collective-permute-start | bytes 589832 | tf_op jit(solution)/shard_map/ppermute | solution.py:363
  182.2 5.1 %collective-permute-start.22 = (bf16[256,384]{1,0:T(8,128)(2,1)S(1)}, bf16[256,384]{1,0:T(8,128)(2,1)S(1)}, u32[]{:S(2)}, u32[]{:S(2)}) collective-permute-start(bf16[256,384]{1,0:T(8,128)(2,1)S(1)} %shard_map.125.refs_0_), channel_id=1, source_target_pairs={{0,1},{1,0},{2,3},{3,2},{4,5},{5,4},{6,7},{7,6},{8,9},{9,8},{10,11... | collective-permute-start | bytes 589832 | tf_op jit(solution)/shard_map/ppermute | solution.py:363
  184.0 1.5 collective-permute-start.31
  184.4 2.9 %collective-permute-start.25 = (bf16[256,384]{1,0:T(8,128)(2,1)S(1)}, bf16[256,384]{1,0:T(8,128)(2,1)S(1)}, u32[]{:S(2)}, u32[]{:S(2)}) collective-permute-start(bf16[256,384]{1,0:T(8,128)(2,1)S(1)} %collective-permute-done.21.refs_3_), channel_id=1, source_target_pairs={{0,1},{1,0},{2,3},{3,2},{4,5},{5,4},{6,7},{7,6},{8,9},{9,8},{10,11... | collective-permute-start | bytes 589832 | tf_op jit(solution)/shard_map/ppermute | solution.py:363
  184.9 2.5 %collective-permute-start.24 = (bf16[256,384]{1,0:T(8,128)(2,1)S(1)}, bf16[256,384]{1,0:T(8,128)(2,1)S(1)}, u32[]{:S(2)}, u32[]{:S(2)}) collective-permute-start(bf16[256,384]{1,0:T(8,128)(2,1)S(1)} %collective-permute-done.20.refs_2_), channel_id=1, source_target_pairs={{0,1},{1,0},{2,3},{3,2},{4,5},{5,4},{6,7},{7,6},{8,9},{9,8},{10,11... | collective-permute-start | bytes 589832 | tf_op jit(solution)/shard_map/ppermute | solution.py:363
  185.0 2.4 %collective-permute-start.23 = (bf16[256,384]{1,0:T(8,128)(2,1)S(1)}, bf16[256,384]{1,0:T(8,128)(2,1)S(1)}, u32[]{:S(2)}, u32[]{:S(2)}) collective-permute-start(bf16[256,384]{1,0:T(8,128)(2,1)S(1)} %collective-permute-done.19.refs_1_), channel_id=1, source_target_pairs={{0,1},{1,0},{2,3},{3,2},{4,5},{5,4},{6,7},{7,6},{8,9},{9,8},{10,11... | collective-permute-start | bytes 589832 | tf_op jit(solution)/shard_map/ppermute | solution.py:363
  (1 other events, 1.1 us)

commit v3 on v2

--- a/solution.py
+++ b/solution.py
@@ -149,7 +149,7 @@
         + ([rows_of] * 2 if last else []),
         [rows_of] * (3 if last else 2),
         mib=20,
-    )(scal, *in_hbm(t_half, wg, wu), *(sums or ()))
+    )(scal, *([t_half] if last else in_hbm(t_half)), *in_hbm(wg, wu), *(sums or ()))
 
 
 def back_hidden(scal, chunks, wd, sums):
@@ -237,7 +237,7 @@
 
 def add(scal, *parts):
     rows, cols = parts[0].shape
-    rb = rows // 4 if rows > 256 else rows
+    rb = rows // 2 if rows > 256 else rows
 
     def kernel(s, *refs):
         acc = refs[0][...].astype(F32)
@@ -319,7 +319,7 @@
         ],
         [pl.BlockSpec((kb, ff), place_of)] * 2,
         mib=20,
-    )(scal, *in_hbm(own, oth), dgu)
+    )(scal, *in_hbm(own), oth, dgu)
 
 
 def grad_out(scal, hid, chunks):
@@ -341,22 +341,25 @@
     )(scal, hid, *chunks)
 
 
-def assemble(scal, chunks):
-    rows, cols = chunks[0].shape
+def assemble(scal, *lists):
+    rows, cols = lists[0][0].shape
+    n, rb = len(lists), rows // 4
 
     def kernel(s, *refs):
-        for j in range(8):
-            at = pl.multiple_of(chunk_index(s, j) * cols, 128)
-            refs[8][:, pl.ds(at, cols)] = refs[j][...]
-
-    return call(
-        kernel,
-        shape(rows, 8 * cols),
-        (1,),
-        [block((rows, cols))] * 8,
-        block((rows, 8 * cols)),
-        mib=8,
-    )(scal, *chunks)
+        for i in range(n):
+            for j in range(8):
+                at = pl.multiple_of(chunk_index(s, j) * cols, 128)
+                refs[8 * n + i][:, pl.ds(at, cols)] = refs[8 * i + j][...]
+
+    rows_of = lambda k, s: (k, 0)
+    return call(
+        kernel,
+        [pltpu.HBM((rows, 8 * cols), BF16)] * n,
+        (4,),
+        [pl.BlockSpec((rb, cols), rows_of)] * (8 * n),
+        [pl.BlockSpec((rb, 8 * cols), rows_of)] * n,
+        mib=12,
+    )(scal, *[v for chunks in lists for v in chunks])
 
 
 def swap(v, axis="c"):
@@ -390,7 +393,7 @@
     other = [(yh * 4 + x, (1 - yh) * 4 + (x + 2) % 4) for yh in range(2) for x in range(4)]
     total = add(scal, mine, lax.ppermute(mine, ("yh", "x"), other))
     chunks = gather_q(total, True)
-    return assemble(scal, chunks + [swap(v) for v in chunks])
+    return chunks + [swap(v) for v in chunks]
 
 
 def on_device(tokens, cotangent, expert_ids, gates, w_gate, w_up, w_down):
@@ -439,20 +442,19 @@
     sent[3] = to_q(parts[3], 3, False)
     dgu, hid = after((dgu, hid), parts[0])
     grad_gate, grad_up = grad_in(scal, t_own, t_oth, dgu)
-    hid, sent[2], sent[1] = after((hid, sent[2], sent[1]), grad_up)
-    hid = after(hid, sent[2], sent[1])
-    grad_down = grad_out(scal, hid, d_own + d_oth)
-    sent, home, grad_gate, grad_up, grad_down = lax.optimization_barrier(
-        (sent, home, grad_gate, grad_up, grad_down)
-    )
-    g_home = add(scal, parts[0], sent[2], sent[1], sent[3])
+    grad_down = grad_out(scal, after(hid, grad_up), d_own + d_oth)
+    home, sent[2], sent[1], grad_down = lax.optimization_barrier(
+        (home, sent[2], sent[1], grad_down)
+    )
     quarters = combine(scal, [w_hi, w_lo], home, True)
-    g_home = all_exchange(g_home)
     m_sent = [to_q(quarters[d], d, True) for d in (2, 1, 3)]
+    sent = after(sent, quarters)
+    g_home = all_exchange(add(scal, *in_hbm(parts[0], sent[2], sent[1]), sent[3]))
     g_mine = combine(scal, [placing], g_home, False)[0]
     m_sent = after(m_sent, g_mine)
-    token_grad = finish(scal, g_mine)
-    mixed = finish(scal, add(scal, quarters[0], *m_sent))
+    g_chunks = finish(scal, g_mine)
+    m_chunks = finish(scal, add(scal, quarters[0], *m_sent))
+    mixed, token_grad = assemble(scal, m_chunks, g_chunks)
     return (mixed, token_grad, grad_gate[None], grad_up[None], grad_down[None])
 
 

time: 190 us -> 189 us (level)
  local copies, waits for them, and re-layouts: 7.68 us -> 4.16 us
    ppermute x12, waiting for transfers between devices: 36.2 us -> 31.9 us  [shift(): return lax.ppermute(v, axis, [(i, (i + d) % n) for i in range(n)])]
    all_to_all x4, waiting for transfers between devices: 0.64 us -> 4.49 us  [all_exchange(): lax.all_to_all(cut, EXP, split_axis=0, concat_axis=0, tiled=True)]
    unnamed x54 -> x46, local copies, waits for them, and re-layouts: 4.19 us -> 0.67 us
  transfers between devices with their start and end apart: 38 -> 38, of which waited for: 10 -> 13; matrix products, arithmetic and copies ran while one was open for 3% -> 3% of each run, Pallas kernels for 31% -> 31%
where the time goes in v3:
time: 189 us; the launch traced here: 188 us
  Pallas kernels  73.7 us (39%)
  starting transfers between devices  65.1 us (34%)
  waiting for transfers between devices  42.2 us (22%)
  local copies, waits for them, and re-layouts  4.16 us (2%)
  other arithmetic  1.94 us (1%)
    ppermute x12, waiting for transfers between devices, shift(): return lax.ppermute(v, axis, [(i, (i + d) % n) for i in range(n)])  31.9 us
    all_to_all x4, starting transfers between devices, all_exchange(): lax.all_to_all(cut, EXP, split_axis=0, concat_axis=0, tiled=True)  22.3 us
    ppermute x20, starting transfers between devices, swap(): return lax.ppermute(v, axis, [(0, 1), (1, 0)])  21.2 us
    ppermute x12, starting transfers between devices, shift(): return lax.ppermute(v, axis, [(i, (i + d) % n) for i in range(n)])  16.8 us
    pallas_call x2, Pallas kernels, in_part(): call(kernel, [pltpu.HBM((rows, cols), BF16)] * 2, (1,), [block((rows, 2 *...  12.1 us
    pallas_call x2, Pallas kernels, gate_up(): call(kernel, [pltpu.VMEM((rows, ff), BF16), wide, wide] if last else [wid...  11.9 us
    pallas_call x1, Pallas kernels, grad_in(): call(kernel, [pltpu.HBM((2 * half, ff), BF16)] * 2, (4,), [pl.BlockSpec((...  9.25 us
    pallas_call x2, Pallas kernels, back_hidden(): call(kernel, pltpu.VMEM((rows, 2 * ff), BF16) if last else pltpu.VMEM((ro...  7.54 us
  transfers between devices with their start and end apart: 38, of which 13 were waited for; matrix products, arithmetic and copies ran while one was open for 3% of the time, Pallas kernels for 31%

profile of v3, /device:TPU:1, one launch (start us, length us, event | category | flops | bytes accessed | tf_op | source)
XLA Modules:
  0.0 188.1 jit_solution(4967436378951406898)
XLA Ops:
  0.7 4.2 %shard_map.110 = (bf16[768,384]{1,0:T(8,128)(2,1)}, bf16[256,768]{1,0:T(8,128)(2,1)S(1)}, bf16[256,768]{1,0:T(8,128)(2,1)}, bf16[256,768]{1,0:T(8,128)(2,1)}) custom-call(s32[2]{0:T(128)S(1)} %pad_add_fusion.s, s32[2,256]{1,0:T(2,128)} %bitcast.49, f32[2,256]{1,0:T(2,128)} %bitcast.50, bf16[256,3072]{1,0:T(8,128)(2,1)} %cot_ref.1), custom_call_target="tpu_custom_call" | custom-call | flops 1 | bytes 1 | tf_op jit(solution)/shard_map/pallas_call | solution.py:88
  4.9 6.9 %all-to-all-start = ((bf16[8,96,384]{2,1,0:T(8,128)(2,1)}), bf16[8,96,384]{2,1,0:T(8,128)(2,1)S(1)}, u32[]{:S(2)}, u32[]{:S(2)}) async-start(bf16[8,96,384]{2,1,0:T(8,128)(2,1)} %bitcast.48), calls=%async_computation | async-start | bytes 1179648 | tf_op jit(solution)/shard_map/all_to_all | solution.py:376
  11.8 2.2 %dynamic-slice_bitcast_fusion.1 = (bf16[1536,512]{1,0:T(8,128)(2,1)S(1)}, bf16[1536,512]{1,0:T(8,128)(2,1)S(1)}) fusion(bf16[1,3072,512]{2,1,0:T(8,128)(2,1)} %param.12, s32[]{:T(128)S(6)} %select_n.2, bf16[1,3072,512]{2,1,0:T(8,128)(2,1)} %param.11), kind=kLoop, calls=%fused_computation.2 | loop fusion | bytes 6291460 | tf_op jit(solution)/shard_map/dynamic_slice | solution.py:414
  14.0 0.6 copy-done.22
  14.6 1.2 dynamic-slice_bitcast_fusion
  15.8 4.3 %shard_map.111 = bf16[768,1536]{1,0:T(8,128)(2,1)} custom-call(s32[2]{0:T(128)S(1)} %pad_add_fusion.s, bf16[256,768]{1,0:T(8,128)(2,1)S(1)} %get-tuple-element.56.place_ref.refs_0_, bf16[256,3072]{1,0:T(8,128)(2,1)} %tok_ref.1), custom_call_target="tpu_custom_call" | custom-call | flops 1 | bytes 1 | tf_op jit(solution)/shard_map/pallas_call | solution.py:109
  20.2 1.9 pad_maximum_fusion
  22.0 1.5 collective-permute-start.3
  23.5 4.9 %all-to-all-start.1 = ((bf16[8,96,1536]{2,1,0:T(8,128)(2,1)}), bf16[8,96,1536]{2,1,0:T(8,128)(2,1)}, u32[]{:S(2)}, u32[]{:S(2)}) async-start(bf16[8,96,1536]{2,1,0:T(8,128)(2,1)} %bitcast.9), calls=%async_computation.1 | async-start | bytes 4718592 | tf_op jit(solution)/shard_map/all_to_all | solution.py:376
  28.4 0.3 collective-permute-start.4
  28.7 1.2 collective-permute-start.2
  29.9 2.5 %collective-permute-start.1 = (bf16[768,384]{1,0:T(8,128)(2,1)S(1)}, bf16[768,384]{1,0:T(8,128)(2,1)S(1)}, u32[]{:S(2)}, u32[]{:S(2)}) collective-permute-start(bf16[768,384]{1,0:T(8,128)(2,1)S(1)} %bitcast.25), channel_id=1, source_target_pairs={{0,4},{2,6},{4,0},{6,2},{1,5},{3,7},{5,1},{7,3},{8,12},{10,14},{12... | collective-permute-start | bytes 1769480 | tf_op jit(solution)/shard_map/ppermute | solution.py:371
  32.4 1.1 collective-permute-start
  33.5 11.2 %collective-permute-done.2.c3.refs_3_ = bf16[768,384]{1,0:T(8,128)(2,1)S(1)} collective-permute-done((bf16[768,384]{1,0:T(8,128)(2,1)S(1)}, bf16[768,384]{1,0:T(8,128)(2,1)S(1)}, u32[]{:S(2)}, u32[]{:S(2)}) %collective-permute-start.2) | collective-permute-done | bytes 589856 | tf_op jit(solution)/shard_map/ppermute | solution.py:371
  44.8 13.6 %collective-permute-done.1.c2.refs_2_ = bf16[768,384]{1,0:T(8,128)(2,1)S(1)} collective-permute-done((bf16[768,384]{1,0:T(8,128)(2,1)S(1)}, bf16[768,384]{1,0:T(8,128)(2,1)S(1)}, u32[]{:S(2)}, u32[]{:S(2)}) %collective-permute-start.1) | collective-permute-done | bytes 589856 | tf_op jit(solution)/shard_map/ppermute | solution.py:371
  58.4 1.0 collective-permute-start.5
  59.4 5.8 %shard_map.112 = (f32[768,512]{1,0:T(8,128)S(1)}, f32[768,512]{1,0:T(8,128)S(1)}) custom-call(s32[2]{0:T(128)S(1)} %pad_add_fusion.s, bf16[768,1536]{1,0:T(8,128)(2,1)} %bitcast.10.t_ref.own_ref, bf16[3072,512]{1,0:T(8,128)(2,1)} %bitcast.31, bf16[3072,512]{1,0:T(8,128)(2,1)} %bitcast.37), custom_call_target="tpu_custom_call" | custom-call | flops 1 | bytes 1 | tf_op jit(solution)/shard_map/pallas_call | solution.py:144
  65.2 6.1 %shard_map.113 = (bf16[768,512]{1,0:T(8,128)(2,1)S(1)}, f32[768,512]{1,0:T(8,128)S(1)}, f32[768,512]{1,0:T(8,128)S(1)}) custom-call(s32[2]{0:T(128)S(1)} %pad_add_fusion.s, bf16[768,1536]{1,0:T(8,128)(2,1)S(1)} %collective-permute-done.5.t_ref.oth_ref, bf16[3072,512]{1,0:T(8,128)(2,1)} %bitcast.32, bf16[3072,512]{1,0:T(8,128)(2,1)} %bitcast.38, ...), custom_call_target="tpu_custom_call" | custom-call | flops 1 | bytes 1 | tf_op jit(solution)/shard_map/pallas_call | solution.py:144
  71.5 0.5 collective-permute-start.7
  72.1 0.4 collective-permute-start.9
  72.6 3.8 %shard_map.115.refs_0_ = f32[768,512]{1,0:T(8,128)S(1)} custom-call(s32[2]{0:T(128)S(1)} %pad_add_fusion.s, bf16[768,384]{1,0:T(8,128)(2,1)S(1)} %bitcast.28, bf16[768,384]{1,0:T(8,128)(2,1)S(1)} %collective-permute-done.c1.refs_1_, bf16[768,384]{1,0:T(8,128)(2,1)S(1)} %collective-permute-done.1.c2.refs_2_, ...), custom_call_target="tpu_custom_call" | custom-call | flops 1 | bytes 1 | tf_op jit(solution)/shard_map/pallas_call | solution.py:174
  76.4 0.7 collective-permute-done.10.c3.refs_7_
  77.1 3.8 %shard_map.116.m.dgu_ref = bf16[768,1024]{1,0:T(8,128)(2,1)S(1)} custom-call(s32[2]{0:T(128)S(1)} %pad_add_fusion.s, bf16[768,384]{1,0:T(8,128)(2,1)S(1)} %collective-permute-done.7.c0.refs_4_, bf16[768,384]{1,0:T(8,128)(2,1)S(1)} %collective-permute-done.8.c1.refs_5_, bf16[768,384]{1,0:T(8,128)(2,1)S(1)} %collective-permute-done.9.c2.refs_6_, ...), custom_call_target="tpu_custom_call" | custom-call | flops 1 | bytes 1 | tf_op jit(solution)/shard_map/pallas_call | solution.py:174
  81.0 0.2 collective-permute-start.11
  81.2 5.9 %shard_map.114 = bf16[768,1536]{1,0:T(8,128)(2,1)} custom-call(s32[2]{0:T(128)S(1)} %pad_add_fusion.s, bf16[768,512]{1,0:T(8,128)(2,1)S(1)} %get-tuple-element.82.h0.hid_ref, bf16[768,512]{1,0:T(8,128)(2,1)S(1)} %collective-permute-done.6.h1, bf16[512,3072]{1,0:T(8,128)(2,1)} %bitcast.45, bf16[512,1536]{1,0:T(8,128)(2,1)} %collective-permute-done.4.w1), custom_call_target="tpu_custom_call" | custom-call | flops 1 | bytes 1 | tf_op jit(solution)/shard_map/pallas_call | solution.py:223
  87.1 5.4 %all-to-all-start.2 = ((bf16[8,96,1536]{2,1,0:T(8,128)(2,1)}), bf16[8,96,1536]{2,1,0:T(8,128)(2,1)}, u32[]{:S(2)}, u32[]{:S(2)}) async-start(bf16[8,96,1536]{2,1,0:T(8,128)(2,1)} %bitcast.46), calls=%async_computation.2 | async-start | bytes 4718592 | tf_op jit(solution)/shard_map/all_to_all | solution.py:376
  92.5 6.1 %shard_map.117 = (bf16[768,384]{1,0:T(8,128)(2,1)}, bf16[768,384]{1,0:T(8,128)(2,1)}) custom-call(s32[2]{0:T(128)S(1)} %pad_add_fusion.s, bf16[768,1024]{1,0:T(8,128)(2,1)S(1)} %shard_map.116.m.dgu_ref, bf16[768,1024]{1,0:T(8,128)(2,1)S(1)} %collective-permute-done.11.t, bf16[3072,512]{1,0:T(8,128)(2,1)} %bitcast.33, bf16[3072,512]{1,0:T(8,128)(2,1)} %bitcast.34, ...), custom_call_target="tpu_custom_call" | custom-call | flops 1 | bytes 1 | tf_op jit(solution)/shard_map/pallas_call | solution.py:205
  98.6 2.4 %collective-permute-start.12 = (bf16[768,384]{1,0:T(8,128)(2,1)}, bf16[768,384]{1,0:T(8,128)(2,1)}, u32[]{:S(2)}, u32[]{:S(2)}) collective-permute-start(bf16[768,384]{1,0:T(8,128)(2,1)} %get-tuple-element.75), channel_id=1, source_target_pairs={{0,4},{2,6},{4,0},{6,2},{1,5},{3,7},{5,1},{7,3},{8,12},{10,14},{12... | collective-permute-start | bytes 1769480 | tf_op jit(solution)/shard_map/ppermute | solution.py:371
  101.1 6.0 %shard_map.118 = (bf16[768,384]{1,0:T(8,128)(2,1)}, bf16[768,384]{1,0:T(8,128)(2,1)}) custom-call(s32[2]{0:T(128)S(1)} %pad_add_fusion.s, bf16[768,1024]{1,0:T(8,128)(2,1)S(1)} %shard_map.116.m.dgu_ref, bf16[768,1024]{1,0:T(8,128)(2,1)S(1)} %collective-permute-done.11.t, bf16[3072,512]{1,0:T(8,128)(2,1)} %bitcast.35, bf16[3072,512]{1,0:T(8,128)(2,1)} %bitcast.36, ...), custom_call_target="tpu_custom_call" | custom-call | flops 1 | bytes 1 | tf_op jit(solution)/shard_map/pallas_call | solution.py:205
  107.2 2.5 %collective-permute-start.17 = (bf16[768,384]{1,0:T(8,128)(2,1)}, bf16[768,384]{1,0:T(8,128)(2,1)S(1)}, u32[]{:S(2)}, u32[]{:S(2)}) collective-permute-start(bf16[768,384]{1,0:T(8,128)(2,1)} %get-tuple-element.90), channel_id=1, source_target_pairs={{0,6},{2,0},{4,2},{6,4},{1,7},{3,1},{5,3},{7,5},{8,14},{10,8},{12,... | collective-permute-start | bytes 1769480 | tf_op jit(solution)/shard_map/ppermute | solution.py:371
  109.7 9.2 %shard_map.119 = (bf16[3072,512]{1,0:T(8,128)(2,1)}, bf16[3072,512]{1,0:T(8,128)(2,1)}) custom-call(s32[2]{0:T(128)S(1)} %pad_add_fusion.s, bf16[768,1536]{1,0:T(8,128)(2,1)} %bitcast.10.t_ref.own_ref, bf16[768,1536]{1,0:T(8,128)(2,1)S(1)} %copy-done.1, bf16[768,1024]{1,0:T(8,128)(2,1)S(1)} %shard_map.116.m.dgu_ref), custom_call_target="tpu_custom_call" | custom-call | flops 1 | bytes 1 | tf_op jit(solution)/shard_map/pallas_call | solution.py:311
  119.0 5.7 %shard_map.120 = bf16[512,3072]{1,0:T(8,128)(2,1)} custom-call(s32[2]{0:T(128)S(1)} %pad_add_fusion.s, bf16[768,512]{1,0:T(8,128)(2,1)S(1)} %copy-done.5, bf16[768,384]{1,0:T(8,128)(2,1)S(1)} %bitcast.29, bf16[768,384]{1,0:T(8,128)(2,1)S(1)} %copy-done.11, bf16[768,384]{1,0:T(8,128)(2,1)S(1)} %copy-done.9, bf16[768,384]{1,0:T(8,128)(2,1)S(1)} %copy-done.7, ...), custom_call_target="tpu_custom_call" | custom-call | flops 1 | bytes 1 | tf_op jit(solution)/shard_map/pallas_call | solution.py:334
  124.7 3.6 %collective-permute-done.13.refs_2_ = bf16[768,384]{1,0:T(8,128)(2,1)} collective-permute-done((bf16[768,384]{1,0:T(8,128)(2,1)}, bf16[768,384]{1,0:T(8,128)(2,1)}, u32[]{:S(2)}, u32[]{:S(2)}) %collective-permute-start.13) | collective-permute-done | bytes 589856 | tf_op jit(solution)/shard_map/ppermute | solution.py:371
  128.3 4.5 %shard_map.121 = (bf16[256,384]{1,0:T(8,128)(2,1)S(1)}, bf16[256,384]{1,0:T(8,128)(2,1)}, bf16[256,384]{1,0:T(8,128)(2,1)}, bf16[256,384]{1,0:T(8,128)(2,1)S(1)}) custom-call(s32[2]{0:T(128)S(1)} %pad_add_fusion.s, bf16[256,768]{1,0:T(8,128)(2,1)S(1)} %copy-done.20, bf16[256,768]{1,0:T(8,128)(2,1)S(1)} %copy-done.21, bf16[768,1536]{1,0:T(8,128)(2,1)} %bitcast.15.refs_2_), custom_call_target="tpu_custom_call" | custom-call | flops 1 | bytes 1 | tf_op jit(solution)/shard_map/pallas_call | solution.py:282
  132.8 2.9 %shard_map.122 = bf16[768,384]{1,0:T(8,128)(2,1)} custom-call(s32[2]{0:T(128)S(1)} %pad_add_fusion.s, bf16[768,384]{1,0:T(8,128)(2,1)} %get-tuple-element.78.refs_0_, bf16[768,384]{1,0:T(8,128)(2,1)} %collective-permute-done.12.refs_1_, bf16[768,384]{1,0:T(8,128)(2,1)} %collective-permute-done.13.refs_2_, bf16[768,384]{1,0:T(8,128)(2,1)S(1)} %collective-permute-done.17.refs_3_), custom_call_target="tpu_custom_call" | custom-call | flops 1 | bytes 1 | tf_op jit(solution)/shard_map/pallas_call | solution.py:249
  135.7 5.1 %all-to-all-start.3 = ((bf16[8,96,384]{2,1,0:T(8,128)(2,1)}), bf16[8,96,384]{2,1,0:T(8,128)(2,1)S(1)}, u32[]{:S(2)}, u32[]{:S(2)}) async-start(bf16[8,96,384]{2,1,0:T(8,128)(2,1)} %bitcast.16), calls=%async_computation.3 | async-start | bytes 1179648 | tf_op jit(solution)/shard_map/all_to_all | solution.py:376
  140.8 2.6 %collective-permute-start.14 = (bf16[256,384]{1,0:T(8,128)(2,1)}, bf16[256,384]{1,0:T(8,128)(2,1)S(1)}, u32[]{:S(2)}, u32[]{:S(2)}) collective-permute-start(bf16[256,384]{1,0:T(8,128)(2,1)} %get-tuple-element.85), channel_id=1, source_target_pairs={{0,8},{8,0},{1,9},{9,1},{2,10},{10,2},{3,11},{11,3},{4,12},{12,4},... | collective-permute-start | bytes 589832 | tf_op jit(solution)/shard_map/ppermute | solution.py:366
  143.5 2.7 %collective-permute-start.16 = (bf16[256,384]{1,0:T(8,128)(2,1)S(1)}, bf16[256,384]{1,0:T(8,128)(2,1)S(1)}, u32[]{:S(2)}, u32[]{:S(2)}) collective-permute-start(bf16[256,384]{1,0:T(8,128)(2,1)S(1)} %get-tuple-element.87), channel_id=1, source_target_pairs={{0,6},{2,0},{4,2},{6,4},{1,7},{3,1},{5,3},{7,5},{8,14},{10,8},{12,... | collective-permute-start | bytes 589832 | tf_op jit(solution)/shard_map/ppermute | solution.py:371
  146.1 4.5 %all-to-all-done.3 = bf16[8,96,384]{2,1,0:T(8,128)(2,1)S(1)} async-done(((bf16[8,96,384]{2,1,0:T(8,128)(2,1)}), bf16[8,96,384]{2,1,0:T(8,128)(2,1)S(1)}, u32[]{:S(2)}, u32[]{:S(2)}) %all-to-all-start.3) | async-done | bytes 589856 | tf_op jit(solution)/shard_map/all_to_all | solution.py:376
  150.6 0.9 shard_map.123.refs_0_
  151.5 2.2 %collective-permute-start.26 = (bf16[256,384]{1,0:T(8,128)(2,1)S(1)}, bf16[256,384]{1,0:T(8,128)(2,1)S(1)}, u32[]{:S(2)}, u32[]{:S(2)}) collective-permute-start(bf16[256,384]{1,0:T(8,128)(2,1)S(1)} %shard_map.123.refs_0_), channel_id=1, source_target_pairs={{0,12},{2,14},{4,8},{6,10},{8,4},{10,6},{12,0},{14,2},{1,13},{3,15... | collective-permute-start | bytes 589832 | tf_op jit(solution)/shard_map/ppermute | solution.py:394
  153.7 0.7 collective-permute-done.14.refs_1_
  154.5 0.6 shard_map.124.refs_0_
  155.1 2.6 %collective-permute-start.18 = (bf16[256,384]{1,0:T(8,128)(2,1)S(1)}, bf16[256,384]{1,0:T(8,128)(2,1)S(1)}, u32[]{:S(2)}, u32[]{:S(2)}) collective-permute-start(bf16[256,384]{1,0:T(8,128)(2,1)S(1)} %shard_map.124.refs_0_), channel_id=1, source_target_pairs={{0,12},{2,14},{4,8},{6,10},{8,4},{10,6},{12,0},{14,2},{1,13},{3,15... | collective-permute-start | bytes 589832 | tf_op jit(solution)/shard_map/ppermute | solution.py:394
  157.7 2.3 %collective-permute-done.26.refs_1_ = bf16[256,384]{1,0:T(8,128)(2,1)S(1)} collective-permute-done((bf16[256,384]{1,0:T(8,128)(2,1)S(1)}, bf16[256,384]{1,0:T(8,128)(2,1)S(1)}, u32[]{:S(2)}, u32[]{:S(2)}) %collective-permute-start.26) | collective-permute-done | bytes 196640 | tf_op jit(solution)/shard_map/ppermute | solution.py:394
  160.0 0.6 shard_map.126.refs_8_
  160.6 6.5 %collective-permute-start.30 = (bf16[256,384]{1,0:T(8,128)(2,1)S(1)}, bf16[256,384]{1,0:T(8,128)(2,1)S(1)}, u32[]{:S(2)}, u32[]{:S(2)}) collective-permute-start(bf16[256,384]{1,0:T(8,128)(2,1)S(1)} %shard_map.126.refs_8_), channel_id=1, source_target_pairs={{0,1},{1,0},{2,3},{3,2},{4,5},{5,4},{6,7},{7,6},{8,9},{9,8},{10,11... | collective-permute-start | bytes 589832 | tf_op jit(solution)/shard_map/ppermute | solution.py:366
  167.1 1.1 collective-permute-start.28
  168.2 2.7 %collective-permute-start.27 = (bf16[256,384]{1,0:T(8,128)(2,1)S(1)}, bf16[256,384]{1,0:T(8,128)(2,1)S(1)}, u32[]{:S(2)}, u32[]{:S(2)}) collective-permute-start(bf16[256,384]{1,0:T(8,128)(2,1)S(1)} %shard_map.126.refs_8_), channel_id=1, source_target_pairs={{0,6},{2,0},{4,2},{6,4},{1,7},{3,1},{5,3},{7,5},{8,14},{10,8},{12,... | collective-permute-start | bytes 589832 | tf_op jit(solution)/shard_map/ppermute | solution.py:371
  170.9 0.6 shard_map.125.refs_0_
  171.5 1.0 collective-permute-start.22
  172.5 2.3 %collective-permute-done.29.refs_11_ = bf16[256,384]{1,0:T(8,128)(2,1)S(1)} collective-permute-done((bf16[256,384]{1,0:T(8,128)(2,1)S(1)}, bf16[256,384]{1,0:T(8,128)(2,1)S(1)}, u32[]{:S(2)}, u32[]{:S(2)}) %collective-permute-start.29) | collective-permute-done | bytes 196640 | tf_op jit(solution)/shard_map/ppermute | solution.py:371
  174.8 1.1 collective-permute-start.20
  175.9 1.5 collective-permute-start.19
  177.5 1.5 collective-permute-start.33
  179.0 1.2 collective-permute-done.21.refs_3_
  180.2 0.9 collective-permute-start.31
  181.1 0.8 collective-permute-done.20.refs_2_
  181.9 1.8 collective-permute-start.25
  183.6 0.5 collective-permute-start.23
  184.2 0.5 collective-permute-done.25.refs_7_
  184.7 0.4 collective-permute-done.24.refs_6_
  185.1 0.3 collective-permute-done.23.refs_5_
  185.4 2.8 %shard_map.127 = (bf16[256,3072]{1,0:T(8,128)(2,1)}, bf16[256,3072]{1,0:T(8,128)(2,1)}) custom-call(s32[2]{0:T(128)S(1)} %pad_add_fusion.s, bf16[256,384]{1,0:T(8,128)(2,1)S(1)} %shard_map.125.refs_0_, bf16[256,384]{1,0:T(8,128)(2,1)S(1)} %collective-permute-done.19.refs_1_, bf16[256,384]{1,0:T(8,128)(2,1)S(1)} %collective-permute-done.20.refs_2_, ...), custom_call_target="tpu_custom_call" | custom-call | flops 1 | bytes 1 | tf_op jit(solution)/shard_map/pallas_call | solution.py:355
  (80 shorter events, 0.8 us)
Async XLA Ops:
  4.9 17.1 %all-to-all-start = ((bf16[8,96,384]{2,1,0:T(8,128)(2,1)}), bf16[8,96,384]{2,1,0:T(8,128)(2,1)S(1)}, u32[]{:S(2)}, u32[]{:S(2)}) async-start(bf16[8,96,384]{2,1,0:T(8,128)(2,1)} %bitcast.48), calls=%async_computation | async-start | bytes 1179648 | tf_op jit(solution)/shard_map/all_to_all | solution.py:376
  11.8 2.8 %copy-start.22 = (bf16[1,512,3072]{2,1,0:T(8,128)(2,1)S(1)}, bf16[1,512,3072]{2,1,0:T(8,128)(2,1)}, u32[]{:S(2)}) copy-start(bf16[1,512,3072]{2,1,0:T(8,128)(2,1)} %param.13) | copy-start | bytes 9437188
  22.0 50.6 %copy-start.2 = (bf16[8,96,384]{2,1,0:T(8,128)(2,1)}, bf16[8,96,384]{2,1,0:T(8,128)(2,1)S(1)}, u32[]{:S(2)}) copy-start(bf16[8,96,384]{2,1,0:T(8,128)(2,1)S(1)} %all-to-all-done) | copy-start | bytes 1769476
  22.0 36.4 %collective-permute-start.3 = (bf16[3072,512]{1,0:T(8,128)(2,1)}, bf16[3072,512]{1,0:T(8,128)(2,1)}, u32[]{:S(2)}, u32[]{:S(2)}) collective-permute-start(bf16[3072,512]{1,0:T(8,128)(2,1)} %pad_maximum_fusion), channel_id=1, source_target_pairs={{0,1},{1,0},{2,3},{3,2},{4,5},{5,4},{6,7},{7,6},{8,9},{9,8},{10,11... | collective-permute-start | bytes 9437192 | tf_op jit(solution)/shard_map/ppermute | solution.py:366
  23.5 34.9 %all-to-all-start.1 = ((bf16[8,96,1536]{2,1,0:T(8,128)(2,1)}), bf16[8,96,1536]{2,1,0:T(8,128)(2,1)}, u32[]{:S(2)}, u32[]{:S(2)}) async-start(bf16[8,96,1536]{2,1,0:T(8,128)(2,1)} %bitcast.9), calls=%async_computation.1 | async-start | bytes 4718592 | tf_op jit(solution)/shard_map/all_to_all | solution.py:376
  28.4 30.0 %collective-permute-start.4 = (bf16[512,1536]{1,0:T(8,128)(2,1)}, bf16[512,1536]{1,0:T(8,128)(2,1)}, u32[]{:S(2)}, u32[]{:S(2)}) collective-permute-start(bf16[512,1536]{1,0:T(8,128)(2,1)} %dynamic-slice_bitcast_fusion), channel_id=1, source_target_pairs={{0,1},{1,0},{2,3},{3,2},{4,5},{5,4},{6,7},{7,6},{8,9},{9,8},{10,11... | collective-permute-start | bytes 4718600 | tf_op jit(solution)/shard_map/ppermute | solution.py:366
  28.7 16.0 %collective-permute-start.2 = (bf16[768,384]{1,0:T(8,128)(2,1)S(1)}, bf16[768,384]{1,0:T(8,128)(2,1)S(1)}, u32[]{:S(2)}, u32[]{:S(2)}) collective-permute-start(bf16[768,384]{1,0:T(8,128)(2,1)S(1)} %bitcast.24), channel_id=1, source_target_pairs={{0,2},{2,4},{4,6},{6,0},{1,3},{3,5},{5,7},{7,1},{8,10},{10,12},{12... | collective-permute-start | bytes 1769480 | tf_op jit(solution)/shard_map/ppermute | solution.py:371
  29.9 28.5 %collective-permute-start.1 = (bf16[768,384]{1,0:T(8,128)(2,1)S(1)}, bf16[768,384]{1,0:T(8,128)(2,1)S(1)}, u32[]{:S(2)}, u32[]{:S(2)}) collective-permute-start(bf16[768,384]{1,0:T(8,128)(2,1)S(1)} %bitcast.25), channel_id=1, source_target_pairs={{0,4},{2,6},{4,0},{6,2},{1,5},{3,7},{5,1},{7,3},{8,12},{10,14},{12... | collective-permute-start | bytes 1769480 | tf_op jit(solution)/shard_map/ppermute | solution.py:371
  32.4 26.0 %collective-permute-start = (bf16[768,384]{1,0:T(8,128)(2,1)S(1)}, bf16[768,384]{1,0:T(8,128)(2,1)S(1)}, u32[]{:S(2)}, u32[]{:S(2)}) collective-permute-start(bf16[768,384]{1,0:T(8,128)(2,1)S(1)} %bitcast.26), channel_id=1, source_target_pairs={{0,6},{2,0},{4,2},{6,4},{1,7},{3,1},{5,3},{7,5},{8,14},{10,8},{12,... | collective-permute-start | bytes 1769480 | tf_op jit(solution)/shard_map/ppermute | solution.py:371
  44.7 27.9 %copy-start.6 = (bf16[768,384]{1,0:T(8,128)(2,1)}, bf16[768,384]{1,0:T(8,128)(2,1)S(1)}, u32[]{:S(2)}) copy-start(bf16[768,384]{1,0:T(8,128)(2,1)S(1)} %collective-permute-done.2.c3.refs_3_) | copy-start | bytes 1769476
  58.4 14.2 %copy-start.8 = (bf16[768,384]{1,0:T(8,128)(2,1)}, bf16[768,384]{1,0:T(8,128)(2,1)S(1)}, u32[]{:S(2)}) copy-start(bf16[768,384]{1,0:T(8,128)(2,1)S(1)} %collective-permute-done.1.c2.refs_2_) | copy-start | bytes 1769476
  58.4 14.2 %copy-start.10 = (bf16[768,384]{1,0:T(8,128)(2,1)}, bf16[768,384]{1,0:T(8,128)(2,1)S(1)}, u32[]{:S(2)}) copy-start(bf16[768,384]{1,0:T(8,128)(2,1)S(1)} %collective-permute-done.c1.refs_1_) | copy-start | bytes 1769476
  58.4 6.8 %collective-permute-start.5 = (bf16[768,1536]{1,0:T(8,128)(2,1)}, bf16[768,1536]{1,0:T(8,128)(2,1)S(1)}, u32[]{:S(2)}, u32[]{:S(2)}) collective-permute-start(bf16[768,1536]{1,0:T(8,128)(2,1)} %bitcast.10.t_ref.own_ref), channel_id=1, source_target_pairs={{0,1},{1,0},{2,3},{3,2},{4,5},{5,4},{6,7},{7,6},{8,9},{9,8},{10,11... | collective-permute-start | bytes 7077896 | tf_op jit(solution)/shard_map/ppermute | solution.py:366
  65.2 6.2 %copy-start = (bf16[768,1536]{1,0:T(8,128)(2,1)}, bf16[768,1536]{1,0:T(8,128)(2,1)S(1)}, u32[]{:S(2)}) copy-start(bf16[768,1536]{1,0:T(8,128)(2,1)S(1)} %collective-permute-done.5.t_ref.oth_ref) | copy-start | bytes 7077892
  71.4 9.8 %copy-start.4 = (bf16[768,512]{1,0:T(8,128)(2,1)}, bf16[768,512]{1,0:T(8,128)(2,1)S(1)}, u32[]{:S(2)}) copy-start(bf16[768,512]{1,0:T(8,128)(2,1)S(1)} %get-tuple-element.82.h0.hid_ref) | copy-start | bytes 2359300
  71.4 9.8 %collective-permute-start.6 = (bf16[768,512]{1,0:T(8,128)(2,1)S(1)}, bf16[768,512]{1,0:T(8,128)(2,1)S(1)}, u32[]{:S(2)}, u32[]{:S(2)}) collective-permute-start(bf16[768,512]{1,0:T(8,128)(2,1)S(1)} %get-tuple-element.82.h0.hid_ref), channel_id=1, source_target_pairs={{0,1},{1,0},{2,3},{3,2},{4,5},{5,4},{6,7},{7,6},{8,9},{9,8},{10,11... | collective-permute-start | bytes 2359304 | tf_op jit(solution)/shard_map/ppermute | solution.py:366
  71.5 4.9 %collective-permute-start.7 = (bf16[768,384]{1,0:T(8,128)(2,1)S(1)}, bf16[768,384]{1,0:T(8,128)(2,1)S(1)}, u32[]{:S(2)}, u32[]{:S(2)}) collective-permute-start(bf16[768,384]{1,0:T(8,128)(2,1)S(1)} %bitcast.27), channel_id=1, source_target_pairs={{0,1},{1,0},{2,3},{3,2},{4,5},{5,4},{6,7},{7,6},{8,9},{9,8},{10,11... | collective-permute-start | bytes 1769480 | tf_op jit(solution)/shard_map/ppermute | solution.py:366
  72.0 4.4 %collective-permute-start.8 = (bf16[768,384]{1,0:T(8,128)(2,1)S(1)}, bf16[768,384]{1,0:T(8,128)(2,1)S(1)}, u32[]{:S(2)}, u32[]{:S(2)}) collective-permute-start(bf16[768,384]{1,0:T(8,128)(2,1)S(1)} %collective-permute-done.c1.refs_1_), channel_id=1, source_target_pairs={{0,1},{1,0},{2,3},{3,2},{4,5},{5,4},{6,7},{7,6},{8,9},{9,8},{10,11... | collective-permute-start | bytes 1769480 | tf_op jit(solution)/shard_map/ppermute | solution.py:366
  72.1 4.3 %collective-permute-start.9 = (bf16[768,384]{1,0:T(8,128)(2,1)S(1)}, bf16[768,384]{1,0:T(8,128)(2,1)S(1)}, u32[]{:S(2)}, u32[]{:S(2)}) collective-permute-start(bf16[768,384]{1,0:T(8,128)(2,1)S(1)} %collective-permute-done.1.c2.refs_2_), channel_id=1, source_target_pairs={{0,1},{1,0},{2,3},{3,2},{4,5},{5,4},{6,7},{7,6},{8,9},{9,8},{10,11... | collective-permute-start | bytes 1769480 | tf_op jit(solution)/shard_map/ppermute | solution.py:366
  72.5 4.6 %collective-permute-start.10 = (bf16[768,384]{1,0:T(8,128)(2,1)S(1)}, bf16[768,384]{1,0:T(8,128)(2,1)S(1)}, u32[]{:S(2)}, u32[]{:S(2)}) collective-permute-start(bf16[768,384]{1,0:T(8,128)(2,1)S(1)} %collective-permute-done.2.c3.refs_3_), channel_id=1, source_target_pairs={{0,1},{1,0},{2,3},{3,2},{4,5},{5,4},{6,7},{7,6},{8,9},{9,8},{10,11... | collective-permute-start | bytes 1769480 | tf_op jit(solution)/shard_map/ppermute | solution.py:366
  76.4 4.5 %copy-start.12 = (bf16[768,384]{1,0:T(8,128)(2,1)}, bf16[768,384]{1,0:T(8,128)(2,1)S(1)}, u32[]{:S(2)}) copy-start(bf16[768,384]{1,0:T(8,128)(2,1)S(1)} %collective-permute-done.7.c0.refs_4_) | copy-start | bytes 1769476
  76.4 4.5 %copy-start.14 = (bf16[768,384]{1,0:T(8,128)(2,1)}, bf16[768,384]{1,0:T(8,128)(2,1)S(1)}, u32[]{:S(2)}) copy-start(bf16[768,384]{1,0:T(8,128)(2,1)S(1)} %collective-permute-done.8.c1.refs_5_) | copy-start | bytes 1769476
  76.4 4.5 %copy-start.16 = (bf16[768,384]{1,0:T(8,128)(2,1)}, bf16[768,384]{1,0:T(8,128)(2,1)S(1)}, u32[]{:S(2)}) copy-start(bf16[768,384]{1,0:T(8,128)(2,1)S(1)} %collective-permute-done.9.c2.refs_6_) | copy-start | bytes 1769476
  77.1 3.8 %copy-start.18 = (bf16[768,384]{1,0:T(8,128)(2,1)}, bf16[768,384]{1,0:T(8,128)(2,1)S(1)}, u32[]{:S(2)}) copy-start(bf16[768,384]{1,0:T(8,128)(2,1)S(1)} %collective-permute-done.10.c3.refs_7_) | copy-start | bytes 1769476
  81.0 11.5 %collective-permute-start.11 = (bf16[768,1024]{1,0:T(8,128)(2,1)S(1)}, bf16[768,1024]{1,0:T(8,128)(2,1)S(1)}, u32[]{:S(2)}, u32[]{:S(2)}) collective-permute-start(bf16[768,1024]{1,0:T(8,128)(2,1)S(1)} %shard_map.116.m.dgu_ref), channel_id=1, source_target_pairs={{0,1},{1,0},{2,3},{3,2},{4,5},{5,4},{6,7},{7,6},{8,9},{9,8},{10,11... | collective-permute-start | bytes 4718600 | tf_op jit(solution)/shard_map/ppermute | solution.py:366
  87.1 41.2 %all-to-all-start.2 = ((bf16[8,96,1536]{2,1,0:T(8,128)(2,1)}), bf16[8,96,1536]{2,1,0:T(8,128)(2,1)}, u32[]{:S(2)}, u32[]{:S(2)}) async-start(bf16[8,96,1536]{2,1,0:T(8,128)(2,1)} %bitcast.46), calls=%async_computation.2 | async-start | bytes 4718592 | tf_op jit(solution)/shard_map/all_to_all | solution.py:376
  98.6 26.1 %collective-permute-start.12 = (bf16[768,384]{1,0:T(8,128)(2,1)}, bf16[768,384]{1,0:T(8,128)(2,1)}, u32[]{:S(2)}, u32[]{:S(2)}) collective-permute-start(bf16[768,384]{1,0:T(8,128)(2,1)} %get-tuple-element.75), channel_id=1, source_target_pairs={{0,4},{2,6},{4,0},{6,2},{1,5},{3,7},{5,1},{7,3},{8,12},{10,14},{12... | collective-permute-start | bytes 1769480 | tf_op jit(solution)/shard_map/ppermute | solution.py:371
  100.9 8.7 %copy-start.1 = (bf16[768,1536]{1,0:T(8,128)(2,1)S(1)}, bf16[768,1536]{1,0:T(8,128)(2,1)}, u32[]{:S(2)}) copy-start(bf16[768,1536]{1,0:T(8,128)(2,1)} %copy-done) | copy-start | bytes 7077892
  100.9 27.3 %collective-permute-start.13 = (bf16[768,384]{1,0:T(8,128)(2,1)}, bf16[768,384]{1,0:T(8,128)(2,1)}, u32[]{:S(2)}, u32[]{:S(2)}) collective-permute-start(bf16[768,384]{1,0:T(8,128)(2,1)} %get-tuple-element.76), channel_id=1, source_target_pairs={{0,2},{2,4},{4,6},{6,0},{1,3},{3,5},{5,7},{7,1},{8,10},{10,12},{12... | collective-permute-start | bytes 1769480 | tf_op jit(solution)/shard_map/ppermute | solution.py:371
  107.2 25.7 %collective-permute-start.17 = (bf16[768,384]{1,0:T(8,128)(2,1)}, bf16[768,384]{1,0:T(8,128)(2,1)S(1)}, u32[]{:S(2)}, u32[]{:S(2)}) collective-permute-start(bf16[768,384]{1,0:T(8,128)(2,1)} %get-tuple-element.90), channel_id=1, source_target_pairs={{0,6},{2,0},{4,2},{6,4},{1,7},{3,1},{5,3},{7,5},{8,14},{10,8},{12,... | collective-permute-start | bytes 1769480 | tf_op jit(solution)/shard_map/ppermute | solution.py:371
  109.6 9.3 %copy-start.3 = (bf16[8,96,384]{2,1,0:T(8,128)(2,1)S(1)}, bf16[8,96,384]{2,1,0:T(8,128)(2,1)}, u32[]{:S(2)}) copy-start(bf16[8,96,384]{2,1,0:T(8,128)(2,1)} %copy-done.2) | copy-start | bytes 1769476
  109.6 9.3 %copy-start.5 = (bf16[768,512]{1,0:T(8,128)(2,1)S(1)}, bf16[768,512]{1,0:T(8,128)(2,1)}, u32[]{:S(2)}) copy-start(bf16[768,512]{1,0:T(8,128)(2,1)} %copy-done.4) | copy-start | bytes 2359300
  109.6 9.3 %copy-start.7 = (bf16[768,384]{1,0:T(8,128)(2,1)S(1)}, bf16[768,384]{1,0:T(8,128)(2,1)}, u32[]{:S(2)}) copy-start(bf16[768,384]{1,0:T(8,128)(2,1)} %copy-done.6) | copy-start | bytes 1769476
  109.7 9.3 %copy-start.9 = (bf16[768,384]{1,0:T(8,128)(2,1)S(1)}, bf16[768,384]{1,0:T(8,128)(2,1)}, u32[]{:S(2)}) copy-start(bf16[768,384]{1,0:T(8,128)(2,1)} %copy-done.8) | copy-start | bytes 1769476
  109.7 9.3 %copy-start.11 = (bf16[768,384]{1,0:T(8,128)(2,1)S(1)}, bf16[768,384]{1,0:T(8,128)(2,1)}, u32[]{:S(2)}) copy-start(bf16[768,384]{1,0:T(8,128)(2,1)} %copy-done.10) | copy-start | bytes 1769476
  109.7 9.3 %copy-start.13 = (bf16[768,384]{1,0:T(8,128)(2,1)S(1)}, bf16[768,384]{1,0:T(8,128)(2,1)}, u32[]{:S(2)}) copy-start(bf16[768,384]{1,0:T(8,128)(2,1)} %copy-done.12) | copy-start | bytes 1769476
  109.7 9.3 %copy-start.15 = (bf16[768,384]{1,0:T(8,128)(2,1)S(1)}, bf16[768,384]{1,0:T(8,128)(2,1)}, u32[]{:S(2)}) copy-start(bf16[768,384]{1,0:T(8,128)(2,1)} %copy-done.14) | copy-start | bytes 1769476
  109.7 9.3 %copy-start.17 = (bf16[768,384]{1,0:T(8,128)(2,1)S(1)}, bf16[768,384]{1,0:T(8,128)(2,1)}, u32[]{:S(2)}) copy-start(bf16[768,384]{1,0:T(8,128)(2,1)} %copy-done.16) | copy-start | bytes 1769476
  109.7 9.3 %copy-start.19 = (bf16[768,384]{1,0:T(8,128)(2,1)S(1)}, bf16[768,384]{1,0:T(8,128)(2,1)}, u32[]{:S(2)}) copy-start(bf16[768,384]{1,0:T(8,128)(2,1)} %copy-done.18) | copy-start | bytes 1769476
  119.0 9.3 %copy-start.20 = (bf16[256,768]{1,0:T(8,128)(2,1)S(1)}, bf16[256,768]{1,0:T(8,128)(2,1)}, u32[]{:S(2)}) copy-start(bf16[256,768]{1,0:T(8,128)(2,1)} %get-tuple-element.53.refs_0_) | copy-start | bytes 1179652
  119.0 9.2 %copy-start.21 = (bf16[256,768]{1,0:T(8,128)(2,1)S(1)}, bf16[256,768]{1,0:T(8,128)(2,1)}, u32[]{:S(2)}) copy-start(bf16[256,768]{1,0:T(8,128)(2,1)} %get-tuple-element.54.refs_1_) | copy-start | bytes 1179652
  135.7 14.9 %all-to-all-start.3 = ((bf16[8,96,384]{2,1,0:T(8,128)(2,1)}), bf16[8,96,384]{2,1,0:T(8,128)(2,1)S(1)}, u32[]{:S(2)}, u32[]{:S(2)}) async-start(bf16[8,96,384]{2,1,0:T(8,128)(2,1)} %bitcast.16), calls=%async_computation.3 | async-start | bytes 1179648 | tf_op jit(solution)/shard_map/all_to_all | solution.py:376
  140.8 13.7 %collective-permute-start.14 = (bf16[256,384]{1,0:T(8,128)(2,1)}, bf16[256,384]{1,0:T(8,128)(2,1)S(1)}, u32[]{:S(2)}, u32[]{:S(2)}) collective-permute-start(bf16[256,384]{1,0:T(8,128)(2,1)} %get-tuple-element.85), channel_id=1, source_target_pairs={{0,8},{8,0},{1,9},{9,1},{2,10},{10,2},{3,11},{11,3},{4,12},{12,4},... | collective-permute-start | bytes 589832 | tf_op jit(solution)/shard_map/ppermute | solution.py:366
  143.4 11.0 %collective-permute-start.15 = (bf16[256,384]{1,0:T(8,128)(2,1)}, bf16[256,384]{1,0:T(8,128)(2,1)S(1)}, u32[]{:S(2)}, u32[]{:S(2)}) collective-permute-start(bf16[256,384]{1,0:T(8,128)(2,1)} %get-tuple-element.86), channel_id=1, source_target_pairs={{0,2},{2,4},{4,6},{6,0},{1,3},{3,5},{5,7},{7,1},{8,10},{10,12},{12... | collective-permute-start | bytes 589832 | tf_op jit(solution)/shard_map/ppermute | solution.py:371
  143.5 11.0 %collective-permute-start.16 = (bf16[256,384]{1,0:T(8,128)(2,1)S(1)}, bf16[256,384]{1,0:T(8,128)(2,1)S(1)}, u32[]{:S(2)}, u32[]{:S(2)}) collective-permute-start(bf16[256,384]{1,0:T(8,128)(2,1)S(1)} %get-tuple-element.87), channel_id=1, source_target_pairs={{0,6},{2,0},{4,2},{6,4},{1,7},{3,1},{5,3},{7,5},{8,14},{10,8},{12,... | collective-permute-start | bytes 589832 | tf_op jit(solution)/shard_map/ppermute | solution.py:371
  151.5 8.5 %collective-permute-start.26 = (bf16[256,384]{1,0:T(8,128)(2,1)S(1)}, bf16[256,384]{1,0:T(8,128)(2,1)S(1)}, u32[]{:S(2)}, u32[]{:S(2)}) collective-permute-start(bf16[256,384]{1,0:T(8,128)(2,1)S(1)} %shard_map.123.refs_0_), channel_id=1, source_target_pairs={{0,12},{2,14},{4,8},{6,10},{8,4},{10,6},{12,0},{14,2},{1,13},{3,15... | collective-permute-start | bytes 589832 | tf_op jit(solution)/shard_map/ppermute | solution.py:394
  155.1 15.8 %collective-permute-start.18 = (bf16[256,384]{1,0:T(8,128)(2,1)S(1)}, bf16[256,384]{1,0:T(8,128)(2,1)S(1)}, u32[]{:S(2)}, u32[]{:S(2)}) collective-permute-start(bf16[256,384]{1,0:T(8,128)(2,1)S(1)} %shard_map.124.refs_0_), channel_id=1, source_target_pairs={{0,12},{2,14},{4,8},{6,10},{8,4},{10,6},{12,0},{14,2},{1,13},{3,15... | collective-permute-start | bytes 589832 | tf_op jit(solution)/shard_map/ppermute | solution.py:394
  160.6 11.9 %collective-permute-start.30 = (bf16[256,384]{1,0:T(8,128)(2,1)S(1)}, bf16[256,384]{1,0:T(8,128)(2,1)S(1)}, u32[]{:S(2)}, u32[]{:S(2)}) collective-permute-start(bf16[256,384]{1,0:T(8,128)(2,1)S(1)} %shard_map.126.refs_8_), channel_id=1, source_target_pairs={{0,1},{1,0},{2,3},{3,2},{4,5},{5,4},{6,7},{7,6},{8,9},{9,8},{10,11... | collective-permute-start | bytes 589832 | tf_op jit(solution)/shard_map/ppermute | solution.py:366
  167.1 7.7 %collective-permute-start.29 = (bf16[256,384]{1,0:T(8,128)(2,1)S(1)}, bf16[256,384]{1,0:T(8,128)(2,1)S(1)}, u32[]{:S(2)}, u32[]{:S(2)}) collective-permute-start(bf16[256,384]{1,0:T(8,128)(2,1)S(1)} %shard_map.126.refs_8_), channel_id=1, source_target_pairs={{0,2},{2,4},{4,6},{6,0},{1,3},{3,5},{5,7},{7,1},{8,10},{10,12},{12... | collective-permute-start | bytes 589832 | tf_op jit(solution)/shard_map/ppermute | solution.py:371
  167.1 8.8 %collective-permute-start.28 = (bf16[256,384]{1,0:T(8,128)(2,1)S(1)}, bf16[256,384]{1,0:T(8,128)(2,1)S(1)}, u32[]{:S(2)}, u32[]{:S(2)}) collective-permute-start(bf16[256,384]{1,0:T(8,128)(2,1)S(1)} %shard_map.126.refs_8_), channel_id=1, source_target_pairs={{0,8},{8,0},{1,9},{9,1},{2,10},{10,2},{3,11},{11,3},{4,12},{12,4},... | collective-permute-start | bytes 589832 | tf_op jit(solution)/shard_map/ppermute | solution.py:366
  168.2 9.2 %collective-permute-start.27 = (bf16[256,384]{1,0:T(8,128)(2,1)S(1)}, bf16[256,384]{1,0:T(8,128)(2,1)S(1)}, u32[]{:S(2)}, u32[]{:S(2)}) collective-permute-start(bf16[256,384]{1,0:T(8,128)(2,1)S(1)} %shard_map.126.refs_8_), channel_id=1, source_target_pairs={{0,6},{2,0},{4,2},{6,4},{1,7},{3,1},{5,3},{7,5},{8,14},{10,8},{12,... | collective-permute-start | bytes 589832 | tf_op jit(solution)/shard_map/ppermute | solution.py:371
  171.5 7.4 %collective-permute-start.22 = (bf16[256,384]{1,0:T(8,128)(2,1)S(1)}, bf16[256,384]{1,0:T(8,128)(2,1)S(1)}, u32[]{:S(2)}, u32[]{:S(2)}) collective-permute-start(bf16[256,384]{1,0:T(8,128)(2,1)S(1)} %shard_map.125.refs_0_), channel_id=1, source_target_pairs={{0,1},{1,0},{2,3},{3,2},{4,5},{5,4},{6,7},{7,6},{8,9},{9,8},{10,11... | collective-permute-start | bytes 589832 | tf_op jit(solution)/shard_map/ppermute | solution.py:366
  172.5 7.7 %collective-permute-start.21 = (bf16[256,384]{1,0:T(8,128)(2,1)S(1)}, bf16[256,384]{1,0:T(8,128)(2,1)S(1)}, u32[]{:S(2)}, u32[]{:S(2)}) collective-permute-start(bf16[256,384]{1,0:T(8,128)(2,1)S(1)} %shard_map.125.refs_0_), channel_id=1, source_target_pairs={{0,2},{2,4},{4,6},{6,0},{1,3},{3,5},{5,7},{7,1},{8,10},{10,12},{12... | collective-permute-start | bytes 589832 | tf_op jit(solution)/shard_map/ppermute | solution.py:371
  174.8 7.1 %collective-permute-start.20 = (bf16[256,384]{1,0:T(8,128)(2,1)S(1)}, bf16[256,384]{1,0:T(8,128)(2,1)S(1)}, u32[]{:S(2)}, u32[]{:S(2)}) collective-permute-start(bf16[256,384]{1,0:T(8,128)(2,1)S(1)} %shard_map.125.refs_0_), channel_id=1, source_target_pairs={{0,8},{8,0},{1,9},{9,1},{2,10},{10,2},{3,11},{11,3},{4,12},{12,4},... | collective-permute-start | bytes 589832 | tf_op jit(solution)/shard_map/ppermute | solution.py:366
  175.9 7.7 %collective-permute-start.19 = (bf16[256,384]{1,0:T(8,128)(2,1)S(1)}, bf16[256,384]{1,0:T(8,128)(2,1)S(1)}, u32[]{:S(2)}, u32[]{:S(2)}) collective-permute-start(bf16[256,384]{1,0:T(8,128)(2,1)S(1)} %shard_map.125.refs_0_), channel_id=1, source_target_pairs={{0,6},{2,0},{4,2},{6,4},{1,7},{3,1},{5,3},{7,5},{8,14},{10,8},{12,... | collective-permute-start | bytes 589832 | tf_op jit(solution)/shard_map/ppermute | solution.py:371
  177.5 6.2 %collective-permute-start.33 = (bf16[256,384]{1,0:T(8,128)(2,1)S(1)}, bf16[256,384]{1,0:T(8,128)(2,1)S(1)}, u32[]{:S(2)}, u32[]{:S(2)}) collective-permute-start(bf16[256,384]{1,0:T(8,128)(2,1)S(1)} %collective-permute-done.29.refs_11_), channel_id=1, source_target_pairs={{0,1},{1,0},{2,3},{3,2},{4,5},{5,4},{6,7},{7,6},{8,9},{9,8},{10,11... | collective-permute-start | bytes 589832 | tf_op jit(solution)/shard_map/ppermute | solution.py:366
  178.9 5.2 %collective-permute-start.32 = (bf16[256,384]{1,0:T(8,128)(2,1)S(1)}, bf16[256,384]{1,0:T(8,128)(2,1)S(1)}, u32[]{:S(2)}, u32[]{:S(2)}) collective-permute-start(bf16[256,384]{1,0:T(8,128)(2,1)S(1)} %collective-permute-done.28.refs_10_), channel_id=1, source_target_pairs={{0,1},{1,0},{2,3},{3,2},{4,5},{5,4},{6,7},{7,6},{8,9},{9,8},{10,11... | collective-permute-start | bytes 589832 | tf_op jit(solution)/shard_map/ppermute | solution.py:366
  180.2 4.0 %collective-permute-start.31 = (bf16[256,384]{1,0:T(8,128)(2,1)S(1)}, bf16[256,384]{1,0:T(8,128)(2,1)S(1)}, u32[]{:S(2)}, u32[]{:S(2)}) collective-permute-start(bf16[256,384]{1,0:T(8,128)(2,1)S(1)} %collective-permute-done.27.refs_9_), channel_id=1, source_target_pairs={{0,1},{1,0},{2,3},{3,2},{4,5},{5,4},{6,7},{7,6},{8,9},{9,8},{10,11... | collective-permute-start | bytes 589832 | tf_op jit(solution)/shard_map/ppermute | solution.py:366
  181.9 2.8 %collective-permute-start.25 = (bf16[256,384]{1,0:T(8,128)(2,1)S(1)}, bf16[256,384]{1,0:T(8,128)(2,1)S(1)}, u32[]{:S(2)}, u32[]{:S(2)}) collective-permute-start(bf16[256,384]{1,0:T(8,128)(2,1)S(1)} %collective-permute-done.21.refs_3_), channel_id=1, source_target_pairs={{0,1},{1,0},{2,3},{3,2},{4,5},{5,4},{6,7},{7,6},{8,9},{9,8},{10,11... | collective-permute-start | bytes 589832 | tf_op jit(solution)/shard_map/ppermute | solution.py:366
  183.6 1.4 collective-permute-start.24
  183.6 1.7 collective-permute-start.23
